TPU v7x, 128 devices: a whole 4x4x4 slice. The times are simulated.
128 devices in a mesh: outer: 16 (over x_lo, z, core), inner: 8 (over y, x_hi).
Axes of the slice: x: 4 (x_hi: 2, x_lo: 2; x = x_hi * 2 + x_lo), y: 4, z: 4, core: 2. Of those that a mesh axis runs over, the one named last changes fastest.
Arguments:
- raw_q: bfloat16 [128, 512, 2048], P(('outer', 'inner')), may hold values from -170 to 170
- raw_k: bfloat16 [128, 512, 2048], P(('outer', 'inner')), may hold values from -7 to 7
- raw_v: bfloat16 [128, 512, 2048], P(('outer', 'inner')), may hold values from -6 to 6
- raw_grad: bfloat16 [128, 512, 2048], P(('outer', 'inner')), may hold values from -6 to 6
- beacon_q: bfloat16 [128, 4, 2048], P(('outer', 'inner')), may hold values from -6 to 6
- beacon_k: bfloat16 [128, 4, 2048], P(('outer', 'inner')), may hold values from -6 to 6
- beacon_v: bfloat16 [128, 4, 2048], P(('outer', 'inner')), may hold values from -6 to 6
- beacon_grad: bfloat16 [128, 4, 2048], P(('outer', 'inner')), may hold values from -6 to 6
- assign: int32 [128], replicated, may hold values from 0 to 127, each once
- prefix: int32 [128], replicated, may hold values from 0 to 127, as said below
Outputs:
- raw_dq: bfloat16 [128, 512, 2048], P(('outer', 'inner'))
- raw_dk: bfloat16 [128, 512, 2048], P(('outer', 'inner'))
- raw_dv: bfloat16 [128, 512, 2048], P(('outer', 'inner'))
- beacon_dq: bfloat16 [128, 4, 2048], P(('outer', 'inner'))
- beacon_dk: bfloat16 [128, 4, 2048], P(('outer', 'inner'))
- beacon_dv: bfloat16 [128, 4, 2048], P(('outer', 'inner'))
Inputs may be any that keep to these rules, and one draw needn't show every extreme that they name: `assign`: each stretch number appears once. prefix[c] is at most c; the last stretch sees all earlier stretches.
All inputs are finite; a program needn't handle non-finite values.
Results may differ from a plain program's by a relative error of at most 0.015.
Values may be sent and summed in bfloat16 or wider, within the bound.
No kernel may reach another device: no remote copies, remote signals or barrier semaphores. Data moves between devices by JAX's collectives and lax.ppermute only.
A program may use at most 128 MiB of HBM per device.

v0:
```python
import jax
import jax.numpy as jnp
from jax import lax
from jax.sharding import PartitionSpec as P

HEADS = 16
HEAD_DIM = 128
BEACONS = 4


def visibility(total_rows, stretch_rows, key_stretch, stretch, lowest):
    rows = jnp.arange(total_rows, dtype=jnp.int32)[:, None]
    far_seen = (key_stretch >= lowest) & (key_stretch < stretch)
    far_block = jnp.broadcast_to(far_seen[None, :], (total_rows, key_stretch.shape[0]))
    columns = jnp.arange(stretch_rows, dtype=jnp.int32)[None, :]
    near_block = (columns <= rows) | (rows >= stretch_rows)
    own_columns = jnp.arange(total_rows - stretch_rows, dtype=jnp.int32)[None, :]
    own_block = (rows >= stretch_rows) & (own_columns <= rows - stretch_rows)
    return jnp.concatenate([far_block, near_block, own_block], axis=1)


def head_step(queries, keys, values, grads, visible, head):
    width = HEAD_DIM
    score_scale = width ** (-0.5)
    head_query = lax.dynamic_slice_in_dim(queries, head * width, width, 1)
    head_key = lax.dynamic_slice_in_dim(keys, head * width, width, 1)
    head_value = lax.dynamic_slice_in_dim(values, head * width, width, 1)
    head_grad = lax.dynamic_slice_in_dim(grads, head * width, width, 1)
    scores = jnp.dot(head_query, head_key.T, preferred_element_type=jnp.float32) * score_scale
    scores = jnp.where(visible, scores, -1e30)
    row_top = jnp.max(scores, axis=1, keepdims=True)
    weights = jnp.exp(scores - row_top)
    probs = weights / jnp.sum(weights, axis=1, keepdims=True)
    probs_low = probs.astype(jnp.bfloat16)
    dprobs = jnp.dot(head_grad, head_value.T, preferred_element_type=jnp.float32)
    row_inner = jnp.sum(probs * dprobs, axis=1, keepdims=True)
    dscores = (probs * (dprobs - row_inner) * score_scale).astype(jnp.bfloat16)
    dvalue = jnp.dot(probs_low.T, head_grad, preferred_element_type=jnp.float32)
    dquery = jnp.dot(dscores, head_key, preferred_element_type=jnp.float32)
    dkey = jnp.dot(dscores.T, head_query, preferred_element_type=jnp.float32)
    return (dquery, dkey, dvalue)


def merge_heads(stacked):
    return jnp.transpose(stacked, (1, 0, 2)).reshape(
        stacked.shape[1], stacked.shape[0] * stacked.shape[2]
    )


def slot_grads(queries, keys, values, grads, visible):

    def one_head(head):
        return head_step(queries, keys, values, grads, visible, head)

    dquery, dkey, dvalue = lax.map(one_head, jnp.arange(HEADS, dtype=jnp.int32))
    return (merge_heads(dquery), merge_heads(dkey), merge_heads(dvalue))


def on_device(
    raw_q, raw_k, raw_v, raw_grad, beacon_q, beacon_k, beacon_v, beacon_grad, assign, prefix
):
    local = raw_q.shape[0]
    stretch_rows = raw_q.shape[1]
    features = raw_q.shape[2]
    device = lax.axis_index(("outer", "inner"))
    all_keys, all_values = (
        lax.all_gather(beacon_k, ("outer", "inner"), axis=0, tiled=True),
        lax.all_gather(beacon_v, ("outer", "inner"), axis=0, tiled=True),
    )
    slots = all_keys.shape[0]
    far_rows = slots * BEACONS
    far_keys = all_keys.reshape(far_rows, features)
    far_values = all_values.reshape(far_rows, features)
    key_stretch = assign[jnp.arange(far_rows, dtype=jnp.int32) // BEACONS]

    def step(carry, position):
        acc_key, acc_value = carry
        stretch = assign[device * local + position]
        lowest = stretch - prefix[stretch]
        queries = jnp.concatenate([raw_q[position], beacon_q[position]], axis=0)
        keys = jnp.concatenate([far_keys, raw_k[position], beacon_k[position]], axis=0)
        values = jnp.concatenate([far_values, raw_v[position], beacon_v[position]], axis=0)
        grads = jnp.concatenate([raw_grad[position], beacon_grad[position]], axis=0)
        visible = visibility(stretch_rows + BEACONS, stretch_rows, key_stretch, stretch, lowest)
        dquery, dkey, dvalue = slot_grads(queries, keys, values, grads, visible)
        acc_key = acc_key + dkey[:far_rows]
        acc_value = acc_value + dvalue[:far_rows]
        outs = (
            dquery[:stretch_rows].astype(jnp.bfloat16),
            dquery[stretch_rows:].astype(jnp.bfloat16),
            dkey[far_rows : far_rows + stretch_rows].astype(jnp.bfloat16),
            dvalue[far_rows : far_rows + stretch_rows].astype(jnp.bfloat16),
            dkey[far_rows + stretch_rows :],
            dvalue[far_rows + stretch_rows :],
        )
        return ((acc_key, acc_value), outs)

    start = (
        jnp.zeros((far_rows, features), jnp.float32),
        jnp.zeros((far_rows, features), jnp.float32),
    )
    (acc_key, acc_value), outs = lax.scan(step, start, jnp.arange(local, dtype=jnp.int32))
    raw_dq, beacon_dq, raw_dk, raw_dv, own_key, own_value = outs
    terms_key = acc_key.reshape(slots, BEACONS, features)
    terms_value = acc_value.reshape(slots, BEACONS, features)
    summed_key, summed_value = (
        lax.psum_scatter(terms_key, ("outer", "inner"), scatter_dimension=0, tiled=True),
        lax.psum_scatter(terms_value, ("outer", "inner"), scatter_dimension=0, tiled=True),
    )
    beacon_dk = (own_key + summed_key).astype(jnp.bfloat16)
    beacon_dv = (own_value + summed_value).astype(jnp.bfloat16)
    return (raw_dq, raw_dk, raw_dv, beacon_dq, beacon_dk, beacon_dv)


def solution(mesh):
    placed = (
        P(("outer", "inner"), None, None),
        P(("outer", "inner"), None, None),
        P(("outer", "inner"), None, None),
        P(("outer", "inner"), None, None),
        P(("outer", "inner"), None, None),
        P(("outer", "inner"), None, None),
        P(("outer", "inner"), None, None),
        P(("outer", "inner"), None, None),
        P(),
        P(),
    )
    return jax.shard_map(
        on_device,
        mesh=mesh,
        in_specs=placed,
        out_specs=(
            P(("outer", "inner"), None, None),
            P(("outer", "inner"), None, None),
            P(("outer", "inner"), None, None),
            P(("outer", "inner"), None, None),
            P(("outer", "inner"), None, None),
            P(("outer", "inner"), None, None),
        ),
        check_vma=False,
    )
```

profile of v0, /device:TPU:0, one launch (start us, length us, event | category | flops | bytes accessed | tf_op | source)
XLA Modules:
  0.0 1036.0 jit_solution(17835926722137585385)
XLA Ops:
  14.5 3.4 gather_fusion
  19.1 4.1 pad_maximum_fusion.2
  23.4 289.1 %all-gather.3.cloned.1.call-done = bf16[128,4,2048]{2,1,0:T(4,128)(2,1)} async-done(((bf16[1,4,2048]{2,1,0:T(4,128)(2,1)}), bf16[128,4,2048]{2,1,0:T(4,128)(2,1)}) %all-gather.3.cloned.1.call-update) | async-done | bytes 2097168 | tf_op jit(solution)/shard_map/all_gather | solution.py:67
  312.5 2.5 reshape.149
  315.0 3.5 pad_maximum_fusion
  318.5 297.2 %all-gather.5.cloned.1.call-done = bf16[128,4,2048]{2,1,0:T(4,128)(2,1)} async-done(((bf16[1,4,2048]{2,1,0:T(4,128)(2,1)}), bf16[128,4,2048]{2,1,0:T(4,128)(2,1)}) %all-gather.5.cloned.1.call-update) | async-done | bytes 2097168 | tf_op jit(solution)/shard_map/all_gather | solution.py:68
  615.7 2.5 reshape.150
  618.3 3.5 pad_maximum_fusion.1
  621.8 216.9 %while.19 = (s32[]{:T(128)}, bf16[16,516,128]{2,1,0:T(8,128)(2,1)}, f32[16,1028,128]{2,1,0:T(8,128)}, f32[16,1028,128]{2,1,0:T(8,128)}, s32[16]{0:T(128)S(1)}, /...) while((s32[]{:T(128)}, bf16[16,516,128]{2,1,0:T(8,128)(2,1)}, ...), condition=%wide.region_4.5_spmd, body=%wide.region_0.4_spmd.sunk | while | flops 688520000 | bytes 21240236 | solution.py:55
  625.3 2.9 fusion.51
  630.8 2.4 fusion.50
  638.8 2.9 fusion.51
  652.4 2.9 fusion.51
  657.9 2.4 fusion.50
  666.0 2.9 fusion.51
  671.5 2.4 fusion.50
  679.5 2.9 fusion.51
  685.0 2.4 fusion.50
  693.0 2.9 fusion.51
  698.6 2.4 fusion.50
  706.6 2.9 fusion.51
  712.1 2.4 fusion.50
  720.2 2.9 fusion.51
  725.7 2.4 fusion.50
  733.7 2.9 fusion.51
  747.3 2.9 fusion.51
  760.8 2.9 fusion.51
  766.3 2.4 fusion.50
  774.4 2.9 fusion.51
  787.9 2.9 fusion.51
  793.4 2.4 fusion.50
  801.5 2.9 fusion.51
  815.0 2.9 fusion.51
  828.6 2.9 fusion.51
  834.1 2.4 fusion.50
  838.6 2.5 slice.59
  841.1 4.4 copy.37
  845.5 5.3 reshape.151
  850.8 2.5 slice.61
  853.3 4.4 copy.39
  857.7 5.3 reshape.152
  863.0 2.6 slice.76
  865.6 2.6 slice.75
  868.1 2.7 copy.33
  870.8 4.2 convert_element_type.61
  875.0 2.7 copy.34
  877.7 4.3 convert_element_type.62
  887.3 139.3 %all-reduce.5.cloned.1.call-done = (f32[128,4,2048]{2,1,0:T(4,128)}, f32[128,4,2048]{2,1,0:T(4,128)}) async-done(((f32[128,4,2048]{2,1,0:T(4,128)}, f32[128,4,2048]{2,1,0:T(4,128)}), (f32[128,4,2048]{2,1,0:T(4,128)}, f32[128,4,2048]{2,1,0:T(4,128)})) %all-reduce.5.cloned.1.call-update) | async-done | bytes 8388624
  (141 shorter events, 149.1 us)
Async XLA Ops:
  7.2 11.9 %copy-start.5 = (bf16[1,4,2048]{2,1,0:T(4,128)(2,1)S(1)}, bf16[1,4,2048]{2,1,0:T(4,128)(2,1)}, u32[]{:S(2)}) copy-start(bf16[1,4,2048]{2,1,0:T(4,128)(2,1)} %param.19) | copy-start | bytes 49156
  7.2 11.9 %copy-start.1 = (bf16[1,512,2048]{2,1,0:T(8,128)(2,1)S(1)}, bf16[1,512,2048]{2,1,0:T(8,128)(2,1)}, u32[]{:S(2)}) copy-start(bf16[1,512,2048]{2,1,0:T(8,128)(2,1)} %param.12) | copy-start | bytes 6291460
  7.2 11.9 %copy-start.4 = (bf16[1,4,2048]{2,1,0:T(4,128)(2,1)S(1)}, bf16[1,4,2048]{2,1,0:T(4,128)(2,1)}, u32[]{:S(2)}) copy-start(bf16[1,4,2048]{2,1,0:T(4,128)(2,1)} %param.16) | copy-start | bytes 49156
  7.2 305.3 %all-gather.3.cloned.1.call-start = ((), (), s32[]{:S(2)}) async-start(), calls=%async_computation | async-start | bytes 2113536 | tf_op jit(solution)/shard_map/all_gather | solution.py:67
  7.9 607.8 %all-gather.5.cloned.1.call-start = ((), (), s32[]{:S(2)}) async-start(), calls=%async_computation.1 | async-start | bytes 2113536 | tf_op jit(solution)/shard_map/all_gather | solution.py:68
  8.7 1017.9 %all-reduce.5.cloned.1.call-start = ((), (), s32[]{:S(2)}) async-start(), calls=%async_computation.2 | async-start | bytes 16777216
  23.1 291.9 %copy-start.2 = (bf16[1,4,2048]{2,1,0:T(4,128)(2,1)S(1)}, bf16[1,4,2048]{2,1,0:T(4,128)(2,1)}, u32[]{:S(2)}) copy-start(bf16[1,4,2048]{2,1,0:T(4,128)(2,1)} %param.17) | copy-start | bytes 49156
  318.5 299.7 %copy-start.3 = (bf16[1,4,2048]{2,1,0:T(4,128)(2,1)S(1)}, bf16[1,4,2048]{2,1,0:T(4,128)(2,1)}, u32[]{:S(2)}) copy-start(bf16[1,4,2048]{2,1,0:T(4,128)(2,1)} %param.18) | copy-start | bytes 49156
  877.7 4.4 copy-start
Sparse Core Ops, SparseCore 0:
  9.7 302.7 all-gather.2
  314.2 301.5 all-gather.4
  863.1 163.3 all-reduce.4
where the time goes:
time: 1040 us
  waiting for transfers between devices  727 us (70%)
  matrix products  176 us (17%)
  local copies, waits for them, and re-layouts  68.9 us (7%)
  other arithmetic  35.5 us (3%)
  between operations  17.2 us (2%)
  loops' own time  10.8 us (1%)
    all_gather x1, waiting for transfers between devices, on_device(): lax.all_gather(beacon_v, ('outer', 'inner'), axis=0, tiled=True)  297 us
    all_gather x1, waiting for transfers between devices, on_device(): lax.all_gather(beacon_k, ('outer', 'inner'), axis=0, tiled=True)  289 us
    unnamed x4, waiting for transfers between devices  141 us
    dot_general x16, matrix products, head_step(): dvalue = jnp.dot(probs_low.T, head_grad, preferred_element_type=jnp.float32)  46.7 us
    dot_general x16, matrix products, head_step(): dkey = jnp.dot(dscores.T, head_query, preferred_element_type=jnp.float32)  38 us
    dot_general x16, matrix products, head_step(): dquery = jnp.dot(dscores, head_key, preferred_element_type=jnp.float32)  33.9 us
    dot_general x16, matrix products, head_step(): jnp.dot(head_grad, head_value.T, preferred_element_type=jnp.float32)  29.9 us
    dot_general x16, matrix products, head_step(): jnp.dot(head_query, head_key.T, preferred_element_type=jnp.float32)  28 us
  transfers between devices with their start and end apart: 3, of which 3 were waited for; matrix products, arithmetic and copies ran while one was open for 4% of the time, Pallas kernels for 0%

commit v1 on v0

v1 whole, which is shorter than its diff:
```python
import math

import jax
import jax.numpy as jnp
import numpy as np
from jax import lax
from jax.experimental import pallas as pl
from jax.experimental.pallas import tpu as pltpu
from jax.sharding import Mesh
from jax.sharding import PartitionSpec as P

HEAD_DIM = 128
PAIR = 2 * HEAD_DIM
BEACONS = 4
STRETCH = 512
FEAT = 2048
PAIRS = FEAT // PAIR
LANES = 128
HALF = 256
BLOCK = 64
SCALE = HEAD_DIM ** (-0.5)
LOG_SCALE = SCALE * math.log2(math.e)
HIDDEN = -1e30
F32 = jnp.float32
BF16 = jnp.bfloat16

NAMES = ("x_lo", "z", "core", "y", "x_hi")
SIZES = (2, 4, 2, 4, 2)

X0, X1, Y0, Y1, Z0, Z1 = 1, 2, 4, 8, 16, 32
STEPS = ((Z0, Z1, Y0, Y1, X0, X1), (X0, X1, Z0, Z1, Y0, Y1))


def gray(position):
    return position ^ (position >> 1)


def slot_of(label, core):
    x, y, z = (gray((label >> shift) & 3) for shift in (0, 2, 4))
    return ((((x & 1) * 4 + z) * 2 + core) * 4 + y) * 2 + (x >> 1)


def exchange(value, step):
    pairs = []
    for label in range(64):
        for core in range(2):
            partner = label ^ STEPS[core][step]
            pairs.append((slot_of(label, core), slot_of(partner, core)))
    return lax.ppermute(value, NAMES, sorted(pairs))


def swap(value):
    return lax.ppermute(value, "core", [(0, 1), (1, 0)])


def gather(beacon_k, beacon_v):
    both = jnp.concatenate([beacon_k, beacon_v], axis=1)
    for step in range(4):
        both = jnp.concatenate([both, exchange(both, step)], axis=0)
    key, value = both[:, :FEAT], both[:, FEAT:]
    for first, second in ((4, 5), (5, 4)):
        got_key, got_value = exchange(key, first), exchange(value, second)
        key = jnp.concatenate([key, got_key], axis=0)
        value = jnp.concatenate([value, got_value], axis=0)
    return key, value, swap(key), swap(value)


def added(kept, got):
    return (kept.astype(F32) + got.astype(F32)).astype(BF16)


def scatter(key, value, key_other, value_other):
    got_key, got_value = swap(key_other), swap(value_other)
    key, value = added(key, got_key), added(value, got_value)
    for first, second in ((5, 4), (4, 5)):
        half = key.shape[0] // 2
        got_key, got_value = exchange(key[half:], first), exchange(value[half:], second)
        key, value = added(key[:half], got_key), added(value[:half], got_value)
    both = jnp.concatenate([key, value], axis=1)
    for step in (3, 2, 1):
        half = both.shape[0] // 2
        both = added(both[:half], exchange(both[half:], step))
    half = both.shape[0] // 2
    both = both[:half].astype(F32) + exchange(both[half:], 0).astype(F32)
    return both[:, :FEAT], both[:, FEAT:]


def far_bias(assign, prefix):
    coords = [lax.axis_index(name) for name in NAMES]
    x_lo, z, core, y, x_hi = coords
    mine = gray(x_hi * 2 + x_lo) | (gray(y) << 2) | (gray(z) << 4)
    tables = np.zeros((2, BLOCK * BEACONS), np.int32)
    for which in range(2):
        for row in range(BLOCK * BEACONS):
            place = row // BEACONS
            tables[which, row] = sum(
                bit for step, bit in enumerate(STEPS[which]) if place >> step & 1
            )
    first = jnp.where(core == 0, tables[0], tables[1])
    second = jnp.where(core == 0, tables[1], tables[0])
    slots = jnp.concatenate([slot_of(mine ^ first, core), slot_of(mine ^ second, 1 - core)])
    numbers = jnp.arange(assign.shape[0], dtype=jnp.int32)
    own = slot_of(mine, core)
    stretch = jnp.sum(jnp.where(numbers == own, assign, 0))
    lowest = stretch - jnp.sum(jnp.where(numbers == stretch, prefix, 0))
    seen = (assign >= lowest) & (assign < stretch)
    hit = (slots[:, None] == numbers[None, :]) & seen[None, :]
    visible = jnp.any(hit, axis=1, keepdims=True)
    return jnp.broadcast_to(jnp.where(visible, 0.0, HIDDEN).astype(F32), (2 * HALF, LANES))


def spread(rows):
    pairs = rows.reshape(BEACONS, PAIRS, 2, HEAD_DIM).transpose(1, 2, 0, 3)
    zero = jnp.zeros((PAIRS, BEACONS, HEAD_DIM), rows.dtype)
    top = jnp.concatenate([pairs[:, 0], zero], axis=2)
    low = jnp.concatenate([zero, pairs[:, 1]], axis=2)
    rest = jnp.zeros((PAIRS, LANES - 2 * BEACONS, PAIR), rows.dtype)
    return jnp.concatenate([top, low, rest], axis=1)


def nt(a, b):
    return lax.dot_general(a, b, (((1,), (1,)), ((), ())), preferred_element_type=F32)


def nn(a, b):
    return lax.dot_general(a, b, (((1,), (0,)), ((), ())), preferred_element_type=F32)


def tn(a, b):
    return lax.dot_general(a, b, (((0,), (0,)), ((), ())), preferred_element_type=F32)


def top_of(scores):
    return jnp.max(scores, axis=0, keepdims=True)


def sum_of(values):
    return jnp.sum(values, axis=0, keepdims=True)


def causal(scores):
    rows = lax.broadcasted_iota(jnp.int32, scores.shape, 0)
    columns = lax.broadcasted_iota(jnp.int32, scores.shape, 1)
    return jnp.where(rows <= columns, scores, HIDDEN)


def own_mask(scores):
    rows = lax.broadcasted_iota(jnp.int32, scores.shape, 0)
    columns = lax.broadcasted_iota(jnp.int32, scores.shape, 1)
    return jnp.where((rows <= (columns & 3)) & (rows < BEACONS), scores, HIDDEN)


def power(scores, top):
    return jnp.exp2((scores - top) * LOG_SCALE)


def stats_of(parts):
    top = top_of(parts[0][0])
    for scores, _ in parts[1:]:
        top = jnp.maximum(top, top_of(scores))
    total = inner = None
    for scores, dprobs in parts:
        weights = power(scores, top)
        part, part_inner = sum_of(weights), sum_of(weights * dprobs)
        total = part if total is None else total + part
        inner = part_inner if inner is None else inner + part_inner
    return top, total, inner


def head(index):
    return slice(index * HEAD_DIM, (index + 1) * HEAD_DIM)


def raw_parts(q, k, v, g):
    low, high = slice(0, HALF), slice(HALF, 2 * HALF)
    s00 = causal(nt(k[low], q[low]))
    s01 = nt(k[low], q[high])
    s11 = causal(nt(k[high], q[high]))
    d00 = nt(v[low], g[low])
    d01 = nt(v[low], g[high])
    d11 = nt(v[high], g[high])
    return (s00, d00), (s01, d01), (s11, d11)


def stats_kernel(q_ref, k_ref, v_ref, g_ref, bk_ref, bv_ref, qb_ref, gb_ref, st_ref):
    for index in range(2):
        columns = head(index)
        p00, p01, p11 = raw_parts(
            q_ref[:, columns], k_ref[:, columns], v_ref[:, columns], g_ref[:, columns]
        )
        for place, stats in ((0, stats_of([p00])), (HALF, stats_of([p01, p11]))):
            for row, entry in enumerate(stats):
                st_ref[3 * index + row : 3 * index + row + 1, place : place + HALF] = entry
    qb, gb = qb_ref[...], gb_ref[...]
    far = nt(k_ref[...], qb), nt(v_ref[...], gb)
    own = own_mask(nt(bk_ref[...], qb)), nt(bv_ref[...], gb)
    for row, entry in enumerate(stats_of([far, own])):
        st_ref[row : row + 1, STRETCH:] = entry


def merged(scores, dprobs, stats):
    top, total, inner = stats
    new_top = jnp.maximum(top, top_of(scores))
    weights = power(scores, new_top)
    factor = power(top, new_top)
    total = total * factor + sum_of(weights)
    inner = inner * factor + sum_of(weights * dprobs)
    scaled = 1.0 / total
    return weights, (new_top, scaled, inner * scaled)


def split_grad(weights, dprobs, stats):
    _, scaled, inner = stats
    probs = weights * scaled
    return probs.astype(BF16), (probs * (dprobs - inner)).astype(BF16)


def aligned(value):
    return jnp.concatenate(
        [value[block * BLOCK : (block + 1) * BLOCK] for block in (0, 2, 1, 3)], axis=0
    )


def far_kernel(
    q_ref, g_ref, fk_ref, fv_ref, ok_ref, ov_ref, qb_ref, gb_ref, bias_ref, st_ref,
    dk_ref, dv_ref, dok_ref, dov_ref, dq_ref, dqb_ref, out_ref,
):
    bias = bias_ref[...]
    wide = jnp.concatenate([bias] * 4, axis=1)
    key = jnp.concatenate([fk_ref[...], ok_ref[...]], axis=0)
    value = jnp.concatenate([aligned(fv_ref[...]), aligned(ov_ref[...])], axis=0)
    qb, gb = qb_ref[...], gb_ref[...]
    scores = nt(key, qb) + bias
    dprobs = nt(value, gb)
    stats = tuple(st_ref[row : row + 1, STRETCH:] for row in range(3))
    weights, stats = merged(scores, dprobs, stats)
    for row, entry in enumerate(stats):
        out_ref[row : row + 1, STRETCH:] = entry
    probs, dscores = split_grad(weights, dprobs, stats)
    dkey, dvalue = nn(dscores, qb), nn(probs, gb)
    dqb_ref[...] = tn(dscores, key)[: 2 * BEACONS]
    for index in range(2):
        columns = head(index)
        q, g = q_ref[:, columns], g_ref[:, columns]
        scores = nt(key[:, columns], q) + wide
        dprobs = nt(value[:, columns], g)
        stats = tuple(st_ref[3 * index + row : 3 * index + row + 1, :STRETCH] for row in range(3))
        weights, stats = merged(scores, dprobs, stats)
        for row, entry in enumerate(stats):
            out_ref[3 * index + row : 3 * index + row + 1, :STRETCH] = entry
        probs, dscores = split_grad(weights, dprobs, stats)
        head_key = ((nn(dscores, q) + dkey[:, columns]) * SCALE).astype(BF16)
        head_value = (nn(probs, g) + dvalue[:, columns]).astype(BF16)
        dk_ref[:, columns] = head_key[:HALF]
        dok_ref[:, columns] = head_key[HALF:]
        dv_ref[:, columns] = aligned(head_value[:HALF])
        dov_ref[:, columns] = aligned(head_value[HALF:])
        dq_ref[columns, :] = tn(key[:, columns], dscores)


def grads(scores, dprobs, stats):
    return split_grad(power(scores, stats[0]), dprobs, stats)


def raw_kernel(
    q_ref, k_ref, v_ref, g_ref, bk_ref, bv_ref, qb_ref, gb_ref, st_ref, dqf_ref, dqb_ref,
    dq_ref, dk_ref, dv_ref, dbq_ref, own_k_ref, own_v_ref,
):
    qb, gb = qb_ref[...], gb_ref[...]
    key, value = k_ref[...], v_ref[...]
    stats = tuple(st_ref[row : row + 1, STRETCH:] for row in range(3))
    probs, dscores = grads(nt(key, qb), nt(value, gb), stats)
    dkey, dvalue = nn(dscores, qb), nn(probs, gb)
    dqb = tn(dscores, key)[: 2 * BEACONS] + dqb_ref[...]
    own_key = bk_ref[...]
    probs, dscores = grads(own_mask(nt(own_key, qb)), nt(bv_ref[...], gb), stats)
    own_k_ref[...] = nn(dscores, qb)[: 2 * BEACONS] * SCALE
    own_v_ref[...] = nn(probs, gb)[: 2 * BEACONS]
    dqb = (dqb + tn(dscores, own_key)[: 2 * BEACONS]) * SCALE
    dbq_ref[:, head(0)] = dqb[:BEACONS, head(0)].astype(BF16)
    dbq_ref[:, head(1)] = dqb[BEACONS:, head(1)].astype(BF16)
    low, high = slice(0, HALF), slice(HALF, 2 * HALF)
    for index in range(2):
        columns = head(index)
        q, k, v, g = q_ref[:, columns], key[:, columns], value[:, columns], g_ref[:, columns]
        stats = tuple(st_ref[3 * index + row : 3 * index + row + 1, :STRETCH] for row in range(3))
        first = tuple(entry[:, low] for entry in stats)
        second = tuple(entry[:, high] for entry in stats)
        p00, p01, p11 = raw_parts(q, k, v, g)
        probs00, ds00 = grads(*p00, first)
        probs01, ds01 = grads(*p01, second)
        probs11, ds11 = grads(*p11, second)
        dk_ref[low, columns] = (
            (nn(ds00, q[low]) + nn(ds01, q[high]) + dkey[low, columns]) * SCALE
        ).astype(BF16)
        dk_ref[high, columns] = ((nn(ds11, q[high]) + dkey[high, columns]) * SCALE).astype(BF16)
        dv_ref[low, columns] = (
            nn(probs00, g[low]) + nn(probs01, g[high]) + dvalue[low, columns]
        ).astype(BF16)
        dv_ref[high, columns] = (nn(probs11, g[high]) + dvalue[high, columns]).astype(BF16)
        dq_low = dqf_ref[columns, low] + tn(k[low], ds00)
        dq_high = dqf_ref[columns, high] + tn(k[low], ds01) + tn(k[high], ds11)
        dq_ref[low, columns] = (dq_low.T * SCALE).astype(BF16)
        dq_ref[high, columns] = (dq_high.T * SCALE).astype(BF16)


def three(rows):
    return pl.BlockSpec((None, rows, PAIR), lambda pair: (0, 0, pair))


def two(rows):
    return pl.BlockSpec((rows, PAIR), lambda pair: (0, pair))


def paired(rows, columns):
    return pl.BlockSpec((None, rows, columns), lambda pair: (pair, 0, 0))


def shape(dims, dtype):
    return jax.ShapeDtypeStruct(dims, dtype)


def params():
    return pltpu.CompilerParams(
        dimension_semantics=("arbitrary",), vmem_limit_bytes=40 * 1024 * 1024
    )


def cost(flops, moved):
    return pl.CostEstimate(flops=flops, bytes_accessed=moved, transcendentals=0)


STAT_LANES = STRETCH + LANES


def on_device(
    raw_q, raw_k, raw_v, raw_grad, beacon_q, beacon_k, beacon_v, beacon_grad, assign, prefix
):
    far_key, far_value, other_key, other_value = gather(beacon_k[0], beacon_v[0])
    bias = far_bias(assign, prefix)
    qb, gb = spread(beacon_q[0]), spread(beacon_grad[0])
    fill = jnp.zeros((12, FEAT), BF16)
    own_k = jnp.concatenate([beacon_k[0], fill], axis=0)
    own_v = jnp.concatenate([beacon_v[0], fill], axis=0)
    stat = shape((PAIRS, 8, STAT_LANES), F32)
    raw = three(STRETCH)
    spreads = [paired(LANES, PAIR)] * 2
    stats = pl.pallas_call(
        stats_kernel,
        grid=(PAIRS,),
        in_specs=[raw] * 4 + [two(16)] * 2 + spreads,
        out_specs=paired(8, STAT_LANES),
        out_shape=stat,
        compiler_params=params(),
        cost_estimate=cost(4 * 10**9, 8 * 2**20),
        name="raw_stats",
    )(raw_q, raw_k, raw_v, raw_grad, own_k, own_v, qb, gb)
    half = shape((HALF, FEAT), BF16)
    dk, dv, dok, dov, dqf, dqb, stats = pl.pallas_call(
        far_kernel,
        grid=(PAIRS,),
        in_specs=[raw] * 2
        + [two(HALF)] * 4
        + spreads
        + [pl.BlockSpec((2 * HALF, LANES), lambda pair: (0, 0)), paired(8, STAT_LANES)],
        out_specs=[two(HALF)] * 4
        + [
            pl.BlockSpec((PAIR, STRETCH), lambda pair: (pair, 0)),
            paired(8, PAIR),
            paired(8, STAT_LANES),
        ],
        out_shape=[half] * 4 + [shape((FEAT, STRETCH), F32), shape((PAIRS, 8, PAIR), F32), stat],
        compiler_params=params(),
        cost_estimate=cost(6 * 10**9, 16 * 2**20),
        name="far_grads",
    )(raw_q, raw_grad, far_key, far_value, other_key, other_value, qb, gb, bias, stats)
    summed_key, summed_value = scatter(dk, dv, dok, dov)
    raw_out = shape((1, STRETCH, FEAT), BF16)
    raw_dq, raw_dk, raw_dv, beacon_dq, own_dk, own_dv = pl.pallas_call(
        raw_kernel,
        grid=(PAIRS,),
        in_specs=[raw] * 4
        + [two(16)] * 2
        + spreads
        + [
            paired(8, STAT_LANES),
            pl.BlockSpec((PAIR, STRETCH), lambda pair: (pair, 0)),
            paired(8, PAIR),
        ],
        out_specs=[raw] * 3 + [three(BEACONS)] + [two(8)] * 2,
        out_shape=[raw_out] * 3
        + [shape((1, BEACONS, FEAT), BF16)]
        + [shape((8, FEAT), F32)] * 2,
        compiler_params=params(),
        cost_estimate=cost(6 * 10**9, 20 * 2**20),
        name="raw_grads",
    )(raw_q, raw_k, raw_v, raw_grad, own_k, own_v, qb, gb, stats, dqf, dqb)
    beacon_dk = (own_dk[:BEACONS] + summed_key).astype(BF16)[None]
    beacon_dv = (own_dv[:BEACONS] + summed_value).astype(BF16)[None]
    return (raw_dq, raw_dk, raw_dv, beacon_dq, beacon_dk, beacon_dv)


def solution(mesh):
    named = Mesh(mesh.devices.reshape(SIZES), NAMES)
    placed = P(NAMES, None, None)
    return jax.shard_map(
        on_device,
        mesh=named,
        in_specs=(placed,) * 8 + (P(), P()),
        out_specs=(placed,) * 6,
        check_vma=False,
    )
```

time: 1040 us -> 147 us (0.14)
  waiting for transfers between devices: 727 us -> 47.8 us
  matrix products: 176 us -> 0 us
  local copies, waits for them, and re-layouts: 68.9 us -> 2.29 us
  Pallas kernels: 0 us -> 51 us
  starting transfers between devices: 0.11 us -> 30.2 us
  other arithmetic: 35.5 us -> 12.1 us
  between operations: 17.2 us -> 2.43 us
  loops' own time: 10.8 us -> 0 us
    all_gather x2 -> x0, waiting for transfers between devices: 586 us -> none  [the longest x1 297 us: on_device(): lax.all_gather(beacon_v, ('outer', 'inner'), axis=0, tiled=True)]
    dot_general x80 -> x0, matrix products: 176 us -> none  [the longest x16 46.7 us: head_step(): dvalue = jnp.dot(probs_low.T, head_grad, preferred_element_type=jnp.float32)]
    unnamed x4 -> x0, waiting for transfers between devices: 141 us -> none
    pallas_call x0 -> x3, Pallas kernels: none -> 51 us  [the longest x1 26 us: on_device(): pl.pallas_call(far_kernel, grid=(PAIRS,), in_specs=[raw] * 2 + [two(HALF)...]
    ppermute x0 -> x20, waiting for transfers between devices: none -> 47.8 us  [the longest x16 45.5 us: exchange(): return lax.ppermute(value, NAMES, sorted(pairs))]
    ppermute x0 -> x20, starting transfers between devices: none -> 30.2 us  [the longest x16 29.5 us: exchange(): return lax.ppermute(value, NAMES, sorted(pairs))]
    slice x10 -> x8, local copies, waits for them, and re-layouts: 25.8 us -> 0.2 us  [the longest x2 0.06 us: scatter(): key[half:]]
    reshape x4 -> x0, local copies, waits for them, and re-layouts: 15.6 us -> none  [the longest x1 5.27 us: on_device(): terms_key = acc_key.reshape(slots, BEACONS, features)]
  transfers between devices with their start and end apart: 3 -> 20, of which waited for: 3 -> 15; matrix products, arithmetic and copies ran while one was open for 4% -> 6% of each run, Pallas kernels for 0% -> 17%
where the time goes in v1:
time: 147 us; the launch traced here: 146 us
  Pallas kernels  51 us (35%)
  waiting for transfers between devices  47.8 us (33%)
  starting transfers between devices  30.2 us (21%)
  other arithmetic  12.1 us (8%)
  between operations  2.43 us (2%)
  local copies, waits for them, and re-layouts  2.29 us (2%)
    ppermute x16, waiting for transfers between devices, exchange(): return lax.ppermute(value, NAMES, sorted(pairs))  45.5 us
    ppermute x16, starting transfers between devices, exchange(): return lax.ppermute(value, NAMES, sorted(pairs))  29.5 us
    pallas_call x1, Pallas kernels, on_device(): pl.pallas_call(far_kernel, grid=(PAIRS,), in_specs=[raw] * 2 + [two(HALF)...  26 us
    pallas_call x1, Pallas kernels, on_device(): pl.pallas_call(raw_kernel, grid=(PAIRS,), in_specs=[raw] * 4 + [two(16)]...  17.2 us
    pallas_call x1, Pallas kernels, on_device(): pl.pallas_call(stats_kernel, grid=(PAIRS,), in_specs=[raw] * 4 + [two(16)...  7.84 us
  transfers between devices with their start and end apart: 20, of which 15 were waited for; matrix products, arithmetic and copies ran while one was open for 6% of the time, Pallas kernels for 17%

profile of v1, /device:TPU:0, one launch (start us, length us, event | category | flops | bytes accessed | tf_op | source)
XLA Modules:
  0.0 145.8 jit_solution(9590542036069466869)
XLA Ops:
  0.7 0.8 pad_maximum_fusion.8
  1.5 2.1 %collective-permute-start = (bf16[4,4096]{1,0:T(4,128)(2,1)S(1)}, bf16[4,4096]{1,0:T(4,128)(2,1)S(1)}, u32[]{:S(2)}, u32[]{:S(2)}) collective-permute-start(bf16[4,4096]{1,0:T(4,128)(2,1)S(1)} %pad_maximum_fusion.8), channel_id=1, source_target_pairs={{0,16},{1,17},{2,18},{3,19},{4,20},{5,21},{6,22},{7,23},{8,72},{9,... | collective-permute-start | bytes 98312 | tf_op jit(solution)/shard_map/ppermute | solution.py:49
  3.5 1.9 %collective-permute-done = bf16[4,4096]{1,0:T(4,128)(2,1)S(1)} collective-permute-done((bf16[4,4096]{1,0:T(4,128)(2,1)S(1)}, bf16[4,4096]{1,0:T(4,128)(2,1)S(1)}, u32[]{:S(2)}, u32[]{:S(2)}) %collective-permute-start) | collective-permute-done | bytes 32800 | tf_op jit(solution)/shard_map/ppermute | solution.py:49
  5.4 0.8 pad_maximum_fusion.7
  6.2 4.2 %collective-permute-start.1 = (bf16[8,4096]{1,0:T(8,128)(2,1)S(1)}, bf16[8,4096]{1,0:T(8,128)(2,1)S(1)}, u32[]{:S(2)}, u32[]{:S(2)}) collective-permute-start(bf16[8,4096]{1,0:T(8,128)(2,1)S(1)} %pad_maximum_fusion.7), channel_id=1, source_target_pairs={{0,48},{1,49},{2,50},{3,51},{4,52},{5,53},{6,54},{7,55},{8,73},{9,... | collective-permute-start | bytes 196616 | tf_op jit(solution)/shard_map/ppermute | solution.py:49
  10.4 2.2 %collective-permute-done.1 = bf16[8,4096]{1,0:T(8,128)(2,1)S(1)} collective-permute-done((bf16[8,4096]{1,0:T(8,128)(2,1)S(1)}, bf16[8,4096]{1,0:T(8,128)(2,1)S(1)}, u32[]{:S(2)}, u32[]{:S(2)}) %collective-permute-start.1) | collective-permute-done | bytes 65568 | tf_op jit(solution)/shard_map/ppermute | solution.py:49
  12.7 0.8 pad_maximum_fusion.6
  13.5 1.7 %collective-permute-start.2 = (bf16[16,4096]{1,0:T(8,128)(2,1)S(1)}, bf16[16,4096]{1,0:T(8,128)(2,1)S(1)}, u32[]{:S(2)}, u32[]{:S(2)}) collective-permute-start(bf16[16,4096]{1,0:T(8,128)(2,1)S(1)} %pad_maximum_fusion.6), channel_id=1, source_target_pairs={{0,2},{1,3},{2,0},{3,1},{4,6},{5,7},{6,4},{7,5},{8,24},{9,25},{10,... | collective-permute-start | bytes 393224 | tf_op jit(solution)/shard_map/ppermute | solution.py:49
  15.1 3.4 %collective-permute-done.2 = bf16[16,4096]{1,0:T(8,128)(2,1)S(1)} collective-permute-done((bf16[16,4096]{1,0:T(8,128)(2,1)S(1)}, bf16[16,4096]{1,0:T(8,128)(2,1)S(1)}, u32[]{:S(2)}, u32[]{:S(2)}) %collective-permute-start.2) | collective-permute-done | bytes 131104 | tf_op jit(solution)/shard_map/ppermute | solution.py:49
  18.5 0.8 pad_maximum_fusion.5
  19.3 3.1 %collective-permute-start.3 = (bf16[32,4096]{1,0:T(8,128)(2,1)S(1)}, bf16[32,4096]{1,0:T(8,128)(2,1)S(1)}, u32[]{:S(2)}, u32[]{:S(2)}) collective-permute-start(bf16[32,4096]{1,0:T(8,128)(2,1)S(1)} %pad_maximum_fusion.5), channel_id=1, source_target_pairs={{0,6},{1,7},{2,4},{3,5},{4,2},{5,3},{6,0},{7,1},{8,56},{9,57},{10,... | collective-permute-start | bytes 786440 | tf_op jit(solution)/shard_map/ppermute | solution.py:49
  22.4 4.8 %collective-permute-done.3 = bf16[32,4096]{1,0:T(8,128)(2,1)S(1)} collective-permute-done((bf16[32,4096]{1,0:T(8,128)(2,1)S(1)}, bf16[32,4096]{1,0:T(8,128)(2,1)S(1)}, u32[]{:S(2)}, u32[]{:S(2)}) %collective-permute-start.3) | collective-permute-done | bytes 262176 | tf_op jit(solution)/shard_map/ppermute | solution.py:49
  27.2 0.2 concatenate.74
  27.4 2.8 %collective-permute-start.6 = (bf16[64,2048]{1,0:T(8,128)(2,1)S(1)}, bf16[64,2048]{1,0:T(8,128)(2,1)S(1)}, u32[]{:S(2)}, u32[]{:S(2)}) collective-permute-start(bf16[64,2048]{1,0:T(8,128)(2,1)S(1)} %get-tuple-element.32), channel_id=1, source_target_pairs={{0,65},{1,64},{2,67},{3,66},{4,69},{5,68},{6,71},{7,70},{8,14},{9,... | collective-permute-start | bytes 786440 | tf_op jit(solution)/shard_map/ppermute | solution.py:49
  30.3 0.6 fusion.28
  31.0 1.5 %collective-permute-start.4 = (bf16[64,2048]{1,0:T(8,128)(2,1)S(1)}, bf16[64,2048]{1,0:T(8,128)(2,1)S(1)}, u32[]{:S(2)}, u32[]{:S(2)}) collective-permute-start(bf16[64,2048]{1,0:T(8,128)(2,1)S(1)} %get-tuple-element.33), channel_id=1, source_target_pairs={{0,64},{1,65},{2,66},{3,67},{4,68},{5,69},{6,70},{7,71},{8,10},{9,... | collective-permute-start | bytes 786440 | tf_op jit(solution)/shard_map/ppermute | solution.py:49
  32.4 1.3 fusion.29
  35.1 0.8 pad_maximum_fusion.3
  35.9 1.5 %collective-permute-start.7 = (bf16[128,2048]{1,0:T(8,128)(2,1)}, bf16[128,2048]{1,0:T(8,128)(2,1)}, u32[]{:S(2)}, u32[]{:S(2)}) collective-permute-start(bf16[128,2048]{1,0:T(8,128)(2,1)} %pad_maximum_fusion.3), channel_id=1, source_target_pairs={{0,64},{1,65},{2,66},{3,67},{4,68},{5,69},{6,70},{7,71},{8,10},{9,... | collective-permute-start | bytes 1572872 | tf_op jit(solution)/shard_map/ppermute | solution.py:49
  37.4 0.8 pad_maximum_fusion.2
  38.3 2.1 %collective-permute-start.5 = (bf16[128,2048]{1,0:T(8,128)(2,1)}, bf16[128,2048]{1,0:T(8,128)(2,1)}, u32[]{:S(2)}, u32[]{:S(2)}) collective-permute-start(bf16[128,2048]{1,0:T(8,128)(2,1)} %pad_maximum_fusion.2), channel_id=1, source_target_pairs={{0,65},{1,64},{2,67},{3,66},{4,69},{5,68},{6,71},{7,70},{8,14},{9,... | collective-permute-start | bytes 1572872 | tf_op jit(solution)/shard_map/ppermute | solution.py:49
  40.4 0.6 compare_and_fusion
  41.3 0.2 fusion.11
  41.5 3.9 %collective-permute-done.7 = bf16[128,2048]{1,0:T(8,128)(2,1)} collective-permute-done((bf16[128,2048]{1,0:T(8,128)(2,1)}, bf16[128,2048]{1,0:T(8,128)(2,1)}, u32[]{:S(2)}, u32[]{:S(2)}) %collective-permute-start.7) | collective-permute-done | bytes 524320 | tf_op jit(solution)/shard_map/ppermute | solution.py:49
  45.4 1.3 pad_maximum_fusion.1.fv_ref
  46.8 2.2 %collective-permute-done.5 = bf16[128,2048]{1,0:T(8,128)(2,1)} collective-permute-done((bf16[128,2048]{1,0:T(8,128)(2,1)}, bf16[128,2048]{1,0:T(8,128)(2,1)}, u32[]{:S(2)}, u32[]{:S(2)}) %collective-permute-start.5) | collective-permute-done | bytes 524320 | tf_op jit(solution)/shard_map/ppermute | solution.py:49
  49.0 1.1 pad_maximum_fusion.fk_ref
  50.2 0.2 fusion.8
  50.5 1.6 %copy-done.3 = bf16[1,512,2048]{2,1,0:T(8,128)(2,1)S(1)} copy-done((bf16[1,512,2048]{2,1,0:T(8,128)(2,1)S(1)}, bf16[1,512,2048]{2,1,0:T(8,128)(2,1)}, u32[]{:S(2)}) %copy-start.3) | copy-done | bytes 2097176
  52.0 7.8 %raw_stats.1.st_ref = f32[8,8,640]{2,1,0:T(8,128)S(1)} custom-call(bf16[1,512,2048]{2,1,0:T(8,128)(2,1)S(1)} %copy-done, bf16[1,512,2048]{2,1,0:T(8,128)(2,1)S(1)} %copy-done.1, bf16[1,512,2048]{2,1,0:T(8,128)(2,1)S(1)} %copy-done.2, bf16[1,512,2048]{2,1,0:T(8,128)(2,1)S(1)} %copy-done.3, bf16[16,2048]{1,0:T(8,128)(2,1)S(1)} %concatenate.62.bk_ref, ...), custom_call_target="tpu_custom_call" | custom-call | flops 4000000000 | bytes 8388608 | tf_op jit(solution)/shard_map/raw_stats/pallas_call | solution.py:348
  60.1 26.0 %far_grads.1 = (bf16[256,2048]{1,0:T(8,128)(2,1)S(1)}, bf16[256,2048]{1,0:T(8,128)(2,1)S(1)}, bf16[256,2048]{1,0:T(8,128)(2,1)S(1)}, bf16[256,2048]{1,0:T(8,128)...) custom-call(bf16[1,512,2048]{2,1,0:T(8,128)(2,1)S(1)} %copy-done, ...), custom_call_target="tpu_custom_call" | custom-call | flops 6000000000 | bytes 16777216 | tf_op jit(solution)/shard_map/far_grads/pallas_call | solution.py:359
  86.0 0.5 collective-permute-start.10
  86.5 2.3 %collective-permute-done.10 = bf16[256,2048]{1,0:T(8,128)(2,1)S(1)} collective-permute-done((bf16[256,2048]{1,0:T(8,128)(2,1)S(1)}, bf16[256,2048]{1,0:T(8,128)(2,1)S(1)}, u32[]{:S(2)}, u32[]{:S(2)}) %collective-permute-start.10) | collective-permute-done | bytes 1048608 | tf_op jit(solution)/shard_map/ppermute | solution.py:53
  88.8 0.4 add_convert_fusion.1
  89.2 2.2 %collective-permute-start.11 = (bf16[128,2048]{1,0:T(8,128)(2,1)S(1)}, bf16[128,2048]{1,0:T(8,128)(2,1)S(1)}, u32[]{:S(2)}, u32[]{:S(2)}) collective-permute-start(bf16[128,2048]{1,0:T(8,128)(2,1)S(1)} %slice.111), channel_id=1, source_target_pairs={{0,65},{1,64},{2,67},{3,66},{4,69},{5,68},{6,71},{7,70},{8,14},{9,... | collective-permute-start | bytes 1572872 | tf_op jit(solution)/shard_map/ppermute | solution.py:49
  91.4 0.4 add_convert_fusion
  91.9 7.8 %collective-permute-done.11 = bf16[128,2048]{1,0:T(8,128)(2,1)S(1)} collective-permute-done((bf16[128,2048]{1,0:T(8,128)(2,1)S(1)}, bf16[128,2048]{1,0:T(8,128)(2,1)S(1)}, u32[]{:S(2)}, u32[]{:S(2)}) %collective-permute-start.11) | collective-permute-done | bytes 524320 | tf_op jit(solution)/shard_map/ppermute | solution.py:49
  100.0 1.2 collective-permute-done.14
  101.3 1.2 collective-permute-start.15
  102.5 3.8 %collective-permute-done.12 = bf16[64,2048]{1,0:T(8,128)(2,1)S(1)} collective-permute-done((bf16[64,2048]{1,0:T(8,128)(2,1)S(1)}, bf16[64,2048]{1,0:T(8,128)(2,1)S(1)}, u32[]{:S(2)}, u32[]{:S(2)}) %collective-permute-start.12) | collective-permute-done | bytes 262176 | tf_op jit(solution)/shard_map/ppermute | solution.py:49
  106.4 2.6 %collective-permute-done.15 = bf16[64,2048]{1,0:T(8,128)(2,1)S(1)} collective-permute-done((bf16[64,2048]{1,0:T(8,128)(2,1)S(1)}, bf16[64,2048]{1,0:T(8,128)(2,1)S(1)}, u32[]{:S(2)}, u32[]{:S(2)}) %collective-permute-start.15) | collective-permute-done | bytes 262176 | tf_op jit(solution)/shard_map/ppermute | solution.py:49
  109.0 3.2 %collective-permute-start.16 = (bf16[32,4096]{1,0:T(8,128)(2,1)S(1)}, bf16[32,4096]{1,0:T(8,128)(2,1)S(1)}, u32[]{:S(2)}, u32[]{:S(2)}) collective-permute-start(bf16[32,4096]{1,0:T(8,128)(2,1)S(1)} %pad_maximum_fusion.4), channel_id=1, source_target_pairs={{0,6},{1,7},{2,4},{3,5},{4,2},{5,3},{6,0},{7,1},{8,56},{9,57},{10,... | collective-permute-start | bytes 786440 | tf_op jit(solution)/shard_map/ppermute | solution.py:49
  112.2 4.5 %collective-permute-done.16 = bf16[32,4096]{1,0:T(8,128)(2,1)S(1)} collective-permute-done((bf16[32,4096]{1,0:T(8,128)(2,1)S(1)}, bf16[32,4096]{1,0:T(8,128)(2,1)S(1)}, u32[]{:S(2)}, u32[]{:S(2)}) %collective-permute-start.16) | collective-permute-done | bytes 262176 | tf_op jit(solution)/shard_map/ppermute | solution.py:49
  116.9 5.0 %collective-permute-done.17 = bf16[16,4096]{1,0:T(8,128)(2,1)S(1)} collective-permute-done((bf16[16,4096]{1,0:T(8,128)(2,1)S(1)}, bf16[16,4096]{1,0:T(8,128)(2,1)S(1)}, u32[]{:S(2)}, u32[]{:S(2)}) %collective-permute-start.17) | collective-permute-done | bytes 131104 | tf_op jit(solution)/shard_map/ppermute | solution.py:49
  121.9 3.6 %collective-permute-start.18 = (bf16[8,4096]{1,0:T(8,128)(2,1)S(1)}, bf16[8,4096]{1,0:T(8,128)(2,1)S(1)}, u32[]{:S(2)}, u32[]{:S(2)}) collective-permute-start(bf16[8,4096]{1,0:T(8,128)(2,1)S(1)} %slice.123), channel_id=1, source_target_pairs={{0,48},{1,49},{2,50},{3,51},{4,52},{5,53},{6,54},{7,55},{8,73},{9,... | collective-permute-start | bytes 196616 | tf_op jit(solution)/shard_map/ppermute | solution.py:49
  125.5 2.2 %collective-permute-done.18 = bf16[8,4096]{1,0:T(8,128)(2,1)S(1)} collective-permute-done((bf16[8,4096]{1,0:T(8,128)(2,1)S(1)}, bf16[8,4096]{1,0:T(8,128)(2,1)S(1)}, u32[]{:S(2)}, u32[]{:S(2)}) %collective-permute-start.18) | collective-permute-done | bytes 65568 | tf_op jit(solution)/shard_map/ppermute | solution.py:49
  127.9 17.2 %raw_grads.1 = (bf16[1,512,2048]{2,1,0:T(8,128)(2,1)}, bf16[1,512,2048]{2,1,0:T(8,128)(2,1)}, bf16[1,512,2048]{2,1,0:T(8,128)(2,1)}, bf16[1,4,2048]{2,1,0:T(4,12...) custom-call(bf16[1,512,2048]{2,1,0:T(8,128)(2,1)S(1)} %copy-done, bf16[1,512,2048]{2,1,0:T(8,128)(2,1)S(1)} %copy-done.1, ...), custom_call_target="tpu_custom_call" | custom-call | flops 6000000000 | bytes 20971520 | tf_op jit(solution)/shard_map/raw_grads/pallas_call | solution.py:379
  145.1 0.6 fusion.15
  (70 shorter events, 1.8 us)
Async XLA Ops:
  0.6 29.6 %copy-start.10 = (s32[256]{0:T(256)S(1)}, s32[256]{0:T(256)}, u32[]{:S(2)}) copy-start(s32[256]{0:T(256)} %constant.48.clone) | copy-start | bytes 3076
  0.6 29.6 %copy-start.11 = (s32[256]{0:T(256)S(1)}, s32[256]{0:T(256)}, u32[]{:S(2)}) copy-start(s32[256]{0:T(256)} %constant.49.clone) | copy-start | bytes 3076
  0.7 29.7 %copy-start.12 = (s32[128]{0:T(128)S(1)}, s32[128]{0:T(128)}, u32[]{:S(2)}) copy-start(s32[128]{0:T(128)} %param.22) | copy-start | bytes 1540
  0.7 31.7 %copy-start.13 = (s32[128]{0:T(128)S(1)}, s32[128]{0:T(128)}, u32[]{:S(2)}) copy-start(s32[128]{0:T(128)} %param.23) | copy-start | bytes 1540
  1.5 4.0 %collective-permute-start = (bf16[4,4096]{1,0:T(4,128)(2,1)S(1)}, bf16[4,4096]{1,0:T(4,128)(2,1)S(1)}, u32[]{:S(2)}, u32[]{:S(2)}) collective-permute-start(bf16[4,4096]{1,0:T(4,128)(2,1)S(1)} %pad_maximum_fusion.8), channel_id=1, source_target_pairs={{0,16},{1,17},{2,18},{3,19},{4,20},{5,21},{6,22},{7,23},{8,72},{9,... | collective-permute-start | bytes 98312 | tf_op jit(solution)/shard_map/ppermute | solution.py:49
  6.2 6.4 %collective-permute-start.1 = (bf16[8,4096]{1,0:T(8,128)(2,1)S(1)}, bf16[8,4096]{1,0:T(8,128)(2,1)S(1)}, u32[]{:S(2)}, u32[]{:S(2)}) collective-permute-start(bf16[8,4096]{1,0:T(8,128)(2,1)S(1)} %pad_maximum_fusion.7), channel_id=1, source_target_pairs={{0,48},{1,49},{2,50},{3,51},{4,52},{5,53},{6,54},{7,55},{8,73},{9,... | collective-permute-start | bytes 196616 | tf_op jit(solution)/shard_map/ppermute | solution.py:49
  13.5 5.0 %collective-permute-start.2 = (bf16[16,4096]{1,0:T(8,128)(2,1)S(1)}, bf16[16,4096]{1,0:T(8,128)(2,1)S(1)}, u32[]{:S(2)}, u32[]{:S(2)}) collective-permute-start(bf16[16,4096]{1,0:T(8,128)(2,1)S(1)} %pad_maximum_fusion.6), channel_id=1, source_target_pairs={{0,2},{1,3},{2,0},{3,1},{4,6},{5,7},{6,4},{7,5},{8,24},{9,25},{10,... | collective-permute-start | bytes 393224 | tf_op jit(solution)/shard_map/ppermute | solution.py:49
  19.3 7.9 %collective-permute-start.3 = (bf16[32,4096]{1,0:T(8,128)(2,1)S(1)}, bf16[32,4096]{1,0:T(8,128)(2,1)S(1)}, u32[]{:S(2)}, u32[]{:S(2)}) collective-permute-start(bf16[32,4096]{1,0:T(8,128)(2,1)S(1)} %pad_maximum_fusion.5), channel_id=1, source_target_pairs={{0,6},{1,7},{2,4},{3,5},{4,2},{5,3},{6,0},{7,1},{8,56},{9,57},{10,... | collective-permute-start | bytes 786440 | tf_op jit(solution)/shard_map/ppermute | solution.py:49
  22.4 18.6 %copy-start.6 = (bf16[1,4,2048]{2,1,0:T(4,128)(2,1)S(1)}, bf16[1,4,2048]{2,1,0:T(4,128)(2,1)}, u32[]{:S(2)}) copy-start(bf16[1,4,2048]{2,1,0:T(4,128)(2,1)} %param.19) | copy-start | bytes 49156
  22.4 18.7 %copy-start.7 = (bf16[1,4,2048]{2,1,0:T(4,128)(2,1)S(1)}, bf16[1,4,2048]{2,1,0:T(4,128)(2,1)}, u32[]{:S(2)}) copy-start(bf16[1,4,2048]{2,1,0:T(4,128)(2,1)} %param.20) | copy-start | bytes 49156
  22.4 18.7 %copy-start.8 = (bf16[1,4,2048]{2,1,0:T(4,128)(2,1)S(1)}, bf16[1,4,2048]{2,1,0:T(4,128)(2,1)}, u32[]{:S(2)}) copy-start(bf16[1,4,2048]{2,1,0:T(4,128)(2,1)} %param.21) | copy-start | bytes 49156
  22.4 18.7 %copy-start.9 = (bf16[1,4,2048]{2,1,0:T(4,128)(2,1)S(1)}, bf16[1,4,2048]{2,1,0:T(4,128)(2,1)}, u32[]{:S(2)}) copy-start(bf16[1,4,2048]{2,1,0:T(4,128)(2,1)} %param.18) | copy-start | bytes 49156
  27.4 7.7 %collective-permute-start.6 = (bf16[64,2048]{1,0:T(8,128)(2,1)S(1)}, bf16[64,2048]{1,0:T(8,128)(2,1)S(1)}, u32[]{:S(2)}, u32[]{:S(2)}) collective-permute-start(bf16[64,2048]{1,0:T(8,128)(2,1)S(1)} %get-tuple-element.32), channel_id=1, source_target_pairs={{0,65},{1,64},{2,67},{3,66},{4,69},{5,68},{6,71},{7,70},{8,14},{9,... | collective-permute-start | bytes 786440 | tf_op jit(solution)/shard_map/ppermute | solution.py:49
  31.0 6.5 %collective-permute-start.4 = (bf16[64,2048]{1,0:T(8,128)(2,1)S(1)}, bf16[64,2048]{1,0:T(8,128)(2,1)S(1)}, u32[]{:S(2)}, u32[]{:S(2)}) collective-permute-start(bf16[64,2048]{1,0:T(8,128)(2,1)S(1)} %get-tuple-element.33), channel_id=1, source_target_pairs={{0,64},{1,65},{2,66},{3,67},{4,68},{5,69},{6,70},{7,71},{8,10},{9,... | collective-permute-start | bytes 786440 | tf_op jit(solution)/shard_map/ppermute | solution.py:49
  35.9 9.5 %collective-permute-start.7 = (bf16[128,2048]{1,0:T(8,128)(2,1)}, bf16[128,2048]{1,0:T(8,128)(2,1)}, u32[]{:S(2)}, u32[]{:S(2)}) collective-permute-start(bf16[128,2048]{1,0:T(8,128)(2,1)} %pad_maximum_fusion.3), channel_id=1, source_target_pairs={{0,64},{1,65},{2,66},{3,67},{4,68},{5,69},{6,70},{7,71},{8,10},{9,... | collective-permute-start | bytes 1572872 | tf_op jit(solution)/shard_map/ppermute | solution.py:49
  37.4 13.0 %copy-start.2 = (bf16[1,512,2048]{2,1,0:T(8,128)(2,1)S(1)}, bf16[1,512,2048]{2,1,0:T(8,128)(2,1)}, u32[]{:S(2)}) copy-start(bf16[1,512,2048]{2,1,0:T(8,128)(2,1)} %v_ref.3) | copy-start | bytes 6291460
  38.3 10.7 %collective-permute-start.5 = (bf16[128,2048]{1,0:T(8,128)(2,1)}, bf16[128,2048]{1,0:T(8,128)(2,1)}, u32[]{:S(2)}, u32[]{:S(2)}) collective-permute-start(bf16[128,2048]{1,0:T(8,128)(2,1)} %pad_maximum_fusion.2), channel_id=1, source_target_pairs={{0,65},{1,64},{2,67},{3,66},{4,69},{5,68},{6,71},{7,70},{8,14},{9,... | collective-permute-start | bytes 1572872 | tf_op jit(solution)/shard_map/ppermute | solution.py:49
  45.4 5.0 %copy-start.1 = (bf16[1,512,2048]{2,1,0:T(8,128)(2,1)S(1)}, bf16[1,512,2048]{2,1,0:T(8,128)(2,1)}, u32[]{:S(2)}) copy-start(bf16[1,512,2048]{2,1,0:T(8,128)(2,1)} %k_ref.3) | copy-start | bytes 6291460
  46.7 3.7 %copy-start = (bf16[1,512,2048]{2,1,0:T(8,128)(2,1)S(1)}, bf16[1,512,2048]{2,1,0:T(8,128)(2,1)}, u32[]{:S(2)}) copy-start(bf16[1,512,2048]{2,1,0:T(8,128)(2,1)} %q_ref.5) | copy-start | bytes 6291460
  46.7 13.2 %collective-permute-start.9 = (bf16[256,2048]{1,0:T(8,128)(2,1)S(1)}, bf16[256,2048]{1,0:T(8,128)(2,1)S(1)}, u32[]{:S(2)}, u32[]{:S(2)}) collective-permute-start(bf16[256,2048]{1,0:T(8,128)(2,1)S(1)} %pad_maximum_fusion.1.fv_ref), channel_id=1, source_target_pairs={{0,8},{8,0},{1,9},{9,1},{2,10},{10,2},{3,11},{11,3},{4,12},{12,4},... | collective-permute-start | bytes 3145736 | tf_op jit(solution)/shard_map/ppermute | solution.py:53
  50.1 9.8 %collective-permute-start.8 = (bf16[256,2048]{1,0:T(8,128)(2,1)S(1)}, bf16[256,2048]{1,0:T(8,128)(2,1)S(1)}, u32[]{:S(2)}, u32[]{:S(2)}) collective-permute-start(bf16[256,2048]{1,0:T(8,128)(2,1)S(1)} %pad_maximum_fusion.fk_ref), channel_id=1, source_target_pairs={{0,8},{8,0},{1,9},{9,1},{2,10},{10,2},{3,11},{11,3},{4,12},{12,4},... | collective-permute-start | bytes 3145736 | tf_op jit(solution)/shard_map/ppermute | solution.py:53
  50.5 1.6 %copy-start.3 = (bf16[1,512,2048]{2,1,0:T(8,128)(2,1)S(1)}, bf16[1,512,2048]{2,1,0:T(8,128)(2,1)}, u32[]{:S(2)}) copy-start(bf16[1,512,2048]{2,1,0:T(8,128)(2,1)} %g_ref.5) | copy-start | bytes 6291460
  52.0 8.0 %copy-start.4 = (bf16[1,512,2048]{2,1,0:T(8,128)(2,1)S(1)}, bf16[1,512,2048]{2,1,0:T(8,128)(2,1)}, u32[]{:S(2)}) copy-start(bf16[1,512,2048]{2,1,0:T(8,128)(2,1)} %g_ref.5) | copy-start | bytes 6291460
  86.0 2.8 %collective-permute-start.10 = (bf16[256,2048]{1,0:T(8,128)(2,1)S(1)}, bf16[256,2048]{1,0:T(8,128)(2,1)S(1)}, u32[]{:S(2)}, u32[]{:S(2)}) collective-permute-start(bf16[256,2048]{1,0:T(8,128)(2,1)S(1)} %get-tuple-element.28), channel_id=1, source_target_pairs={{0,8},{8,0},{1,9},{9,1},{2,10},{10,2},{3,11},{11,3},{4,12},{12,4},... | collective-permute-start | bytes 3145736 | tf_op jit(solution)/shard_map/ppermute | solution.py:53
  86.5 4.9 %collective-permute-start.13 = (bf16[256,2048]{1,0:T(8,128)(2,1)S(1)}, bf16[256,2048]{1,0:T(8,128)(2,1)S(1)}, u32[]{:S(2)}, u32[]{:S(2)}) collective-permute-start(bf16[256,2048]{1,0:T(8,128)(2,1)S(1)} %get-tuple-element.30), channel_id=1, source_target_pairs={{0,8},{8,0},{1,9},{9,1},{2,10},{10,2},{3,11},{11,3},{4,12},{12,4},... | collective-permute-start | bytes 3145736 | tf_op jit(solution)/shard_map/ppermute | solution.py:53
  89.2 10.5 %collective-permute-start.11 = (bf16[128,2048]{1,0:T(8,128)(2,1)S(1)}, bf16[128,2048]{1,0:T(8,128)(2,1)S(1)}, u32[]{:S(2)}, u32[]{:S(2)}) collective-permute-start(bf16[128,2048]{1,0:T(8,128)(2,1)S(1)} %slice.111), channel_id=1, source_target_pairs={{0,65},{1,64},{2,67},{3,66},{4,69},{5,68},{6,71},{7,70},{8,14},{9,... | collective-permute-start | bytes 1572872 | tf_op jit(solution)/shard_map/ppermute | solution.py:49
  91.8 9.3 %collective-permute-start.14 = (bf16[128,2048]{1,0:T(8,128)(2,1)S(1)}, bf16[128,2048]{1,0:T(8,128)(2,1)S(1)}, u32[]{:S(2)}, u32[]{:S(2)}) collective-permute-start(bf16[128,2048]{1,0:T(8,128)(2,1)S(1)} %slice.115), channel_id=1, source_target_pairs={{0,64},{1,65},{2,66},{3,67},{4,68},{5,69},{6,70},{7,71},{8,10},{9,... | collective-permute-start | bytes 1572872 | tf_op jit(solution)/shard_map/ppermute | solution.py:49
  99.9 6.5 %collective-permute-start.12 = (bf16[64,2048]{1,0:T(8,128)(2,1)S(1)}, bf16[64,2048]{1,0:T(8,128)(2,1)S(1)}, u32[]{:S(2)}, u32[]{:S(2)}) collective-permute-start(bf16[64,2048]{1,0:T(8,128)(2,1)S(1)} %slice.113), channel_id=1, source_target_pairs={{0,64},{1,65},{2,66},{3,67},{4,68},{5,69},{6,70},{7,71},{8,10},{9,... | collective-permute-start | bytes 786440 | tf_op jit(solution)/shard_map/ppermute | solution.py:49
  101.3 26.6 %copy-start.5 = (f32[2048,512]{1,0:T(8,128)S(1)}, f32[2048,512]{1,0:T(8,128)}, u32[]{:S(2)}) copy-start(f32[2048,512]{1,0:T(8,128)} %get-tuple-element.20.dqf_ref) | copy-start | bytes 12582916
  101.3 7.7 %collective-permute-start.15 = (bf16[64,2048]{1,0:T(8,128)(2,1)S(1)}, bf16[64,2048]{1,0:T(8,128)(2,1)S(1)}, u32[]{:S(2)}, u32[]{:S(2)}) collective-permute-start(bf16[64,2048]{1,0:T(8,128)(2,1)S(1)} %slice.117), channel_id=1, source_target_pairs={{0,65},{1,64},{2,67},{3,66},{4,69},{5,68},{6,71},{7,70},{8,14},{9,... | collective-permute-start | bytes 786440 | tf_op jit(solution)/shard_map/ppermute | solution.py:49
  109.0 7.7 %collective-permute-start.16 = (bf16[32,4096]{1,0:T(8,128)(2,1)S(1)}, bf16[32,4096]{1,0:T(8,128)(2,1)S(1)}, u32[]{:S(2)}, u32[]{:S(2)}) collective-permute-start(bf16[32,4096]{1,0:T(8,128)(2,1)S(1)} %pad_maximum_fusion.4), channel_id=1, source_target_pairs={{0,6},{1,7},{2,4},{3,5},{4,2},{5,3},{6,0},{7,1},{8,56},{9,57},{10,... | collective-permute-start | bytes 786440 | tf_op jit(solution)/shard_map/ppermute | solution.py:49
  116.8 5.0 %collective-permute-start.17 = (bf16[16,4096]{1,0:T(8,128)(2,1)S(1)}, bf16[16,4096]{1,0:T(8,128)(2,1)S(1)}, u32[]{:S(2)}, u32[]{:S(2)}) collective-permute-start(bf16[16,4096]{1,0:T(8,128)(2,1)S(1)} %slice.121), channel_id=1, source_target_pairs={{0,2},{1,3},{2,0},{3,1},{4,6},{5,7},{6,4},{7,5},{8,24},{9,25},{10,... | collective-permute-start | bytes 393224 | tf_op jit(solution)/shard_map/ppermute | solution.py:49
  121.9 5.9 %collective-permute-start.18 = (bf16[8,4096]{1,0:T(8,128)(2,1)S(1)}, bf16[8,4096]{1,0:T(8,128)(2,1)S(1)}, u32[]{:S(2)}, u32[]{:S(2)}) collective-permute-start(bf16[8,4096]{1,0:T(8,128)(2,1)S(1)} %slice.123), channel_id=1, source_target_pairs={{0,48},{1,49},{2,50},{3,51},{4,52},{5,53},{6,54},{7,55},{8,73},{9,... | collective-permute-start | bytes 196616 | tf_op jit(solution)/shard_map/ppermute | solution.py:49
  127.8 17.3 %collective-permute-start.19 = (bf16[4,4096]{1,0:T(4,128)(2,1)S(1)}, bf16[4,4096]{1,0:T(4,128)(2,1)S(1)}, u32[]{:S(2)}, u32[]{:S(2)}) collective-permute-start(bf16[4,4096]{1,0:T(4,128)(2,1)S(1)} %slice.125), channel_id=1, source_target_pairs={{0,16},{1,17},{2,18},{3,19},{4,20},{5,21},{6,22},{7,23},{8,72},{9,... | collective-permute-start | bytes 98312 | tf_op jit(solution)/shard_map/ppermute | solution.py:49

commit v2 on v1

v2 whole, which is shorter than its diff:
```python
import math

import jax
import jax.numpy as jnp
import numpy as np
from jax import lax
from jax.experimental import pallas as pl
from jax.experimental.pallas import tpu as pltpu
from jax.sharding import Mesh
from jax.sharding import PartitionSpec as P

HEAD_DIM = 128
PAIR = 2 * HEAD_DIM
BEACONS = 4
STRETCH = 512
FEAT = 2048
PAIRS = FEAT // PAIR
LANES = 128
HALF = 256
BLOCK = 64
SCALE = HEAD_DIM ** (-0.5)
LOG_SCALE = SCALE * math.log2(math.e)
HIDDEN = -1e30
F32 = jnp.float32
BF16 = jnp.bfloat16

NAMES = ("x_lo", "z", "core", "y", "x_hi")
SIZES = (2, 4, 2, 4, 2)

X0, X1, Y0, Y1, Z0, Z1 = 1, 2, 4, 8, 16, 32
STEPS = ((Z0, Z1, Y0, Y1, X0, X1), (X0, X1, Z0, Z1, Y0, Y1))


def gray(position):
    return position ^ (position >> 1)


def slot_of(label, core):
    x, y, z = (gray((label >> shift) & 3) for shift in (0, 2, 4))
    return ((((x & 1) * 4 + z) * 2 + core) * 4 + y) * 2 + (x >> 1)


def exchange(value, step):
    pairs = []
    for label in range(64):
        for core in range(2):
            partner = label ^ STEPS[core][step]
            pairs.append((slot_of(label, core), slot_of(partner, core)))
    return lax.ppermute(value, NAMES, sorted(pairs))


def swap(value):
    return lax.ppermute(value, "core", [(0, 1), (1, 0)])


def beside(values, token, work):
    values, token = lax.optimization_barrier((values, token))
    return lax.optimization_barrier(work(values, token))


def joined(kept, got, axis=0):
    return lax.optimization_barrier(jnp.concatenate([kept, got], axis=axis))


def added(first, *more):
    total = first.astype(F32)
    for term in more:
        total = total + term.astype(F32)
    return total.astype(BF16)


def mask_kernel(place_ref, assign_ref, prefix_ref, bias_ref):
    mine, core, own = place_ref[0, 0], place_ref[0, 1], place_ref[0, 2]
    numbers = lax.broadcasted_iota(jnp.int32, (1, LANES), 1)
    assign, prefix = assign_ref[...], prefix_ref[...]

    def pick(values, index):
        return jnp.sum(jnp.where(numbers == index, values, 0).astype(F32), axis=1, keepdims=True)

    stretch = pick(assign, own).astype(jnp.int32)
    lowest = stretch - pick(prefix, stretch).astype(jnp.int32)
    seen = jnp.where((assign >= lowest) & (assign < stretch), 1.0, 0.0)
    place = lax.broadcasted_iota(jnp.int32, (HALF, LANES), 0) >> 2
    labels = []
    for steps in STEPS:
        label = jnp.full((HALF, LANES), mine, jnp.int32)
        for step, bit in enumerate(steps):
            label = label ^ (((place >> step) & 1) * bit)
        labels.append(label)
    for half in range(2):
        label = jnp.where(core == half, labels[0], labels[1])
        slots = slot_of(label, core if half == 0 else 1 - core)
        found = jnp.sum(jnp.where(slots == numbers, seen, 0.0), axis=1, keepdims=True)
        rows = slice(half * HALF, (half + 1) * HALF)
        bias_ref[rows] = jnp.broadcast_to(jnp.where(found > 0.5, 0.0, HIDDEN), (HALF, LANES))


def far_bias(assign, prefix):
    x_lo, z, core, y, x_hi = (lax.axis_index(name) for name in NAMES)
    mine = gray(x_hi * 2 + x_lo) | (gray(y) << 2) | (gray(z) << 4)
    place = jnp.stack([mine, core, slot_of(mine, core)]).astype(jnp.int32).reshape(1, 3)
    line = pl.BlockSpec((1, LANES), lambda: (0, 0))
    return pl.pallas_call(
        mask_kernel,
        in_specs=[pl.BlockSpec(memory_space=pltpu.SMEM), line, line],
        out_specs=pl.BlockSpec((2 * HALF, LANES), lambda: (0, 0)),
        out_shape=jax.ShapeDtypeStruct((2 * HALF, LANES), F32),
        name="far_mask",
    )(place, assign.reshape(1, LANES), prefix.reshape(1, LANES))


def spread(rows):
    twice = jnp.concatenate([rows.astype(F32)] * 2, axis=0)
    row = lax.broadcasted_iota(jnp.int32, twice.shape, 0)
    column = lax.broadcasted_iota(jnp.int32, twice.shape, 1)
    kept = jnp.where((row < BEACONS) == (column < HEAD_DIM), twice, 0.0)
    rest = jnp.zeros((LANES - 2 * BEACONS, rows.shape[1]), F32)
    return jnp.concatenate([kept, rest], axis=0).astype(BF16)


def padded(rows):
    rest = jnp.zeros((12, rows.shape[1]), F32)
    return jnp.concatenate([rows.astype(F32), rest], axis=0).astype(BF16)


def nt(a, b):
    return lax.dot_general(a, b, (((1,), (1,)), ((), ())), preferred_element_type=F32)


def nn(a, b):
    return lax.dot_general(a, b, (((1,), (0,)), ((), ())), preferred_element_type=F32)


def tn(a, b):
    return lax.dot_general(a, b, (((0,), (0,)), ((), ())), preferred_element_type=F32)


def top_of(scores):
    return jnp.max(scores, axis=0, keepdims=True)


def sum_of(values):
    return jnp.sum(values, axis=0, keepdims=True)


def causal(scores):
    rows = lax.broadcasted_iota(jnp.int32, scores.shape, 0)
    columns = lax.broadcasted_iota(jnp.int32, scores.shape, 1)
    return jnp.where(rows <= columns, scores, HIDDEN)


def own_mask(scores):
    rows = lax.broadcasted_iota(jnp.int32, scores.shape, 0)
    columns = lax.broadcasted_iota(jnp.int32, scores.shape, 1)
    return jnp.where((rows <= (columns & 3)) & (rows < BEACONS), scores, HIDDEN)


def power(scores, top):
    return jnp.exp2((scores - top) * LOG_SCALE)


def stats_of(parts):
    top = top_of(parts[0][0])
    for scores, _ in parts[1:]:
        top = jnp.maximum(top, top_of(scores))
    total = inner = None
    for scores, dprobs in parts:
        weights = power(scores, top)
        part, part_inner = sum_of(weights), sum_of(weights * dprobs)
        total = part if total is None else total + part
        inner = part_inner if inner is None else inner + part_inner
    return top, total, inner


def head(index):
    return slice(index * HEAD_DIM, (index + 1) * HEAD_DIM)


def raw_parts(q, k, v, g):
    low, high = slice(0, HALF), slice(HALF, 2 * HALF)
    s00 = causal(nt(k[low], q[low]))
    s01 = nt(k[low], q[high])
    s11 = causal(nt(k[high], q[high]))
    d00 = nt(v[low], g[low])
    d01 = nt(v[low], g[high])
    d11 = nt(v[high], g[high])
    return (s00, d00), (s01, d01), (s11, d11)


def stats_kernel(q_ref, k_ref, v_ref, g_ref, bq_ref, bk_ref, bv_ref, bg_ref, *refs):
    st_ref = refs[-1]
    qb, gb = spread(bq_ref[...]), spread(bg_ref[...])

    def products(index):
        if index < 0:
            raw = nt(k_ref[...], qb), nt(v_ref[...], gb)
            return raw, (own_mask(nt(padded(bk_ref[...]), qb)), nt(padded(bv_ref[...]), gb))
        columns = head(index)
        return raw_parts(
            q_ref[:, columns], k_ref[:, columns], v_ref[:, columns], g_ref[:, columns]
        )

    def store(index, *parts):
        if index < 0:
            found = ((STRETCH, LANES, stats_of(parts)),)
        else:
            p00, p01, p11 = parts
            found = ((0, HALF, stats_of([p00])), (HALF, HALF, stats_of([p01, p11])))
        for place, width, stats in found:
            for row, entry in enumerate(stats):
                row += 3 * max(index, 0)
                st_ref[row : row + 1, place : place + width] = entry

    pipelined([(-1,), (0,), (1,)], products, store)


def units_of(q_ref):
    return [(pair, index) for pair in range(q_ref.shape[1] // PAIR) for index in (-1, 0, 1)]


def columns_of(pair, index):
    if index < 0:
        return slice(pair * PAIR, (pair + 1) * PAIR)
    return head(2 * pair + index)


def block_columns(pair, index, value):
    start = 2 * pair * PAIR + (PAIR if value else 0)
    if index < 0:
        return slice(start, start + PAIR)
    return slice(start + index * HEAD_DIM, start + (index + 1) * HEAD_DIM)


def lanes_of(index):
    return slice(STRETCH, STAT_LANES) if index < 0 else slice(0, STRETCH)


def read_stats(ref, pair, index):
    base = 3 * max(index, 0)
    return tuple(ref[pair, base + row : base + row + 1, lanes_of(index)] for row in range(3))


def write_stats(ref, pair, index, stats):
    base = 3 * max(index, 0)
    for row, entry in enumerate(stats):
        ref[pair, base + row : base + row + 1, lanes_of(index)] = entry


def final_of(stats):
    top, total, inner = stats
    scaled = 1.0 / total
    return top, scaled, inner * scaled


def spread_pairs(*refs):
    pairs = refs[0].shape[1] // PAIR
    return [
        [spread(ref[:, pair * PAIR : (pair + 1) * PAIR]) for ref in refs] for pair in range(pairs)
    ]


def rows_of(refs, columns):
    return jnp.concatenate([ref[:, columns] for ref in refs], axis=0)


def pipelined(units, first, second):
    ready = first(*units[0])
    for place, unit in enumerate(units):
        now = ready
        if place + 1 < len(units):
            ready = first(*units[place + 1])
        second(*unit, *now)


def weighed(scores, dprobs, before, pair, index):
    known = [read_stats(ref, pair, index) for ref in before]
    top = top_of(scores)
    for stats in known:
        top = jnp.maximum(top, stats[0])
    weights = power(scores, top)
    total, inner = sum_of(weights), sum_of(weights * dprobs)
    for stats in known:
        factor = power(stats[0], top)
        total, inner = total + stats[1] * factor, inner + stats[2] * factor
    return weights, (top, total, inner)


def weigh_kernel(places, priors, *refs):
    q_ref, g_ref, bq_ref, bg_ref, bias_ref = refs[:5]
    blocks, before = refs[5 : 5 + len(places)], refs[5 + len(places) : 5 + len(places) + priors]
    w_ref, wb_ref, out_ref = refs[-3:]
    bias = jnp.concatenate([bias_ref[place * BLOCK : (place + 1) * BLOCK] for place in places], 0)
    wide = jnp.concatenate([bias] * 4, axis=1)
    spreads = spread_pairs(bq_ref, bg_ref)

    def products(pair, index):
        columns = columns_of(pair, index)
        if index < 0:
            (q, g), hidden = spreads[pair], bias
        else:
            q, g, hidden = q_ref[:, columns], g_ref[:, columns], wide
        key = rows_of(blocks, block_columns(pair, index, False))
        value = rows_of(blocks, block_columns(pair, index, True))
        return nt(key, q) + hidden, nt(value, g)

    def weigh(pair, index, scores, dprobs):
        weights, stats = weighed(scores, dprobs, before, pair, index)
        write_stats(out_ref, pair, index, stats)
        if index < 0:
            wb_ref[pair] = weights.astype(BF16)
        else:
            w_ref[2 * pair + index] = weights.astype(BF16)

    pipelined(units_of(q_ref), products, weigh)


def diagonal_kernel(places, priors, *refs):
    q_ref, g_ref, bq_ref, bg_ref, bias_ref = refs[:5]
    blocks, before = refs[5:7], refs[7 : 7 + priors]
    d_refs, ds_ref, dsb_ref, out_ref = refs[-5:-3], refs[-3], refs[-2], refs[-1]
    bias = jnp.concatenate([bias_ref[place * BLOCK : (place + 1) * BLOCK] for place in places], 0)
    wide = jnp.concatenate([bias] * 4, axis=1)
    spreads = spread_pairs(bq_ref, bg_ref)
    beacon = {}

    def products(pair, index):
        columns = columns_of(pair, index)
        if index < 0:
            (q, g), hidden = spreads[pair], bias
        else:
            q, g, hidden = q_ref[:, columns], g_ref[:, columns], wide
        key = rows_of(blocks, block_columns(pair, index, False))
        value = rows_of(blocks, block_columns(pair, index, True))
        return nt(key, q) + hidden, nt(value, g)

    def finish(pair, index, scores, dprobs):
        weights, stats = weighed(scores, dprobs, before, pair, index)
        write_stats(out_ref, pair, index, stats)
        _, scaled, inner = final_of(stats)
        probs = weights * scaled
        dscores = (probs * (dprobs - inner)).astype(BF16)
        store_terms(
            pair, index, probs.astype(BF16), dscores, beacon, spreads, q_ref, g_ref,
            d_refs, ds_ref, dsb_ref,
        )

    pipelined(units_of(q_ref), products, finish)


def store_terms(
    pair, index, probs, dscores, beacon, spreads, q_ref, g_ref, d_refs, ds_ref, dsb_ref
):
    if index < 0:
        qb, gb = spreads[pair]
        beacon[pair] = nn(dscores, qb), nn(probs, gb)
        dsb_ref[pair] = dscores
        return
    columns = columns_of(pair, index)
    dkey, dvalue = beacon[pair]
    ds_ref[2 * pair + index] = dscores
    head_key = ((nn(dscores, q_ref[:, columns]) + dkey[:, head(index)]) * SCALE).astype(BF16)
    head_value = (nn(probs, g_ref[:, columns]) + dvalue[:, head(index)]).astype(BF16)
    rows = head_key.shape[0] // len(d_refs)
    for place, d_ref in enumerate(d_refs):
        some = slice(place * rows, (place + 1) * rows)
        d_ref[:, block_columns(pair, index, False)] = head_key[some]
        d_ref[:, block_columns(pair, index, True)] = head_value[some]


def terms_kernel(counts, *refs):
    q_ref, g_ref, bq_ref, bg_ref, final_ref = refs[:5]
    blocks = refs[5 : 5 + sum(counts)]
    calls = refs[5 + sum(counts) : 5 + sum(counts) + 3 * len(counts)]
    d_ref, ds_ref, dsb_ref = refs[-3:]
    spreads = spread_pairs(bq_ref, bg_ref)
    beacon = {}

    def products(pair, index):
        g = spreads[pair][1] if index < 0 else g_ref[:, columns_of(pair, index)]
        return (nt(rows_of(blocks, block_columns(pair, index, True)), g),)

    def finish(pair, index, dprobs):
        top, scaled, inner = final_of(read_stats(final_ref, pair, index))
        parts = []
        for place in range(len(counts)):
            w_ref, wb_ref, st_ref = calls[3 * place : 3 * place + 3]
            weights = wb_ref[pair] if index < 0 else w_ref[2 * pair + index]
            factor = power(read_stats(st_ref, pair, index)[0], top) * scaled
            parts.append(weights.astype(F32) * factor)
        probs = jnp.concatenate(parts, axis=0)
        dscores = (probs * (dprobs - inner)).astype(BF16)
        probs = probs.astype(BF16)
        store_terms(
            pair, index, probs, dscores, beacon, spreads, q_ref, g_ref, (d_ref,), ds_ref, dsb_ref
        )

    pipelined(units_of(q_ref), products, finish)


def split_grad(weights, dprobs, stats):
    _, scaled, inner = stats
    probs = weights * scaled
    return probs.astype(BF16), (probs * (dprobs - inner)).astype(BF16)


def grads(scores, dprobs, stats):
    return split_grad(power(scores, stats[0]), dprobs, stats)


def raw_kernel(*refs):
    q_ref, k_ref, v_ref, g_ref, bq_ref, bk_ref, bv_ref, bg_ref, st_ref = refs[:9]
    far = rows_of(refs[9:17], slice(0, PAIR))
    far_ds = refs[17:20]
    far_dsb = jnp.concatenate([ref[...] for ref in refs[20:23]], axis=0)
    dq_ref, dk_ref, dv_ref, dbq_ref, own_k_ref, own_v_ref = refs[-6:]
    qb, gb = spread(bq_ref[...]), spread(bg_ref[...])
    key, value = k_ref[...], v_ref[...]
    stats = final_of(tuple(st_ref[row : row + 1, STRETCH:] for row in range(3)))
    probs, dscores = grads(nt(key, qb), nt(value, gb), stats)
    dkey, dvalue = nn(dscores, qb), nn(probs, gb)
    dqb = tn(dscores, key) + tn(far_dsb, far)
    dqb = dqb[: 2 * BEACONS]
    own_key = padded(bk_ref[...])
    probs, dscores = grads(own_mask(nt(own_key, qb)), nt(padded(bv_ref[...]), gb), stats)
    own_k_ref[...] = nn(dscores, qb)[: 2 * BEACONS] * SCALE
    own_v_ref[...] = nn(probs, gb)[: 2 * BEACONS]
    dqb = (dqb + tn(dscores, own_key)[: 2 * BEACONS]) * SCALE
    dbq_ref[:, head(0)] = dqb[:BEACONS, head(0)].astype(BF16)
    dbq_ref[:, head(1)] = dqb[BEACONS:, head(1)].astype(BF16)
    low, high = slice(0, HALF), slice(HALF, 2 * HALF)

    def products(index):
        columns = head(index)
        return raw_parts(q_ref[:, columns], key[:, columns], value[:, columns], g_ref[:, columns])

    def finish(index, p00, p01, p11):
        columns = head(index)
        q, k, g = q_ref[:, columns], key[:, columns], g_ref[:, columns]
        stats = tuple(st_ref[3 * index + row : 3 * index + row + 1, :STRETCH] for row in range(3))
        stats = final_of(stats)
        first = tuple(entry[:, low] for entry in stats)
        second = tuple(entry[:, high] for entry in stats)
        probs00, ds00 = grads(*p00, first)
        probs01, ds01 = grads(*p01, second)
        probs11, ds11 = grads(*p11, second)
        dk_ref[low, columns] = (
            (nn(ds00, q[low]) + nn(ds01, q[high]) + dkey[low, columns]) * SCALE
        ).astype(BF16)
        dk_ref[high, columns] = ((nn(ds11, q[high]) + dkey[high, columns]) * SCALE).astype(BF16)
        dv_ref[low, columns] = (
            nn(probs00, g[low]) + nn(probs01, g[high]) + dvalue[low, columns]
        ).astype(BF16)
        dv_ref[high, columns] = (nn(probs11, g[high]) + dvalue[high, columns]).astype(BF16)
        ds_far = jnp.concatenate([ref[index] for ref in far_ds], axis=0)
        dq_far = tn(far[:, columns], ds_far)
        dq_low = dq_far[:, low] + tn(k[low], ds00)
        dq_high = dq_far[:, high] + tn(k[low], ds01) + tn(k[high], ds11)
        dq_ref[low, columns] = (dq_low.T * SCALE).astype(BF16)
        dq_ref[high, columns] = (dq_high.T * SCALE).astype(BF16)

    pipelined([(0,), (1,)], products, finish)


def three(rows, start=0, pairs=1):
    return pl.BlockSpec((None, rows, PAIR * pairs), lambda step: (0, 0, start + step))


def two(rows, start=0, pairs=1):
    return pl.BlockSpec((rows, PAIR * pairs), lambda step: (0, start + step))


def paired(rows, columns, start=0, pairs=None):
    return pl.BlockSpec((pairs, rows, columns), lambda step: (start + step, 0, 0))


def shape(dims, dtype):
    return jax.ShapeDtypeStruct(dims, dtype)


def params(megabytes):
    return pltpu.CompilerParams(
        dimension_semantics=("arbitrary",), vmem_limit_bytes=megabytes * 1024 * 1024
    )


def cost(flops, moved):
    return pl.CostEstimate(flops=flops, bytes_accessed=moved, transcendentals=0)


STAT_LANES = STRETCH + LANES


def pieces(kernel, start, count, inputs, in_specs, out_specs, out_shape, before, name, flops, megabytes):
    before = tuple(before)
    aliases = {len(inputs) + place: place for place in range(len(before))}
    return pl.pallas_call(
        kernel,
        grid=(count,),
        in_specs=in_specs + [pl.BlockSpec(memory_space=pl.ANY)] * len(before),
        out_specs=out_specs,
        out_shape=out_shape,
        input_output_aliases=aliases,
        compiler_params=params(megabytes),
        cost_estimate=cost(flops, 2**10),
        name=name,
    )(*inputs, *before)


def raw_stats(start, count, inputs, before):
    raw = three(STRETCH, start)
    return pieces(
        stats_kernel,
        start, count, inputs,
        [raw] * 4 + [three(BEACONS, start)] * 4,
        [paired(8, STAT_LANES, start)],
        [shape((PAIRS, 8, STAT_LANES), F32)],
        before, f"raw_stats_{start}", 10**6, 56,
    )


def raw_grads(start, count, inputs, before):
    raw = three(STRETCH, start)
    rows = (2 * BLOCK, 3 * BLOCK, 3 * BLOCK)
    return pieces(
        raw_kernel,
        start, count, inputs,
        [raw] * 4
        + [three(BEACONS, start)] * 4
        + [paired(8, STAT_LANES, start)]
        + [pl.BlockSpec((BLOCK, 2 * PAIR), lambda step: (0, start + step))] * 8
        + [paired(count_rows, STRETCH, start, 2) for count_rows in rows]
        + [paired(count_rows, LANES, start) for count_rows in rows],
        [raw] * 3 + [three(BEACONS, start)] + [two(8, start)] * 2,
        [shape((1, STRETCH, FEAT), BF16)] * 3
        + [shape((1, BEACONS, FEAT), BF16)]
        + [shape((8, FEAT), F32)] * 2,
        before, f"raw_grads_{start}", 10**6, 16,
    )


STEP_PAIRS = 2


def block_spec(rows=BLOCK):
    return pl.BlockSpec((rows, 2 * PAIR * STEP_PAIRS), lambda step: (0, step))


def some_rows(rows, columns, per_pair, place=0):
    return pl.BlockSpec((per_pair * STEP_PAIRS, rows, columns), lambda step: (step, place, 0))


def far_call(kernel, name, inputs, in_specs, out_specs, out_shape, flops):
    shared = [three(STRETCH, 0, STEP_PAIRS)] * 2 + [three(BEACONS, 0, STEP_PAIRS)] * 2
    return pl.pallas_call(
        kernel,
        grid=(PAIRS // STEP_PAIRS,),
        in_specs=shared + in_specs,
        out_specs=out_specs,
        out_shape=out_shape,
        compiler_params=params(18),
        cost_estimate=cost(flops, 2**10),
        name=name,
    )(*inputs)


def stat_spec():
    return paired(8, STAT_LANES, 0, STEP_PAIRS)


def weigh(places, queries, bias, blocks, before):
    rows = BLOCK * len(places)
    return far_call(
        lambda *refs: weigh_kernel(places, len(before), *refs),
        "far_weights_" + "_".join(map(str, places)),
        (*queries, bias, *blocks, *before),
        [pl.BlockSpec((2 * HALF, LANES), lambda step: (0, 0))]
        + [block_spec()] * len(places)
        + [stat_spec()] * len(before),
        [some_rows(rows, STRETCH, 2), some_rows(rows, LANES, 1), stat_spec()],
        [
            shape((2 * PAIRS, rows, STRETCH), BF16),
            shape((PAIRS, rows, LANES), BF16),
            shape((PAIRS, 8, STAT_LANES), F32),
        ],
        10**6,
    )


def terms(name, queries, final, blocks, calls):
    counts = tuple(count for _, count, _ in calls)
    rows = BLOCK * sum(counts)
    call_specs, call_inputs = [], []
    for outputs, count, place in calls:
        call_specs += [
            some_rows(BLOCK * count, STRETCH, 2, place),
            some_rows(BLOCK * count, LANES, 1, place),
            stat_spec(),
        ]
        call_inputs += list(outputs)
    return far_call(
        lambda *refs: terms_kernel(counts, *refs),
        name,
        (*queries, final, *blocks, *call_inputs),
        [stat_spec()] + [block_spec()] * len(blocks) + call_specs,
        [block_spec(rows), some_rows(rows, STRETCH, 2), some_rows(rows, LANES, 1)],
        [
            shape((rows, 2 * FEAT), BF16),
            shape((2 * PAIRS, rows, STRETCH), BF16),
            shape((PAIRS, rows, LANES), BF16),
        ],
        10**6,
    )


def diagonal_terms(queries, bias, blocks, before):
    rows = 2 * BLOCK
    return far_call(
        lambda *refs: diagonal_kernel((3, 7), len(before), *refs),
        "far_diagonal",
        (*queries, bias, *blocks, *before),
        [pl.BlockSpec((2 * HALF, LANES), lambda step: (0, 0))]
        + [block_spec()] * 2
        + [stat_spec()] * len(before),
        [block_spec()] * 2 + [some_rows(rows, STRETCH, 2), some_rows(rows, LANES, 1), stat_spec()],
        [shape((BLOCK, 2 * FEAT), BF16)] * 2
        + [
            shape((2 * PAIRS, rows, STRETCH), BF16),
            shape((PAIRS, rows, LANES), BF16),
            shape((PAIRS, 8, STAT_LANES), F32),
        ],
        10**6,
    )


def woven(key, value):
    parts = [rows.reshape(BEACONS, PAIRS, 1, PAIR) for rows in (key, value)]
    return jnp.concatenate(parts, axis=2).reshape(BEACONS, 2 * FEAT)


def unwoven(both):
    parts = both.reshape(BEACONS, PAIRS, 2, PAIR)
    return parts[:, :, 0].reshape(BEACONS, FEAT), parts[:, :, 1].reshape(BEACONS, FEAT)


def on_device(
    raw_q, raw_k, raw_v, raw_grad, beacon_q, beacon_k, beacon_v, beacon_grad, assign, prefix
):
    raw = (raw_q, raw_k, raw_v, raw_grad)
    rest = (beacon_k, beacon_v, beacon_grad)

    def raw_stats_of(place, count, token, stats):
        return raw_stats(place, count, (*raw, token, *rest), stats)

    def queries(token):
        return raw_q, raw_grad, token, beacon_grad

    own0 = lax.optimization_barrier(woven(beacon_k[0], beacon_v[0]))
    (got, bias) = beside(
        own0, assign, lambda value, token: (exchange(value, 0), far_bias(token, prefix))
    )
    own0 = joined(own0, got)
    stats = ()
    for step, place, count in ((1, 0, 1), (2, 1, 1), (3, 2, 2)):
        got, stats = beside(
            own0,
            (beacon_q, stats),
            lambda value, token, step=step, place=place, count=count: (
                exchange(value, step), raw_stats_of(place, count, *token)
            ),
        )
        own0 = joined(own0, got)

    def stage_one(value, token):
        got = exchange(value, 4), exchange(value, 5), swap(value)
        stats = raw_stats_of(4, 4, *token)
        late, token, stats = lax.optimization_barrier((got[2], token[0], stats))
        return got, stats, weigh((0, 4), queries(token), bias, (value, late), ())

    (own_u, own_v, other0), stats, first = beside(own0, (beacon_q, stats), stage_one)

    def stage_two(values, token):
        own_u, own_v = values
        got = exchange(own_v[:, :FEAT], 4), exchange(own_u[:, FEAT:], 5)
        others = swap(own_u), swap(own_v)
        blocks = (own_u, own_v, *others)
        return got, others, weigh((1, 2, 5, 6), queries(token), bias, blocks, first[2:])

    (got_low, got_high), (other_u, other_v), second = beside((own_u, own_v), beacon_q, stage_two)
    own_uv = joined(got_low, got_high, axis=1)
    other_uv = swap(own_uv)
    d_own, d_other, ds_uv, dsb_uv, final = diagonal_terms(
        queries(beacon_q), bias, (own_uv, other_uv), (second[2], *stats)
    )
    got, others = beside(
        d_other,
        beacon_q,
        lambda value, token: (
            swap(value),
            terms(
                "other_rest", queries(token), final, (other0, other_u, other_v),
                [(first, 1, 1), (second, 2, 1)],
            ),
        ),
    )
    diagonal = added(d_own, got)

    def back_two(values, token):
        value, rest = values
        got = exchange(value[:, :FEAT], 4), exchange(value[:, FEAT:], 5)
        return got, swap(rest), terms(
            "own_rest", queries(token), final, (own0, own_u, own_v),
            [(first, 1, 0), (second, 2, 0)],
        )

    (got_low, got_high), got, owns = beside((diagonal, others[0]), beacon_q, back_two)
    blocks = [slice(place * BLOCK, (place + 1) * BLOCK) for place in range(3)]
    sums = [(owns[0][rows], got[rows]) for rows in blocks]
    none = jnp.zeros((BLOCK, FEAT), BF16)
    total = added(*sums[0])
    total_u = added(*sums[1], jnp.concatenate([none, got_high], axis=1))
    total_v = added(*sums[2], jnp.concatenate([got_low, none], axis=1))
    known = (
        final, own_uv, other_uv, other0, other_u, other_v, own0, own_u, own_v,
        ds_uv, others[1], owns[1], dsb_uv, others[2], owns[2],
    )

    def raw_grads_of(place, count, token, outs):
        return raw_grads(place, count, (*raw, token, *rest, *known), outs)

    (got_u, got_v), outs = beside(
        (total_u, total_v),
        beacon_q,
        lambda values, token: (
            (exchange(values[0], 4), exchange(values[1], 5)), raw_grads_of(0, 3, token, ())
        ),
    )
    total = added(total, got_u, got_v)
    for step, place, count in ((3, 3, 2), (2, 5, 1), (1, 6, 1), (0, 7, 1)):
        half = total.shape[0] // 2
        got, outs = beside(
            total[half:],
            (beacon_q, outs),
            lambda value, token, step=step, place=place, count=count: (
                exchange(value, step), raw_grads_of(place, count, *token)
            ),
        )
        kept = total[:half]
        if step:
            total = added(kept, got)
    raw_dq, raw_dk, raw_dv, beacon_dq, own_dk, own_dv = outs
    total_k, total_v = unwoven(kept.astype(F32) + got.astype(F32))
    beacon_dk = (own_dk[:BEACONS] + total_k).astype(BF16)[None]
    beacon_dv = (own_dv[:BEACONS] + total_v).astype(BF16)[None]
    return (raw_dq, raw_dk, raw_dv, beacon_dq, beacon_dk, beacon_dv)


def solution(mesh):
    named = Mesh(mesh.devices.reshape(SIZES), NAMES)
    placed = P(NAMES, None, None)
    return jax.shard_map(
        on_device,
        mesh=named,
        in_specs=(placed,) * 8 + (P(), P()),
        out_specs=(placed,) * 6,
        check_vma=False,
    )
```

time: 147 us -> 105 us (0.71)
  waiting for transfers between devices: 47.8 us -> 11.2 us
  other arithmetic: 12.1 us -> 2.31 us
  Pallas kernels: 51 us -> 59.4 us
  starting transfers between devices: 30.2 us -> 28.3 us
    ppermute x16, waiting for transfers between devices: 45.5 us -> 9.28 us  [exchange(): return lax.ppermute(value, NAMES, sorted(pairs))]
    pallas_call x3 -> x15, Pallas kernels: 51 us -> 59.4 us  [the longest x9 34 us: pieces(): pl.pallas_call(kernel, grid=(count,), in_specs=in_specs + [pl.BlockSpec(m...]
    concatenate x11 -> x6, other arithmetic: 7.38 us -> 0.22 us  [the longest x5 0.13 us: joined(): return lax.optimization_barrier(jnp.concatenate([kept, got], axis=axis))]
    ppermute x16, starting transfers between devices: 29.5 us -> 26.8 us  [exchange(): return lax.ppermute(value, NAMES, sorted(pairs))]
    reduce_sum x2 -> x0, other arithmetic: 1.91 us -> none  [the longest x1 1.28 us: far_bias(): lowest = stretch - jnp.sum(jnp.where(numbers == stretch, prefix, 0))]
    unnamed x28 -> x22, local copies, waits for them, and re-layouts: 1.64 us -> 0.09 us
  transfers between devices with their start and end apart: 20 -> 22, of which waited for: 15 -> 11; matrix products, arithmetic and copies ran while one was open for 6% -> 1% of each run, Pallas kernels for 17% -> 52%
where the time goes in v2:
time: 105 us; the launch traced here: 104 us
  Pallas kernels  59.4 us (57%)
  starting transfers between devices  28.3 us (27%)
  waiting for transfers between devices  11.2 us (11%)
  other arithmetic  2.31 us (2%)
  local copies, waits for them, and re-layouts  1.99 us (2%)
    pallas_call x9, Pallas kernels, pieces(): pl.pallas_call(kernel, grid=(count,), in_specs=in_specs + [pl.BlockSpec(m...  34 us
    ppermute x16, starting transfers between devices, exchange(): return lax.ppermute(value, NAMES, sorted(pairs))  26.8 us
    pallas_call x5, Pallas kernels, far_call(): pl.pallas_call(kernel, grid=(PAIRS // STEP_PAIRS,), in_specs=shared + in_...  23.5 us
    ppermute x16, waiting for transfers between devices, exchange(): return lax.ppermute(value, NAMES, sorted(pairs))  9.28 us
  transfers between devices with their start and end apart: 22, of which 11 were waited for; matrix products, arithmetic and copies ran while one was open for 1% of the time, Pallas kernels for 52%

profile of v2, /device:TPU:0, one launch (start us, length us, event | category | flops | bytes accessed | tf_op | source)
XLA Modules:
  0.0 104.1 jit_solution(8024198304611755980)
XLA Ops:
  0.6 0.7 reshape_squeeze.16
  1.4 0.7 reshape_squeeze.17
  2.2 2.1 %collective-permute-start = (bf16[4,4096]{1,0:T(4,128)(2,1)S(1)}, bf16[4,4096]{1,0:T(4,128)(2,1)S(1)}, u32[]{:S(2)}, u32[]{:S(2)}) collective-permute-start(bf16[4,4096]{1,0:T(4,128)(2,1)S(1)} %reshape.27), channel_id=1, source_target_pairs={{0,16},{1,17},{2,18},{3,19},{4,20},{5,21},{6,22},{7,23},{8,72},{9,... | collective-permute-start | bytes 98312 | tf_op jit(solution)/shard_map/ppermute | solution.py:49
  4.3 0.6 add_bitcast_fusion.place_ref
  4.9 1.9 %far_mask.1.refs_4_ = f32[512,128]{1,0:T(8,128)} custom-call(s32[1,3]{1,0:T(1,128)} %add_bitcast_fusion.place_ref, s32[1,128]{1,0:T(1,128)} %bitcast.19, s32[1,128]{1,0:T(1,128)} %bitcast.20), custom_call_target="tpu_custom_call" | custom-call | tf_op jit(solution)/shard_map/far_mask/pallas_call | solution.py:103
  6.8 3.6 %collective-permute-start.1 = (bf16[8,4096]{1,0:T(8,128)(2,1)S(1)}, bf16[8,4096]{1,0:T(8,128)(2,1)S(1)}, u32[]{:S(2)}, u32[]{:S(2)}) collective-permute-start(bf16[8,4096]{1,0:T(8,128)(2,1)S(1)} %pad_maximum_fusion.4), channel_id=1, source_target_pairs={{0,48},{1,49},{2,50},{3,51},{4,52},{5,53},{6,54},{7,55},{8,73},{9,... | collective-permute-start | bytes 196616 | tf_op jit(solution)/shard_map/ppermute | solution.py:49
  10.5 2.6 %raw_stats_0.1.refs_0_ = f32[8,8,640]{2,1,0:T(8,128)} custom-call(bf16[1,512,2048]{2,1,0:T(8,128)(2,1)} %refs_0_.19, bf16[1,512,2048]{2,1,0:T(8,128)(2,1)} %refs_1_.19, bf16[1,512,2048]{2,1,0:T(8,128)(2,1)} %refs_2_.15, bf16[1,512,2048]{2,1,0:T(8,128)(2,1)} %refs_3_.19, bf16[1,4,2048]{2,1,0:T(4,128)(2,1)} %refs_4_.4, bf16[1,4,2048]{2,1,0:T(4,128)(2,1)} %refs_5_.9, ...), custom_call_target="tpu_custom_call" | custom-call | flops 1000000 | bytes 1024 | tf_op jit(solution)/shard_map/raw_stats_0/pallas_call | solution.py:496
  13.1 1.7 %collective-permute-start.2 = (bf16[16,4096]{1,0:T(8,128)(2,1)S(1)}, bf16[16,4096]{1,0:T(8,128)(2,1)S(1)}, u32[]{:S(2)}, u32[]{:S(2)}) collective-permute-start(bf16[16,4096]{1,0:T(8,128)(2,1)S(1)} %pad_maximum_fusion.3), channel_id=1, source_target_pairs={{0,2},{1,3},{2,0},{3,1},{4,6},{5,7},{6,4},{7,5},{8,24},{9,25},{10,... | collective-permute-start | bytes 393224 | tf_op jit(solution)/shard_map/ppermute | solution.py:49
  14.8 2.7 %raw_stats_1.1.refs_0_ = f32[8,8,640]{2,1,0:T(8,128)} custom-call(bf16[1,512,2048]{2,1,0:T(8,128)(2,1)} %refs_0_.19, bf16[1,512,2048]{2,1,0:T(8,128)(2,1)} %refs_1_.19, bf16[1,512,2048]{2,1,0:T(8,128)(2,1)} %refs_2_.15, bf16[1,512,2048]{2,1,0:T(8,128)(2,1)} %refs_3_.19, bf16[1,4,2048]{2,1,0:T(4,128)(2,1)} %refs_4_.4, ...), custom_call_target="tpu_custom_call", output_to_operand_aliasing={{}: (8, {})} | custom-call | flops 1000000 | bytes 1024 | tf_op jit(solution)/shard_map/raw_stats_1/pallas_call | solution.py:496
  17.5 0.7 collective-permute-done.2
  18.2 3.1 %collective-permute-start.3 = (bf16[32,4096]{1,0:T(8,128)(2,1)S(1)}, bf16[32,4096]{1,0:T(8,128)(2,1)S(1)}, u32[]{:S(2)}, u32[]{:S(2)}) collective-permute-start(bf16[32,4096]{1,0:T(8,128)(2,1)S(1)} %pad_maximum_fusion.2), channel_id=1, source_target_pairs={{0,6},{1,7},{2,4},{3,5},{4,2},{5,3},{6,0},{7,1},{8,56},{9,57},{10,... | collective-permute-start | bytes 786440 | tf_op jit(solution)/shard_map/ppermute | solution.py:49
  21.3 3.5 %raw_stats_2.1.refs_0_ = f32[8,8,640]{2,1,0:T(8,128)} custom-call(bf16[1,512,2048]{2,1,0:T(8,128)(2,1)} %refs_0_.19, bf16[1,512,2048]{2,1,0:T(8,128)(2,1)} %refs_1_.19, bf16[1,512,2048]{2,1,0:T(8,128)(2,1)} %refs_2_.15, bf16[1,512,2048]{2,1,0:T(8,128)(2,1)} %refs_3_.19, bf16[1,4,2048]{2,1,0:T(4,128)(2,1)} %refs_4_.4, ...), custom_call_target="tpu_custom_call", output_to_operand_aliasing={{}: (8, {})} | custom-call | flops 1000000 | bytes 1024 | tf_op jit(solution)/shard_map/raw_stats_2/pallas_call | solution.py:496
  24.8 1.1 %collective-permute-done.3 = bf16[32,4096]{1,0:T(8,128)(2,1)S(1)} collective-permute-done((bf16[32,4096]{1,0:T(8,128)(2,1)S(1)}, bf16[32,4096]{1,0:T(8,128)(2,1)S(1)}, u32[]{:S(2)}, u32[]{:S(2)}) %collective-permute-start.3) | collective-permute-done | bytes 262176 | tf_op jit(solution)/shard_map/ppermute | solution.py:49
  26.1 2.8 %collective-permute-start.5 = (bf16[64,4096]{1,0:T(8,128)(2,1)S(1)}, bf16[64,4096]{1,0:T(8,128)(2,1)S(1)}, u32[]{:S(2)}, u32[]{:S(2)}) collective-permute-start(bf16[64,4096]{1,0:T(8,128)(2,1)S(1)} %pad_maximum_fusion.refs_5_.refs_14_), channel_id=1, source_target_pairs={{0,65},{1,64},{2,67},{3,66},{4,69},{5,68},{6,71},{7,70},{8,14},{9,... | collective-permute-start | bytes 1572872 | tf_op jit(solution)/shard_map/ppermute | solution.py:49
  28.9 0.2 collective-permute-start.4
  29.1 5.7 %raw_stats_4.1.refs_8_ = f32[8,8,640]{2,1,0:T(8,128)} custom-call(bf16[1,512,2048]{2,1,0:T(8,128)(2,1)} %refs_0_.19, bf16[1,512,2048]{2,1,0:T(8,128)(2,1)} %refs_1_.19, bf16[1,512,2048]{2,1,0:T(8,128)(2,1)} %refs_2_.15, bf16[1,512,2048]{2,1,0:T(8,128)(2,1)} %refs_3_.19, bf16[1,4,2048]{2,1,0:T(4,128)(2,1)} %refs_4_.4, ...), custom_call_target="tpu_custom_call", output_to_operand_aliasing={{}: (8, {})} | custom-call | flops 1000000 | bytes 1024 | tf_op jit(solution)/shard_map/raw_stats_4/pallas_call | solution.py:496
  34.8 3.1 %far_weights_0_4.1 = (bf16[16,128,512]{2,1,0:T(8,128)(2,1)S(1)}, bf16[8,128,128]{2,1,0:T(8,128)(2,1)S(1)}, f32[8,8,640]{2,1,0:T(8,128)S(1)}) custom-call(bf16[1,512,2048]{2,1,0:T(8,128)(2,1)S(1)} %copy-done, bf16[1,512,2048]{2,1,0:T(8,128)(2,1)S(1)} %copy-done.1, bf16[1,4,2048]{2,1,0:T(4,128)(2,1)S(1)} %copy-done.6, bf16[1,4,2048]{2,1,0:T(4,128)(2,1)S(1)} %copy-done.7, ...), custom_call_target="tpu_custom_call" | custom-call | flops 1000000 | bytes 1024 | tf_op jit(solution)/shard_map/far_weights_0_4/pallas_call | solution.py:554
  38.2 0.4 collective-permute-start.9
  38.7 2.6 %collective-permute-start.8 = (bf16[64,2048]{1,0:T(8,128)(2,1)S(1)}, bf16[64,2048]{1,0:T(8,128)(2,1)S(1)}, u32[]{:S(2)}, u32[]{:S(2)}) collective-permute-start(bf16[64,2048]{1,0:T(8,128)(2,1)S(1)} %slice.67), channel_id=1, source_target_pairs={{0,65},{1,64},{2,67},{3,66},{4,69},{5,68},{6,71},{7,70},{8,14},{9,... | collective-permute-start | bytes 786440 | tf_op jit(solution)/shard_map/ppermute | solution.py:49
  41.2 0.2 collective-permute-start.7
  41.4 5.1 %far_weights_1_2_5_6.1 = (bf16[16,256,512]{2,1,0:T(8,128)(2,1)S(1)}, bf16[8,256,128]{2,1,0:T(8,128)(2,1)S(1)}, f32[8,8,640]{2,1,0:T(8,128)S(1)}) custom-call(bf16[1,512,2048]{2,1,0:T(8,128)(2,1)S(1)} %copy-done, bf16[1,512,2048]{2,1,0:T(8,128)(2,1)S(1)} %copy-done.1, bf16[1,4,2048]{2,1,0:T(4,128)(2,1)S(1)} %copy-done.6, bf16[1,4,2048]{2,1,0:T(4,128)(2,1)S(1)} %copy-done.7, ...), custom_call_target="tpu_custom_call" | custom-call | flops 1000000 | bytes 1024 | tf_op jit(solution)/shard_map/far_weights_1_2_5_6/pallas_call | solution.py:554
  46.6 1.0 collective-permute-done.7
  47.7 1.9 %collective-permute-done.11.refs_6_.refs_10_ = bf16[64,4096]{1,0:T(8,128)(2,1)S(1)} collective-permute-done((bf16[64,4096]{1,0:T(8,128)(2,1)S(1)}, bf16[64,4096]{1,0:T(8,128)(2,1)S(1)}, u32[]{:S(2)}, u32[]{:S(2)}) %collective-permute-start.11) | collective-permute-done | bytes 524320 | tf_op jit(solution)/shard_map/ppermute | solution.py:53
  49.6 5.6 %far_diagonal.1 = (bf16[64,4096]{1,0:T(8,128)(2,1)S(1)}, bf16[64,4096]{1,0:T(8,128)(2,1)S(1)}, bf16[16,128,512]{2,1,0:T(8,128)(2,1)S(1)}, bf16[8,128,128]{2,1,0:T(8,128)(2,1)S(1)}, f32[8,8,640]{2,1,0:T(8,128)S(1)}) custom-call(bf16[1,512,2048]{2,1,0:T(8,128)(2,1)S(1)} %copy-done, bf16[1,512,2048]{2,1,0:T(8,128)(2,1)S(1)} %copy-done.1, ...), custom_call_target="tpu_custom_call" | custom-call | flops 1000000 | bytes 1024 | tf_op jit(solution)/shard_map/far_diagonal/pallas_call | solution.py:554
  55.3 0.4 collective-permute-start.12
  55.7 4.8 %other_rest.1 = (bf16[192,4096]{1,0:T(8,128)(2,1)S(1)}, bf16[16,192,512]{2,1,0:T(8,128)(2,1)S(1)}, bf16[8,192,128]{2,1,0:T(8,128)(2,1)S(1)}) custom-call(bf16[1,512,2048]{2,1,0:T(8,128)(2,1)S(1)} %copy-done, bf16[1,512,2048]{2,1,0:T(8,128)(2,1)S(1)} %copy-done.1, bf16[1,4,2048]{2,1,0:T(4,128)(2,1)S(1)} %copy-done.6, bf16[1,4,2048]{2,1,0:T(4,128)(2,1)S(1)} %copy-done.7, ...), custom_call_target="tpu_custom_call" | custom-call | flops 1000000 | bytes 1024 | tf_op jit(solution)/shard_map/other_rest/pallas_call | solution.py:554
  60.7 0.5 collective-permute-start.15
  61.2 1.3 %collective-permute-start.14 = (bf16[64,2048]{1,0:T(8,128)(2,1)S(1)}, bf16[64,2048]{1,0:T(8,128)(2,1)S(1)}, u32[]{:S(2)}, u32[]{:S(2)}) collective-permute-start(bf16[64,2048]{1,0:T(8,128)(2,1)S(1)} %get-tuple-element.358), channel_id=1, source_target_pairs={{0,65},{1,64},{2,67},{3,66},{4,69},{5,68},{6,71},{7,70},{8,14},{9,... | collective-permute-start | bytes 786440 | tf_op jit(solution)/shard_map/ppermute | solution.py:49
  62.5 4.8 %own_rest.1 = (bf16[192,4096]{1,0:T(8,128)(2,1)S(1)}, bf16[16,192,512]{2,1,0:T(8,128)(2,1)S(1)}, bf16[8,192,128]{2,1,0:T(8,128)(2,1)S(1)}) custom-call(bf16[1,512,2048]{2,1,0:T(8,128)(2,1)S(1)} %copy-done, bf16[1,512,2048]{2,1,0:T(8,128)(2,1)S(1)} %copy-done.1, bf16[1,4,2048]{2,1,0:T(4,128)(2,1)S(1)} %copy-done.6, bf16[1,4,2048]{2,1,0:T(4,128)(2,1)S(1)} %copy-done.7, ...), custom_call_target="tpu_custom_call" | custom-call | flops 1000000 | bytes 1024 | tf_op jit(solution)/shard_map/own_rest/pallas_call | solution.py:554
  67.4 1.4 %collective-permute-done.14 = bf16[64,2048]{1,0:T(8,128)(2,1)S(1)} collective-permute-done((bf16[64,2048]{1,0:T(8,128)(2,1)S(1)}, bf16[64,2048]{1,0:T(8,128)(2,1)S(1)}, u32[]{:S(2)}, u32[]{:S(2)}) %collective-permute-start.14) | collective-permute-done | bytes 262176 | tf_op jit(solution)/shard_map/ppermute | solution.py:49
  68.8 0.4 add_convert_fusion.1
  69.2 0.6 collective-permute-start.16
  69.8 2.0 %collective-permute-start.17 = (bf16[64,4096]{1,0:T(8,128)(2,1)S(1)}, bf16[64,4096]{1,0:T(8,128)(2,1)S(1)}, u32[]{:S(2)}, u32[]{:S(2)}) collective-permute-start(bf16[64,4096]{1,0:T(8,128)(2,1)S(1)} %get-tuple-element.248), channel_id=1, source_target_pairs={{0,65},{1,64},{2,67},{3,66},{4,69},{5,68},{6,71},{7,70},{8,14},{9,... | collective-permute-start | bytes 1572872 | tf_op jit(solution)/shard_map/ppermute | solution.py:49
  71.9 7.0 %raw_grads_0.1 = (bf16[1,512,2048]{2,1,0:T(8,128)(2,1)}, bf16[1,512,2048]{2,1,0:T(8,128)(2,1)}, bf16[1,512,2048]{2,1,0:T(8,128)(2,1)}, bf16[1,4,2048]{2,1,0:T(4,...) custom-call(bf16[1,512,2048]{2,1,0:T(8,128)(2,1)S(1)} %copy-done, bf16[1,512,2048]{2,1,0:T(8,128)(2,1)S(1)} %copy-done.2, ...), custom_call_target="tpu_custom_call" | custom-call | flops 1000000 | bytes 1024 | tf_op jit(solution)/shard_map/raw_grads_0/pallas_call | solution.py:496
  78.9 1.3 %collective-permute-done.17 = bf16[64,4096]{1,0:T(8,128)(2,1)S(1)} collective-permute-done((bf16[64,4096]{1,0:T(8,128)(2,1)S(1)}, bf16[64,4096]{1,0:T(8,128)(2,1)S(1)}, u32[]{:S(2)}, u32[]{:S(2)}) %collective-permute-start.17) | collective-permute-done | bytes 524320 | tf_op jit(solution)/shard_map/ppermute | solution.py:49
  80.2 0.3 add_convert_fusion
  80.5 2.6 %collective-permute-start.18 = (bf16[32,4096]{1,0:T(8,128)(2,1)S(1)}, bf16[32,4096]{1,0:T(8,128)(2,1)S(1)}, u32[]{:S(2)}, u32[]{:S(2)}) collective-permute-start(bf16[32,4096]{1,0:T(8,128)(2,1)S(1)} %slice.89), channel_id=1, source_target_pairs={{0,6},{1,7},{2,4},{3,5},{4,2},{5,3},{6,0},{7,1},{8,56},{9,57},{10,... | collective-permute-start | bytes 786440 | tf_op jit(solution)/shard_map/ppermute | solution.py:49
  83.2 4.8 %raw_grads_3.1 = (bf16[1,512,2048]{2,1,0:T(8,128)(2,1)}, bf16[1,512,2048]{2,1,0:T(8,128)(2,1)}, bf16[1,512,2048]{2,1,0:T(8,128)(2,1)}, bf16[1,4,2048]{2,1,0:T(4,...) custom-call(bf16[1,512,2048]{2,1,0:T(8,128)(2,1)S(1)} %copy-done, ...), custom_call_target="tpu_custom_call", output_to_operand_aliasing={{0}: (23, {}), {1}: (24, {}), {2}: (25, {}), {3}: (26, {}),... | custom-call | flops 1000000 | bytes 1024 | tf_op jit(solution)/shard_map/raw_grads_3/pallas_call | solution.py:496
  88.0 0.2 collective-permute-done.18
  88.3 0.6 collective-permute-start.19
  88.9 2.5 %raw_grads_5.1 = (bf16[1,512,2048]{2,1,0:T(8,128)(2,1)}, bf16[1,512,2048]{2,1,0:T(8,128)(2,1)}, bf16[1,512,2048]{2,1,0:T(8,128)(2,1)}, bf16[1,4,2048]{2,1,0:T(4,...) custom-call(bf16[1,512,2048]{2,1,0:T(8,128)(2,1)S(1)} %copy-done, ...), custom_call_target="tpu_custom_call", output_to_operand_aliasing={{0}: (23, {}), {1}: (24, {}), {2}: (25, {}), {3}: (26, {}),... | custom-call | flops 1000000 | bytes 1024 | tf_op jit(solution)/shard_map/raw_grads_5/pallas_call | solution.py:496
  91.4 1.9 %collective-permute-done.19 = bf16[16,4096]{1,0:T(8,128)(2,1)S(1)} collective-permute-done((bf16[16,4096]{1,0:T(8,128)(2,1)S(1)}, bf16[16,4096]{1,0:T(8,128)(2,1)S(1)}, u32[]{:S(2)}, u32[]{:S(2)}) %collective-permute-start.19) | collective-permute-done | bytes 131104 | tf_op jit(solution)/shard_map/ppermute | solution.py:49
  93.4 3.1 %collective-permute-start.20 = (bf16[8,4096]{1,0:T(8,128)(2,1)S(1)}, bf16[8,4096]{1,0:T(8,128)(2,1)S(1)}, u32[]{:S(2)}, u32[]{:S(2)}) collective-permute-start(bf16[8,4096]{1,0:T(8,128)(2,1)S(1)} %slice.93), channel_id=1, source_target_pairs={{0,48},{1,49},{2,50},{3,51},{4,52},{5,53},{6,54},{7,55},{8,73},{9,... | collective-permute-start | bytes 196616 | tf_op jit(solution)/shard_map/ppermute | solution.py:49
  96.5 2.5 %raw_grads_6.1 = (bf16[1,512,2048]{2,1,0:T(8,128)(2,1)}, bf16[1,512,2048]{2,1,0:T(8,128)(2,1)}, bf16[1,512,2048]{2,1,0:T(8,128)(2,1)}, bf16[1,4,2048]{2,1,0:T(4,...) custom-call(bf16[1,512,2048]{2,1,0:T(8,128)(2,1)S(1)} %copy-done, ...), custom_call_target="tpu_custom_call", output_to_operand_aliasing={{0}: (23, {}), {1}: (24, {}), {2}: (25, {}), {3}: (26, {}),... | custom-call | flops 1000000 | bytes 1024 | tf_op jit(solution)/shard_map/raw_grads_6/pallas_call | solution.py:496
  99.3 2.6 %raw_grads_7.1 = (bf16[1,512,2048]{2,1,0:T(8,128)(2,1)}, bf16[1,512,2048]{2,1,0:T(8,128)(2,1)}, bf16[1,512,2048]{2,1,0:T(8,128)(2,1)}, bf16[1,4,2048]{2,1,0:T(4,...) custom-call(bf16[1,512,2048]{2,1,0:T(8,128)(2,1)S(1)} %copy-done, ...), custom_call_target="tpu_custom_call", output_to_operand_aliasing={{0}: (23, {}), {1}: (24, {}), {2}: (25, {}), {3}: (26, {}),... | custom-call | flops 1000000 | bytes 1024 | tf_op jit(solution)/shard_map/raw_grads_7/pallas_call | solution.py:496
  101.9 1.3 %collective-permute-done.21 = bf16[4,4096]{1,0:T(4,128)(2,1)S(1)} collective-permute-done((bf16[4,4096]{1,0:T(4,128)(2,1)S(1)}, bf16[4,4096]{1,0:T(4,128)(2,1)S(1)}, u32[]{:S(2)}, u32[]{:S(2)}) %collective-permute-start.21) | collective-permute-done | bytes 32800 | tf_op jit(solution)/shard_map/ppermute | solution.py:49
  103.3 0.2 slice_reduce_fusion
  103.5 0.6 fusion
  (60 shorter events, 1.6 us)
Async XLA Ops:
  2.2 4.6 %collective-permute-start = (bf16[4,4096]{1,0:T(4,128)(2,1)S(1)}, bf16[4,4096]{1,0:T(4,128)(2,1)S(1)}, u32[]{:S(2)}, u32[]{:S(2)}) collective-permute-start(bf16[4,4096]{1,0:T(4,128)(2,1)S(1)} %reshape.27), channel_id=1, source_target_pairs={{0,16},{1,17},{2,18},{3,19},{4,20},{5,21},{6,22},{7,23},{8,72},{9,... | collective-permute-start | bytes 98312 | tf_op jit(solution)/shard_map/ppermute | solution.py:49
  6.8 6.3 %collective-permute-start.1 = (bf16[8,4096]{1,0:T(8,128)(2,1)S(1)}, bf16[8,4096]{1,0:T(8,128)(2,1)S(1)}, u32[]{:S(2)}, u32[]{:S(2)}) collective-permute-start(bf16[8,4096]{1,0:T(8,128)(2,1)S(1)} %pad_maximum_fusion.4), channel_id=1, source_target_pairs={{0,48},{1,49},{2,50},{3,51},{4,52},{5,53},{6,54},{7,55},{8,73},{9,... | collective-permute-start | bytes 196616 | tf_op jit(solution)/shard_map/ppermute | solution.py:49
  13.1 5.0 %collective-permute-start.2 = (bf16[16,4096]{1,0:T(8,128)(2,1)S(1)}, bf16[16,4096]{1,0:T(8,128)(2,1)S(1)}, u32[]{:S(2)}, u32[]{:S(2)}) collective-permute-start(bf16[16,4096]{1,0:T(8,128)(2,1)S(1)} %pad_maximum_fusion.3), channel_id=1, source_target_pairs={{0,2},{1,3},{2,0},{3,1},{4,6},{5,7},{6,4},{7,5},{8,24},{9,25},{10,... | collective-permute-start | bytes 393224 | tf_op jit(solution)/shard_map/ppermute | solution.py:49
  18.2 7.7 %collective-permute-start.3 = (bf16[32,4096]{1,0:T(8,128)(2,1)S(1)}, bf16[32,4096]{1,0:T(8,128)(2,1)S(1)}, u32[]{:S(2)}, u32[]{:S(2)}) collective-permute-start(bf16[32,4096]{1,0:T(8,128)(2,1)S(1)} %pad_maximum_fusion.2), channel_id=1, source_target_pairs={{0,6},{1,7},{2,4},{3,5},{4,2},{5,3},{6,0},{7,1},{8,56},{9,57},{10,... | collective-permute-start | bytes 786440 | tf_op jit(solution)/shard_map/ppermute | solution.py:49
  25.9 8.9 %copy-start = (bf16[1,512,2048]{2,1,0:T(8,128)(2,1)S(1)}, bf16[1,512,2048]{2,1,0:T(8,128)(2,1)}, u32[]{:S(2)}) copy-start(bf16[1,512,2048]{2,1,0:T(8,128)(2,1)} %refs_0_.19) | copy-start | bytes 6291460
  25.9 8.9 %copy-start.1 = (bf16[1,512,2048]{2,1,0:T(8,128)(2,1)S(1)}, bf16[1,512,2048]{2,1,0:T(8,128)(2,1)}, u32[]{:S(2)}) copy-start(bf16[1,512,2048]{2,1,0:T(8,128)(2,1)} %refs_3_.19) | copy-start | bytes 6291460
  25.9 8.9 %copy-start.4 = (f32[512,128]{1,0:T(8,128)S(1)}, f32[512,128]{1,0:T(8,128)}, u32[]{:S(2)}) copy-start(f32[512,128]{1,0:T(8,128)} %far_mask.1.refs_4_) | copy-start | bytes 786436
  26.0 8.9 %copy-start.6 = (bf16[1,4,2048]{2,1,0:T(4,128)(2,1)S(1)}, bf16[1,4,2048]{2,1,0:T(4,128)(2,1)}, u32[]{:S(2)}) copy-start(bf16[1,4,2048]{2,1,0:T(4,128)(2,1)} %refs_4_.4) | copy-start | bytes 49156
  26.0 8.9 %copy-start.7 = (bf16[1,4,2048]{2,1,0:T(4,128)(2,1)S(1)}, bf16[1,4,2048]{2,1,0:T(4,128)(2,1)}, u32[]{:S(2)}) copy-start(bf16[1,4,2048]{2,1,0:T(4,128)(2,1)} %refs_7_.9) | copy-start | bytes 49156
  26.0 8.8 %collective-permute-start.6 = (bf16[64,4096]{1,0:T(8,128)(2,1)S(1)}, bf16[64,4096]{1,0:T(8,128)(2,1)S(1)}, u32[]{:S(2)}, u32[]{:S(2)}) collective-permute-start(bf16[64,4096]{1,0:T(8,128)(2,1)S(1)} %pad_maximum_fusion.refs_5_.refs_14_), channel_id=1, source_target_pairs={{0,8},{8,0},{1,9},{9,1},{2,10},{10,2},{3,11},{11,3},{4,12},{12,4},... | collective-permute-start | bytes 1572872 | tf_op jit(solution)/shard_map/ppermute | solution.py:53
  26.1 11.9 %collective-permute-start.5 = (bf16[64,4096]{1,0:T(8,128)(2,1)S(1)}, bf16[64,4096]{1,0:T(8,128)(2,1)S(1)}, u32[]{:S(2)}, u32[]{:S(2)}) collective-permute-start(bf16[64,4096]{1,0:T(8,128)(2,1)S(1)} %pad_maximum_fusion.refs_5_.refs_14_), channel_id=1, source_target_pairs={{0,65},{1,64},{2,67},{3,66},{4,69},{5,68},{6,71},{7,70},{8,14},{9,... | collective-permute-start | bytes 1572872 | tf_op jit(solution)/shard_map/ppermute | solution.py:49
  28.9 9.2 %collective-permute-start.4 = (bf16[64,4096]{1,0:T(8,128)(2,1)S(1)}, bf16[64,4096]{1,0:T(8,128)(2,1)S(1)}, u32[]{:S(2)}, u32[]{:S(2)}) collective-permute-start(bf16[64,4096]{1,0:T(8,128)(2,1)S(1)} %pad_maximum_fusion.refs_5_.refs_14_), channel_id=1, source_target_pairs={{0,64},{1,65},{2,66},{3,67},{4,68},{5,69},{6,70},{7,71},{8,10},{9,... | collective-permute-start | bytes 1572872 | tf_op jit(solution)/shard_map/ppermute | solution.py:49
  38.1 3.3 %collective-permute-start.10 = (bf16[64,4096]{1,0:T(8,128)(2,1)S(1)}, bf16[64,4096]{1,0:T(8,128)(2,1)S(1)}, u32[]{:S(2)}, u32[]{:S(2)}) collective-permute-start(bf16[64,4096]{1,0:T(8,128)(2,1)S(1)} %collective-permute-done.5.refs_6_.refs_7_.refs_16_), channel_id=1, source_target_pairs={{0,8},{8,0},{1,9},{9,1},{2,10},{10,2},{3,11},{11,3},{4,12},{12,4},... | collective-permute-start | bytes 1572872 | tf_op jit(solution)/shard_map/ppermute | solution.py:53
  38.2 3.2 %collective-permute-start.9 = (bf16[64,4096]{1,0:T(8,128)(2,1)S(1)}, bf16[64,4096]{1,0:T(8,128)(2,1)S(1)}, u32[]{:S(2)}, u32[]{:S(2)}) collective-permute-start(bf16[64,4096]{1,0:T(8,128)(2,1)S(1)} %collective-permute-done.4.refs_5_.refs_6_.refs_15_), channel_id=1, source_target_pairs={{0,8},{8,0},{1,9},{9,1},{2,10},{10,2},{3,11},{11,3},{4,12},{12,4},... | collective-permute-start | bytes 1572872 | tf_op jit(solution)/shard_map/ppermute | solution.py:53
  38.7 11.0 %copy-start.5 = (f32[8,8,640]{2,1,0:T(8,128)S(1)}, f32[8,8,640]{2,1,0:T(8,128)}, u32[]{:S(2)}) copy-start(f32[8,8,640]{2,1,0:T(8,128)} %raw_stats_4.1.refs_8_) | copy-start | bytes 491524
  38.7 7.9 %collective-permute-start.8 = (bf16[64,2048]{1,0:T(8,128)(2,1)S(1)}, bf16[64,2048]{1,0:T(8,128)(2,1)S(1)}, u32[]{:S(2)}, u32[]{:S(2)}) collective-permute-start(bf16[64,2048]{1,0:T(8,128)(2,1)S(1)} %slice.67), channel_id=1, source_target_pairs={{0,65},{1,64},{2,67},{3,66},{4,69},{5,68},{6,71},{7,70},{8,14},{9,... | collective-permute-start | bytes 786440 | tf_op jit(solution)/shard_map/ppermute | solution.py:49
  41.2 6.4 %collective-permute-start.7 = (bf16[64,2048]{1,0:T(8,128)(2,1)S(1)}, bf16[64,2048]{1,0:T(8,128)(2,1)S(1)}, u32[]{:S(2)}, u32[]{:S(2)}) collective-permute-start(bf16[64,2048]{1,0:T(8,128)(2,1)S(1)} %slice.66), channel_id=1, source_target_pairs={{0,64},{1,65},{2,66},{3,67},{4,68},{5,69},{6,70},{7,71},{8,10},{9,... | collective-permute-start | bytes 786440 | tf_op jit(solution)/shard_map/ppermute | solution.py:49
  47.6 2.0 %collective-permute-start.11 = (bf16[64,4096]{1,0:T(8,128)(2,1)S(1)}, bf16[64,4096]{1,0:T(8,128)(2,1)S(1)}, u32[]{:S(2)}, u32[]{:S(2)}) collective-permute-start(bf16[64,4096]{1,0:T(8,128)(2,1)S(1)} %pad_maximum_fusion.1.refs_5_.refs_9_), channel_id=1, source_target_pairs={{0,8},{8,0},{1,9},{9,1},{2,10},{10,2},{3,11},{11,3},{4,12},{12,4},... | collective-permute-start | bytes 1572872 | tf_op jit(solution)/shard_map/ppermute | solution.py:53
  55.3 5.2 %collective-permute-start.12 = (bf16[64,4096]{1,0:T(8,128)(2,1)S(1)}, bf16[64,4096]{1,0:T(8,128)(2,1)S(1)}, u32[]{:S(2)}, u32[]{:S(2)}) collective-permute-start(bf16[64,4096]{1,0:T(8,128)(2,1)S(1)} %get-tuple-element.222), channel_id=1, source_target_pairs={{0,8},{8,0},{1,9},{9,1},{2,10},{10,2},{3,11},{11,3},{4,12},{12,4},... | collective-permute-start | bytes 1572872 | tf_op jit(solution)/shard_map/ppermute | solution.py:53
  60.7 8.2 %collective-permute-start.15 = (bf16[192,4096]{1,0:T(8,128)(2,1)S(1)}, bf16[192,4096]{1,0:T(8,128)(2,1)S(1)}, u32[]{:S(2)}, u32[]{:S(2)}) collective-permute-start(bf16[192,4096]{1,0:T(8,128)(2,1)S(1)} %get-tuple-element.238), channel_id=1, source_target_pairs={{0,8},{8,0},{1,9},{9,1},{2,10},{10,2},{3,11},{11,3},{4,12},{12,4},... | collective-permute-start | bytes 4718600 | tf_op jit(solution)/shard_map/ppermute | solution.py:53
  61.2 7.7 %collective-permute-start.14 = (bf16[64,2048]{1,0:T(8,128)(2,1)S(1)}, bf16[64,2048]{1,0:T(8,128)(2,1)S(1)}, u32[]{:S(2)}, u32[]{:S(2)}) collective-permute-start(bf16[64,2048]{1,0:T(8,128)(2,1)S(1)} %get-tuple-element.358), channel_id=1, source_target_pairs={{0,65},{1,64},{2,67},{3,66},{4,69},{5,68},{6,71},{7,70},{8,14},{9,... | collective-permute-start | bytes 786440 | tf_op jit(solution)/shard_map/ppermute | solution.py:49
  62.5 6.4 %collective-permute-start.13 = (bf16[64,2048]{1,0:T(8,128)(2,1)S(1)}, bf16[64,2048]{1,0:T(8,128)(2,1)S(1)}, u32[]{:S(2)}, u32[]{:S(2)}) collective-permute-start(bf16[64,2048]{1,0:T(8,128)(2,1)S(1)} %get-tuple-element.359), channel_id=1, source_target_pairs={{0,64},{1,65},{2,66},{3,67},{4,68},{5,69},{6,70},{7,71},{8,10},{9,... | collective-permute-start | bytes 786440 | tf_op jit(solution)/shard_map/ppermute | solution.py:49
  62.5 9.3 %copy-start.3 = (bf16[1,512,2048]{2,1,0:T(8,128)(2,1)S(1)}, bf16[1,512,2048]{2,1,0:T(8,128)(2,1)}, u32[]{:S(2)}) copy-start(bf16[1,512,2048]{2,1,0:T(8,128)(2,1)} %refs_2_.15) | copy-start | bytes 6291460
  67.4 4.5 %copy-start.2 = (bf16[1,512,2048]{2,1,0:T(8,128)(2,1)S(1)}, bf16[1,512,2048]{2,1,0:T(8,128)(2,1)}, u32[]{:S(2)}) copy-start(bf16[1,512,2048]{2,1,0:T(8,128)(2,1)} %refs_1_.19) | copy-start | bytes 6291460
  67.4 4.5 %copy-start.8 = (bf16[1,4,2048]{2,1,0:T(4,128)(2,1)S(1)}, bf16[1,4,2048]{2,1,0:T(4,128)(2,1)}, u32[]{:S(2)}) copy-start(bf16[1,4,2048]{2,1,0:T(4,128)(2,1)} %refs_5_.9) | copy-start | bytes 49156
  67.4 4.5 %copy-start.9 = (bf16[1,4,2048]{2,1,0:T(4,128)(2,1)S(1)}, bf16[1,4,2048]{2,1,0:T(4,128)(2,1)}, u32[]{:S(2)}) copy-start(bf16[1,4,2048]{2,1,0:T(4,128)(2,1)} %refs_6_.9) | copy-start | bytes 49156
  69.2 9.7 %collective-permute-start.16 = (bf16[64,4096]{1,0:T(8,128)(2,1)S(1)}, bf16[64,4096]{1,0:T(8,128)(2,1)S(1)}, u32[]{:S(2)}, u32[]{:S(2)}) collective-permute-start(bf16[64,4096]{1,0:T(8,128)(2,1)S(1)} %get-tuple-element.247), channel_id=1, source_target_pairs={{0,64},{1,65},{2,66},{3,67},{4,68},{5,69},{6,70},{7,71},{8,10},{9,... | collective-permute-start | bytes 1572872 | tf_op jit(solution)/shard_map/ppermute | solution.py:49
  69.8 10.4 %collective-permute-start.17 = (bf16[64,4096]{1,0:T(8,128)(2,1)S(1)}, bf16[64,4096]{1,0:T(8,128)(2,1)S(1)}, u32[]{:S(2)}, u32[]{:S(2)}) collective-permute-start(bf16[64,4096]{1,0:T(8,128)(2,1)S(1)} %get-tuple-element.248), channel_id=1, source_target_pairs={{0,65},{1,64},{2,67},{3,66},{4,69},{5,68},{6,71},{7,70},{8,14},{9,... | collective-permute-start | bytes 1572872 | tf_op jit(solution)/shard_map/ppermute | solution.py:49
  80.5 7.7 %collective-permute-start.18 = (bf16[32,4096]{1,0:T(8,128)(2,1)S(1)}, bf16[32,4096]{1,0:T(8,128)(2,1)S(1)}, u32[]{:S(2)}, u32[]{:S(2)}) collective-permute-start(bf16[32,4096]{1,0:T(8,128)(2,1)S(1)} %slice.89), channel_id=1, source_target_pairs={{0,6},{1,7},{2,4},{3,5},{4,2},{5,3},{6,0},{7,1},{8,56},{9,57},{10,... | collective-permute-start | bytes 786440 | tf_op jit(solution)/shard_map/ppermute | solution.py:49
  88.3 5.0 %collective-permute-start.19 = (bf16[16,4096]{1,0:T(8,128)(2,1)S(1)}, bf16[16,4096]{1,0:T(8,128)(2,1)S(1)}, u32[]{:S(2)}, u32[]{:S(2)}) collective-permute-start(bf16[16,4096]{1,0:T(8,128)(2,1)S(1)} %slice.91), channel_id=1, source_target_pairs={{0,2},{1,3},{2,0},{3,1},{4,6},{5,7},{6,4},{7,5},{8,24},{9,25},{10,... | collective-permute-start | bytes 393224 | tf_op jit(solution)/shard_map/ppermute | solution.py:49
  93.4 5.8 %collective-permute-start.20 = (bf16[8,4096]{1,0:T(8,128)(2,1)S(1)}, bf16[8,4096]{1,0:T(8,128)(2,1)S(1)}, u32[]{:S(2)}, u32[]{:S(2)}) collective-permute-start(bf16[8,4096]{1,0:T(8,128)(2,1)S(1)} %slice.93), channel_id=1, source_target_pairs={{0,48},{1,49},{2,50},{3,51},{4,52},{5,53},{6,54},{7,55},{8,73},{9,... | collective-permute-start | bytes 196616 | tf_op jit(solution)/shard_map/ppermute | solution.py:49
  99.2 4.0 %collective-permute-start.21 = (bf16[4,4096]{1,0:T(4,128)(2,1)S(1)}, bf16[4,4096]{1,0:T(4,128)(2,1)S(1)}, u32[]{:S(2)}, u32[]{:S(2)}) collective-permute-start(bf16[4,4096]{1,0:T(4,128)(2,1)S(1)} %slice.94), channel_id=1, source_target_pairs={{0,16},{1,17},{2,18},{3,19},{4,20},{5,21},{6,22},{7,23},{8,72},{9,... | collective-permute-start | bytes 98312 | tf_op jit(solution)/shard_map/ppermute | solution.py:49

commit v3 on v2

--- a/solution.py
+++ b/solution.py
@@ -69,8 +69,10 @@
     return total.astype(BF16)
 
 
-def mask_kernel(place_ref, assign_ref, prefix_ref, bias_ref):
-    mine, core, own = place_ref[0, 0], place_ref[0, 1], place_ref[0, 2]
+def mask_kernel(assign_ref, prefix_ref, bias_ref):
+    x_lo, z, core, y, x_hi = (lax.axis_index(name) for name in NAMES)
+    mine = gray(x_hi * 2 + x_lo) | (gray(y) << 2) | (gray(z) << 4)
+    own = slot_of(mine, core)
     numbers = lax.broadcasted_iota(jnp.int32, (1, LANES), 1)
     assign, prefix = assign_ref[...], prefix_ref[...]
 
@@ -96,17 +98,14 @@
 
 
 def far_bias(assign, prefix):
-    x_lo, z, core, y, x_hi = (lax.axis_index(name) for name in NAMES)
-    mine = gray(x_hi * 2 + x_lo) | (gray(y) << 2) | (gray(z) << 4)
-    place = jnp.stack([mine, core, slot_of(mine, core)]).astype(jnp.int32).reshape(1, 3)
     line = pl.BlockSpec((1, LANES), lambda: (0, 0))
     return pl.pallas_call(
         mask_kernel,
-        in_specs=[pl.BlockSpec(memory_space=pltpu.SMEM), line, line],
+        in_specs=[line, line],
         out_specs=pl.BlockSpec((2 * HALF, LANES), lambda: (0, 0)),
         out_shape=jax.ShapeDtypeStruct((2 * HALF, LANES), F32),
         name="far_mask",
-    )(place, assign.reshape(1, LANES), prefix.reshape(1, LANES))
+    )(assign.reshape(1, LANES), prefix.reshape(1, LANES))
 
 
 def spread(rows):
@@ -288,7 +287,7 @@
 def weigh_kernel(places, priors, *refs):
     q_ref, g_ref, bq_ref, bg_ref, bias_ref = refs[:5]
     blocks, before = refs[5 : 5 + len(places)], refs[5 + len(places) : 5 + len(places) + priors]
-    w_ref, wb_ref, out_ref = refs[-3:]
+    w_ref, wb_ref, dp_ref, dpb_ref, out_ref = refs[-5:]
     bias = jnp.concatenate([bias_ref[place * BLOCK : (place + 1) * BLOCK] for place in places], 0)
     wide = jnp.concatenate([bias] * 4, axis=1)
     spreads = spread_pairs(bq_ref, bg_ref)
@@ -304,12 +303,13 @@
         return nt(key, q) + hidden, nt(value, g)
 
     def weigh(pair, index, scores, dprobs):
-        weights, stats = weighed(scores, dprobs, before, pair, index)
+        kept = dprobs.astype(BF16)
+        weights, stats = weighed(scores, kept.astype(F32), before, pair, index)
         write_stats(out_ref, pair, index, stats)
         if index < 0:
-            wb_ref[pair] = weights.astype(BF16)
+            wb_ref[pair], dpb_ref[pair] = weights.astype(BF16), kept
         else:
-            w_ref[2 * pair + index] = weights.astype(BF16)
+            w_ref[2 * pair + index], dp_ref[2 * pair + index] = weights.astype(BF16), kept
 
     pipelined(units_of(q_ref), products, weigh)
 
@@ -369,25 +369,25 @@
 
 def terms_kernel(counts, *refs):
     q_ref, g_ref, bq_ref, bg_ref, final_ref = refs[:5]
-    blocks = refs[5 : 5 + sum(counts)]
-    calls = refs[5 + sum(counts) : 5 + sum(counts) + 3 * len(counts)]
+    calls = refs[5 : 5 + 5 * len(counts)]
     d_ref, ds_ref, dsb_ref = refs[-3:]
     spreads = spread_pairs(bq_ref, bg_ref)
     beacon = {}
 
     def products(pair, index):
-        g = spreads[pair][1] if index < 0 else g_ref[:, columns_of(pair, index)]
-        return (nt(rows_of(blocks, block_columns(pair, index, True)), g),)
-
-    def finish(pair, index, dprobs):
+        return ()
+
+    def finish(pair, index):
         top, scaled, inner = final_of(read_stats(final_ref, pair, index))
-        parts = []
+        parts, dprobs = [], []
         for place in range(len(counts)):
-            w_ref, wb_ref, st_ref = calls[3 * place : 3 * place + 3]
+            w_ref, wb_ref, dp_ref, dpb_ref, st_ref = calls[5 * place : 5 * place + 5]
             weights = wb_ref[pair] if index < 0 else w_ref[2 * pair + index]
+            kept = dpb_ref[pair] if index < 0 else dp_ref[2 * pair + index]
             factor = power(read_stats(st_ref, pair, index)[0], top) * scaled
             parts.append(weights.astype(F32) * factor)
-        probs = jnp.concatenate(parts, axis=0)
+            dprobs.append(kept.astype(F32))
+        probs, dprobs = jnp.concatenate(parts, axis=0), jnp.concatenate(dprobs, axis=0)
         dscores = (probs * (dprobs - inner)).astype(BF16)
         probs = probs.astype(BF16)
         store_terms(
@@ -557,7 +557,7 @@
         in_specs=shared + in_specs,
         out_specs=out_specs,
         out_shape=out_shape,
-        compiler_params=params(18),
+        compiler_params=params(12),
         cost_estimate=cost(flops, 2**10),
         name=name,
     )(*inputs)
@@ -576,32 +576,32 @@
         [pl.BlockSpec((2 * HALF, LANES), lambda step: (0, 0))]
         + [block_spec()] * len(places)
         + [stat_spec()] * len(before),
-        [some_rows(rows, STRETCH, 2), some_rows(rows, LANES, 1), stat_spec()],
-        [
-            shape((2 * PAIRS, rows, STRETCH), BF16),
-            shape((PAIRS, rows, LANES), BF16),
-            shape((PAIRS, 8, STAT_LANES), F32),
-        ],
+        [some_rows(rows, STRETCH, 2), some_rows(rows, LANES, 1)] * 2 + [stat_spec()],
+        [shape((2 * PAIRS, rows, STRETCH), BF16), shape((PAIRS, rows, LANES), BF16)] * 2
+        + [shape((PAIRS, 8, STAT_LANES), F32)],
         10**6,
     )
 
 
-def terms(name, queries, final, blocks, calls):
+def terms(name, queries, final, calls):
     counts = tuple(count for _, count, _ in calls)
     rows = BLOCK * sum(counts)
     call_specs, call_inputs = [], []
     for outputs, count, place in calls:
         call_specs += [
-            some_rows(BLOCK * count, STRETCH, 2, place),
-            some_rows(BLOCK * count, LANES, 1, place),
+            *[
+                some_rows(BLOCK * count, STRETCH, 2, place),
+                some_rows(BLOCK * count, LANES, 1, place),
+            ]
+            * 2,
             stat_spec(),
         ]
         call_inputs += list(outputs)
     return far_call(
         lambda *refs: terms_kernel(counts, *refs),
         name,
-        (*queries, final, *blocks, *call_inputs),
-        [stat_spec()] + [block_spec()] * len(blocks) + call_specs,
+        (*queries, final, *call_inputs),
+        [stat_spec()] + call_specs,
         [block_spec(rows), some_rows(rows, STRETCH, 2), some_rows(rows, LANES, 1)],
         [
             shape((rows, 2 * FEAT), BF16),
@@ -632,9 +632,9 @@
     )
 
 
-def woven(key, value):
-    parts = [rows.reshape(BEACONS, PAIRS, 1, PAIR) for rows in (key, value)]
-    return jnp.concatenate(parts, axis=2).reshape(BEACONS, 2 * FEAT)
+def woven(both):
+    parts = both.reshape(both.shape[0], 2, PAIRS, PAIR)
+    return lax.optimization_barrier(parts.transpose(0, 2, 1, 3).reshape(both.shape))
 
 
 def unwoven(both):
@@ -654,13 +654,13 @@
     def queries(token):
         return raw_q, raw_grad, token, beacon_grad
 
-    own0 = lax.optimization_barrier(woven(beacon_k[0], beacon_v[0]))
+    own0 = lax.optimization_barrier(jnp.concatenate([beacon_k[0], beacon_v[0]], axis=1))
     (got, bias) = beside(
         own0, assign, lambda value, token: (exchange(value, 0), far_bias(token, prefix))
     )
-    own0 = joined(own0, got)
+    own0 = woven(joined(own0, got))
     stats = ()
-    for step, place, count in ((1, 0, 1), (2, 1, 1), (3, 2, 2)):
+    for step, place, count in ((1, 0, 1), (2, 1, 1), (3, 2, 3)):
         got, stats = beside(
             own0,
             (beacon_q, stats),
@@ -672,7 +672,7 @@
 
     def stage_one(value, token):
         got = exchange(value, 4), exchange(value, 5), swap(value)
-        stats = raw_stats_of(4, 4, *token)
+        stats = raw_stats_of(5, 3, *token)
         late, token, stats = lax.optimization_barrier((got[2], token[0], stats))
         return got, stats, weigh((0, 4), queries(token), bias, (value, late), ())
 
@@ -683,13 +683,13 @@
         got = exchange(own_v[:, :FEAT], 4), exchange(own_u[:, FEAT:], 5)
         others = swap(own_u), swap(own_v)
         blocks = (own_u, own_v, *others)
-        return got, others, weigh((1, 2, 5, 6), queries(token), bias, blocks, first[2:])
+        return got, others, weigh((1, 2, 5, 6), queries(token), bias, blocks, first[4:])
 
     (got_low, got_high), (other_u, other_v), second = beside((own_u, own_v), beacon_q, stage_two)
     own_uv = joined(got_low, got_high, axis=1)
     other_uv = swap(own_uv)
     d_own, d_other, ds_uv, dsb_uv, final = diagonal_terms(
-        queries(beacon_q), bias, (own_uv, other_uv), (second[2], *stats)
+        queries(beacon_q), bias, (own_uv, other_uv), (second[4], *stats)
     )
     got, others = beside(
         d_other,
@@ -697,7 +697,7 @@
         lambda value, token: (
             swap(value),
             terms(
-                "other_rest", queries(token), final, (other0, other_u, other_v),
+                "other_rest", queries(token), final,
                 [(first, 1, 1), (second, 2, 1)],
             ),
         ),
@@ -708,7 +708,7 @@
         value, rest = values
         got = exchange(value[:, :FEAT], 4), exchange(value[:, FEAT:], 5)
         return got, swap(rest), terms(
-            "own_rest", queries(token), final, (own0, own_u, own_v),
+            "own_rest", queries(token), final,
             [(first, 1, 0), (second, 2, 0)],
         )
 

time: 105 us -> 103 us (0.981)
  local copies, waits for them, and re-layouts: 1.99 us -> 0.46 us
  starting transfers between devices: 28.3 us -> 29.5 us
    another operation x2 -> x0, local copies, waits for them, and re-layouts: 1.5 us -> none  [woven(): parts = [rows.reshape(BEACONS, PAIRS, 1, PAIR) for rows in (key, value)]]
  transfers between devices with their start and end apart: 22 -> 22, of which waited for: 11 -> 10; matrix products, arithmetic and copies ran while one was open for 1% -> 0% of each run, Pallas kernels for 52% -> 52%
where the time goes in v3:
time: 103 us
  Pallas kernels  58.9 us (57%)
  starting transfers between devices  29.5 us (29%)
  waiting for transfers between devices  10.3 us (10%)
  other arithmetic  2.39 us (2%)
  between operations  1.03 us (1%)
    pallas_call x9, Pallas kernels, pieces(): pl.pallas_call(kernel, grid=(count,), in_specs=in_specs + [pl.BlockSpec(m...  34.3 us
    ppermute x16, starting transfers between devices, exchange(): return lax.ppermute(value, NAMES, sorted(pairs))  27.4 us
    pallas_call x5, Pallas kernels, far_call(): pl.pallas_call(kernel, grid=(PAIRS // STEP_PAIRS,), in_specs=shared + in_...  22.7 us
    ppermute x16, waiting for transfers between devices, exchange(): return lax.ppermute(value, NAMES, sorted(pairs))  8.61 us
    ppermute x6, starting transfers between devices, swap(): return lax.ppermute(value, 'core', [(0, 1), (1, 0)])  2.12 us
  transfers between devices with their start and end apart: 22, of which 10 were waited for; matrix products, arithmetic and copies ran while one was open for 0% of the time, Pallas kernels for 52%

profile of v3, /device:TPU:0, one launch (start us, length us, event | category | flops | bytes accessed | tf_op | source)
XLA Modules:
  0.0 102.7 jit_solution(2383606818133958969)
XLA Ops:
  0.6 0.8 pad_maximum_fusion.5
  1.4 2.1 %collective-permute-start = (bf16[4,4096]{1,0:T(4,128)(2,1)S(1)}, bf16[4,4096]{1,0:T(4,128)(2,1)S(1)}, u32[]{:S(2)}, u32[]{:S(2)}) collective-permute-start(bf16[4,4096]{1,0:T(4,128)(2,1)S(1)} %pad_maximum_fusion.5), channel_id=1, source_target_pairs={{0,16},{1,17},{2,18},{3,19},{4,20},{5,21},{6,22},{7,23},{8,72},{9,... | collective-permute-start | bytes 98312 | tf_op jit(solution)/shard_map/ppermute | solution.py:49
  3.5 1.9 %far_mask.1.refs_4_ = f32[512,128]{1,0:T(8,128)} custom-call(s32[1,128]{1,0:T(1,128)} %bitcast.25, s32[1,128]{1,0:T(1,128)} %bitcast.26), custom_call_target="tpu_custom_call" | custom-call | tf_op jit(solution)/shard_map/far_mask/pallas_call | solution.py:102
  5.4 4.2 %collective-permute-start.1 = (bf16[8,4096]{1,0:T(8,128)(2,1)S(1)}, bf16[8,4096]{1,0:T(8,128)(2,1)S(1)}, u32[]{:S(2)}, u32[]{:S(2)}) collective-permute-start(bf16[8,4096]{1,0:T(8,128)(2,1)S(1)} %bitcast.19), channel_id=1, source_target_pairs={{0,48},{1,49},{2,50},{3,51},{4,52},{5,53},{6,54},{7,55},{8,73},{9,... | collective-permute-start | bytes 196616 | tf_op jit(solution)/shard_map/ppermute | solution.py:49
  9.6 2.7 %raw_stats_0.1.refs_0_ = f32[8,8,640]{2,1,0:T(8,128)} custom-call(bf16[1,512,2048]{2,1,0:T(8,128)(2,1)} %refs_0_.19, bf16[1,512,2048]{2,1,0:T(8,128)(2,1)} %refs_1_.19, bf16[1,512,2048]{2,1,0:T(8,128)(2,1)} %refs_2_.15, bf16[1,512,2048]{2,1,0:T(8,128)(2,1)} %refs_3_.19, bf16[1,4,2048]{2,1,0:T(4,128)(2,1)} %refs_4_.4, bf16[1,4,2048]{2,1,0:T(4,128)(2,1)} %refs_5_.9, ...), custom_call_target="tpu_custom_call" | custom-call | flops 1000000 | bytes 1024 | tf_op jit(solution)/shard_map/raw_stats_0/pallas_call | solution.py:496
  12.3 1.7 %collective-permute-start.2 = (bf16[16,4096]{1,0:T(8,128)(2,1)S(1)}, bf16[16,4096]{1,0:T(8,128)(2,1)S(1)}, u32[]{:S(2)}, u32[]{:S(2)}) collective-permute-start(bf16[16,4096]{1,0:T(8,128)(2,1)S(1)} %pad_maximum_fusion.3), channel_id=1, source_target_pairs={{0,2},{1,3},{2,0},{3,1},{4,6},{5,7},{6,4},{7,5},{8,24},{9,25},{10,... | collective-permute-start | bytes 393224 | tf_op jit(solution)/shard_map/ppermute | solution.py:49
  14.0 2.7 %raw_stats_1.1.refs_0_ = f32[8,8,640]{2,1,0:T(8,128)} custom-call(bf16[1,512,2048]{2,1,0:T(8,128)(2,1)} %refs_0_.19, bf16[1,512,2048]{2,1,0:T(8,128)(2,1)} %refs_1_.19, bf16[1,512,2048]{2,1,0:T(8,128)(2,1)} %refs_2_.15, bf16[1,512,2048]{2,1,0:T(8,128)(2,1)} %refs_3_.19, bf16[1,4,2048]{2,1,0:T(4,128)(2,1)} %refs_4_.4, ...), custom_call_target="tpu_custom_call", output_to_operand_aliasing={{}: (8, {})} | custom-call | flops 1000000 | bytes 1024 | tf_op jit(solution)/shard_map/raw_stats_1/pallas_call | solution.py:496
  16.6 0.7 collective-permute-done.2
  17.4 3.1 %collective-permute-start.3 = (bf16[32,4096]{1,0:T(8,128)(2,1)S(1)}, bf16[32,4096]{1,0:T(8,128)(2,1)S(1)}, u32[]{:S(2)}, u32[]{:S(2)}) collective-permute-start(bf16[32,4096]{1,0:T(8,128)(2,1)S(1)} %pad_maximum_fusion.2), channel_id=1, source_target_pairs={{0,6},{1,7},{2,4},{3,5},{4,2},{5,3},{6,0},{7,1},{8,56},{9,57},{10,... | collective-permute-start | bytes 786440 | tf_op jit(solution)/shard_map/ppermute | solution.py:49
  20.5 4.7 %raw_stats_2.1.refs_0_ = f32[8,8,640]{2,1,0:T(8,128)} custom-call(bf16[1,512,2048]{2,1,0:T(8,128)(2,1)} %refs_0_.19, bf16[1,512,2048]{2,1,0:T(8,128)(2,1)} %refs_1_.19, bf16[1,512,2048]{2,1,0:T(8,128)(2,1)} %refs_2_.15, bf16[1,512,2048]{2,1,0:T(8,128)(2,1)} %refs_3_.19, bf16[1,4,2048]{2,1,0:T(4,128)(2,1)} %refs_4_.4, ...), custom_call_target="tpu_custom_call", output_to_operand_aliasing={{}: (8, {})} | custom-call | flops 1000000 | bytes 1024 | tf_op jit(solution)/shard_map/raw_stats_2/pallas_call | solution.py:496
  25.4 2.8 %collective-permute-start.5 = (bf16[64,4096]{1,0:T(8,128)(2,1)S(1)}, bf16[64,4096]{1,0:T(8,128)(2,1)S(1)}, u32[]{:S(2)}, u32[]{:S(2)}) collective-permute-start(bf16[64,4096]{1,0:T(8,128)(2,1)S(1)} %pad_maximum_fusion.refs_5_.refs_14_), channel_id=1, source_target_pairs={{0,65},{1,64},{2,67},{3,66},{4,69},{5,68},{6,71},{7,70},{8,14},{9,... | collective-permute-start | bytes 1572872 | tf_op jit(solution)/shard_map/ppermute | solution.py:49
  28.2 0.2 collective-permute-start.4
  28.4 4.7 %raw_stats_5.1.refs_8_ = f32[8,8,640]{2,1,0:T(8,128)} custom-call(bf16[1,512,2048]{2,1,0:T(8,128)(2,1)} %refs_0_.19, bf16[1,512,2048]{2,1,0:T(8,128)(2,1)} %refs_1_.19, bf16[1,512,2048]{2,1,0:T(8,128)(2,1)} %refs_2_.15, bf16[1,512,2048]{2,1,0:T(8,128)(2,1)} %refs_3_.19, bf16[1,4,2048]{2,1,0:T(4,128)(2,1)} %refs_4_.4, ...), custom_call_target="tpu_custom_call", output_to_operand_aliasing={{}: (8, {})} | custom-call | flops 1000000 | bytes 1024 | tf_op jit(solution)/shard_map/raw_stats_5/pallas_call | solution.py:496
  33.2 3.3 %far_weights_0_4.1 = (bf16[16,128,512]{2,1,0:T(8,128)(2,1)S(1)}, bf16[8,128,128]{2,1,0:T(8,128)(2,1)S(1)}, bf16[16,128,512]{2,1,0:T(8,128)(2,1)S(1)}, bf16[8,128,128]{2,1,0:T(8,128)(2,1)S(1)}, f32[8,8,640]{2,1,0:T(8,128)S(1)}) custom-call(bf16[1,512,2048]{2,1,0:T(8,128)(2,1)S(1)} %copy-done, bf16[1,512,2048]{2,1,0:T(8,128)(2,1)S(1)} %copy-done.1, ...), custom_call_target="tpu_custom_call" | custom-call | flops 1000000 | bytes 1024 | tf_op jit(solution)/shard_map/far_weights_0_4/pallas_call | solution.py:554
  36.5 0.9 collective-permute-done.4.refs_5_.refs_15_
  37.4 0.5 collective-permute-start.9
  38.0 1.7 %collective-permute-start.8 = (bf16[64,2048]{1,0:T(8,128)(2,1)S(1)}, bf16[64,2048]{1,0:T(8,128)(2,1)S(1)}, u32[]{:S(2)}, u32[]{:S(2)}) collective-permute-start(bf16[64,2048]{1,0:T(8,128)(2,1)S(1)} %slice.67), channel_id=1, source_target_pairs={{0,65},{1,64},{2,67},{3,66},{4,69},{5,68},{6,71},{7,70},{8,14},{9,... | collective-permute-start | bytes 786440 | tf_op jit(solution)/shard_map/ppermute | solution.py:49
  39.7 0.2 collective-permute-start.7
  39.9 0.2 collective-permute-done.9.refs_7_.refs_12_
  40.1 6.0 %far_weights_1_2_5_6.1 = (bf16[16,256,512]{2,1,0:T(8,128)(2,1)S(1)}, bf16[8,256,128]{2,1,0:T(8,128)(2,1)S(1)}, bf16[16,256,512]{2,1,0:T(8,128)(2,1)S(1)}, bf16[8...) custom-call(bf16[1,512,2048]{2,1,0:T(8,128)(2,1)S(1)} %copy-done, bf16[1,512,2048]{2,1,0:T(8,128)(2,1)S(1)} %copy-done.1, ...), custom_call_target="tpu_custom_call" | custom-call | flops 1000000 | bytes 1024 | tf_op jit(solution)/shard_map/far_weights_1_2_5_6/pallas_call | solution.py:554
  46.1 0.7 collective-permute-start.11
  46.8 1.5 %collective-permute-done.11.refs_6_.refs_10_ = bf16[64,4096]{1,0:T(8,128)(2,1)S(1)} collective-permute-done((bf16[64,4096]{1,0:T(8,128)(2,1)S(1)}, bf16[64,4096]{1,0:T(8,128)(2,1)S(1)}, u32[]{:S(2)}, u32[]{:S(2)}) %collective-permute-start.11) | collective-permute-done | bytes 524320 | tf_op jit(solution)/shard_map/ppermute | solution.py:53
  48.3 5.6 %far_diagonal.1 = (bf16[64,4096]{1,0:T(8,128)(2,1)S(1)}, bf16[64,4096]{1,0:T(8,128)(2,1)S(1)}, bf16[16,128,512]{2,1,0:T(8,128)(2,1)S(1)}, bf16[8,128,128]{2,1,0:T(8,128)(2,1)S(1)}, f32[8,8,640]{2,1,0:T(8,128)S(1)}) custom-call(bf16[1,512,2048]{2,1,0:T(8,128)(2,1)S(1)} %copy-done, bf16[1,512,2048]{2,1,0:T(8,128)(2,1)S(1)} %copy-done.1, ...), custom_call_target="tpu_custom_call" | custom-call | flops 1000000 | bytes 1024 | tf_op jit(solution)/shard_map/far_diagonal/pallas_call | solution.py:554
  53.9 0.6 collective-permute-start.12
  54.6 3.9 %other_rest.1 = (bf16[192,4096]{1,0:T(8,128)(2,1)S(1)}, bf16[16,192,512]{2,1,0:T(8,128)(2,1)S(1)}, bf16[8,192,128]{2,1,0:T(8,128)(2,1)S(1)}) custom-call(bf16[1,512,2048]{2,1,0:T(8,128)(2,1)S(1)} %copy-done, bf16[1,512,2048]{2,1,0:T(8,128)(2,1)S(1)} %copy-done.1, bf16[1,4,2048]{2,1,0:T(4,128)(2,1)S(1)} %copy-done.6, bf16[1,4,2048]{2,1,0:T(4,128)(2,1)S(1)} %copy-done.7, ...), custom_call_target="tpu_custom_call" | custom-call | flops 1000000 | bytes 1024 | tf_op jit(solution)/shard_map/other_rest/pallas_call | solution.py:554
  58.5 0.1 add_convert_fusion.4
  58.6 0.2 collective-permute-start.15
  58.9 1.5 %collective-permute-start.14 = (bf16[64,2048]{1,0:T(8,128)(2,1)S(1)}, bf16[64,2048]{1,0:T(8,128)(2,1)S(1)}, u32[]{:S(2)}, u32[]{:S(2)}) collective-permute-start(bf16[64,2048]{1,0:T(8,128)(2,1)S(1)} %get-tuple-element.374), channel_id=1, source_target_pairs={{0,65},{1,64},{2,67},{3,66},{4,69},{5,68},{6,71},{7,70},{8,14},{9,... | collective-permute-start | bytes 786440 | tf_op jit(solution)/shard_map/ppermute | solution.py:49
  60.4 1.0 collective-permute-start.13
  61.4 3.9 %own_rest.1 = (bf16[192,4096]{1,0:T(8,128)(2,1)S(1)}, bf16[16,192,512]{2,1,0:T(8,128)(2,1)S(1)}, bf16[8,192,128]{2,1,0:T(8,128)(2,1)S(1)}) custom-call(bf16[1,512,2048]{2,1,0:T(8,128)(2,1)S(1)} %copy-done, bf16[1,512,2048]{2,1,0:T(8,128)(2,1)S(1)} %copy-done.1, bf16[1,4,2048]{2,1,0:T(4,128)(2,1)S(1)} %copy-done.6, bf16[1,4,2048]{2,1,0:T(4,128)(2,1)S(1)} %copy-done.7, ...), custom_call_target="tpu_custom_call" | custom-call | flops 1000000 | bytes 1024 | tf_op jit(solution)/shard_map/own_rest/pallas_call | solution.py:554
  65.4 1.2 %collective-permute-done.14 = bf16[64,2048]{1,0:T(8,128)(2,1)S(1)} collective-permute-done((bf16[64,2048]{1,0:T(8,128)(2,1)S(1)}, bf16[64,2048]{1,0:T(8,128)(2,1)S(1)}, u32[]{:S(2)}, u32[]{:S(2)}) %collective-permute-start.14) | collective-permute-done | bytes 262176 | tf_op jit(solution)/shard_map/ppermute | solution.py:49
  66.6 0.2 collective-permute-done.13
  66.8 0.4 add_convert_fusion.1
  67.1 1.1 %collective-permute-start.16 = (bf16[64,4096]{1,0:T(8,128)(2,1)S(1)}, bf16[64,4096]{1,0:T(8,128)(2,1)S(1)}, u32[]{:S(2)}, u32[]{:S(2)}) collective-permute-start(bf16[64,4096]{1,0:T(8,128)(2,1)S(1)} %get-tuple-element.260), channel_id=1, source_target_pairs={{0,64},{1,65},{2,66},{3,67},{4,68},{5,69},{6,70},{7,71},{8,10},{9,... | collective-permute-start | bytes 1572872 | tf_op jit(solution)/shard_map/ppermute | solution.py:49
  68.2 1.6 %collective-permute-start.17 = (bf16[64,4096]{1,0:T(8,128)(2,1)S(1)}, bf16[64,4096]{1,0:T(8,128)(2,1)S(1)}, u32[]{:S(2)}, u32[]{:S(2)}) collective-permute-start(bf16[64,4096]{1,0:T(8,128)(2,1)S(1)} %get-tuple-element.261), channel_id=1, source_target_pairs={{0,65},{1,64},{2,67},{3,66},{4,69},{5,68},{6,71},{7,70},{8,14},{9,... | collective-permute-start | bytes 1572872 | tf_op jit(solution)/shard_map/ppermute | solution.py:49
  69.8 7.0 %raw_grads_0.1 = (bf16[1,512,2048]{2,1,0:T(8,128)(2,1)}, bf16[1,512,2048]{2,1,0:T(8,128)(2,1)}, bf16[1,512,2048]{2,1,0:T(8,128)(2,1)}, bf16[1,4,2048]{2,1,0:T(4,...) custom-call(bf16[1,512,2048]{2,1,0:T(8,128)(2,1)S(1)} %copy-done, bf16[1,512,2048]{2,1,0:T(8,128)(2,1)S(1)} %copy-done.2, ...), custom_call_target="tpu_custom_call" | custom-call | flops 1000000 | bytes 1024 | tf_op jit(solution)/shard_map/raw_grads_0/pallas_call | solution.py:496
  76.9 1.8 %collective-permute-done.17 = bf16[64,4096]{1,0:T(8,128)(2,1)S(1)} collective-permute-done((bf16[64,4096]{1,0:T(8,128)(2,1)S(1)}, bf16[64,4096]{1,0:T(8,128)(2,1)S(1)}, u32[]{:S(2)}, u32[]{:S(2)}) %collective-permute-start.17) | collective-permute-done | bytes 524320 | tf_op jit(solution)/shard_map/ppermute | solution.py:49
  78.6 0.3 add_convert_fusion
  78.9 2.9 %collective-permute-start.18 = (bf16[32,4096]{1,0:T(8,128)(2,1)S(1)}, bf16[32,4096]{1,0:T(8,128)(2,1)S(1)}, u32[]{:S(2)}, u32[]{:S(2)}) collective-permute-start(bf16[32,4096]{1,0:T(8,128)(2,1)S(1)} %slice.89), channel_id=1, source_target_pairs={{0,6},{1,7},{2,4},{3,5},{4,2},{5,3},{6,0},{7,1},{8,56},{9,57},{10,... | collective-permute-start | bytes 786440 | tf_op jit(solution)/shard_map/ppermute | solution.py:49
  81.8 4.8 %raw_grads_3.1 = (bf16[1,512,2048]{2,1,0:T(8,128)(2,1)}, bf16[1,512,2048]{2,1,0:T(8,128)(2,1)}, bf16[1,512,2048]{2,1,0:T(8,128)(2,1)}, bf16[1,4,2048]{2,1,0:T(4,...) custom-call(bf16[1,512,2048]{2,1,0:T(8,128)(2,1)S(1)} %copy-done, ...), custom_call_target="tpu_custom_call", output_to_operand_aliasing={{0}: (23, {}), {1}: (24, {}), {2}: (25, {}), {3}: (26, {}),... | custom-call | flops 1000000 | bytes 1024 | tf_op jit(solution)/shard_map/raw_grads_3/pallas_call | solution.py:496
  86.9 2.6 %raw_grads_5.1 = (bf16[1,512,2048]{2,1,0:T(8,128)(2,1)}, bf16[1,512,2048]{2,1,0:T(8,128)(2,1)}, bf16[1,512,2048]{2,1,0:T(8,128)(2,1)}, bf16[1,4,2048]{2,1,0:T(4,...) custom-call(bf16[1,512,2048]{2,1,0:T(8,128)(2,1)S(1)} %copy-done, ...), custom_call_target="tpu_custom_call", output_to_operand_aliasing={{0}: (23, {}), {1}: (24, {}), {2}: (25, {}), {3}: (26, {}),... | custom-call | flops 1000000 | bytes 1024 | tf_op jit(solution)/shard_map/raw_grads_5/pallas_call | solution.py:496
  89.5 2.4 %collective-permute-done.19 = bf16[16,4096]{1,0:T(8,128)(2,1)S(1)} collective-permute-done((bf16[16,4096]{1,0:T(8,128)(2,1)S(1)}, bf16[16,4096]{1,0:T(8,128)(2,1)S(1)}, u32[]{:S(2)}, u32[]{:S(2)}) %collective-permute-start.19) | collective-permute-done | bytes 131104 | tf_op jit(solution)/shard_map/ppermute | solution.py:49
  91.9 3.1 %collective-permute-start.20 = (bf16[8,4096]{1,0:T(8,128)(2,1)S(1)}, bf16[8,4096]{1,0:T(8,128)(2,1)S(1)}, u32[]{:S(2)}, u32[]{:S(2)}) collective-permute-start(bf16[8,4096]{1,0:T(8,128)(2,1)S(1)} %slice.93), channel_id=1, source_target_pairs={{0,48},{1,49},{2,50},{3,51},{4,52},{5,53},{6,54},{7,55},{8,73},{9,... | collective-permute-start | bytes 196616 | tf_op jit(solution)/shard_map/ppermute | solution.py:49
  95.0 2.5 %raw_grads_6.1 = (bf16[1,512,2048]{2,1,0:T(8,128)(2,1)}, bf16[1,512,2048]{2,1,0:T(8,128)(2,1)}, bf16[1,512,2048]{2,1,0:T(8,128)(2,1)}, bf16[1,4,2048]{2,1,0:T(4,...) custom-call(bf16[1,512,2048]{2,1,0:T(8,128)(2,1)S(1)} %copy-done, ...), custom_call_target="tpu_custom_call", output_to_operand_aliasing={{0}: (23, {}), {1}: (24, {}), {2}: (25, {}), {3}: (26, {}),... | custom-call | flops 1000000 | bytes 1024 | tf_op jit(solution)/shard_map/raw_grads_6/pallas_call | solution.py:496
  97.8 2.6 %raw_grads_7.1 = (bf16[1,512,2048]{2,1,0:T(8,128)(2,1)}, bf16[1,512,2048]{2,1,0:T(8,128)(2,1)}, bf16[1,512,2048]{2,1,0:T(8,128)(2,1)}, bf16[1,4,2048]{2,1,0:T(4,...) custom-call(bf16[1,512,2048]{2,1,0:T(8,128)(2,1)S(1)} %copy-done, ...), custom_call_target="tpu_custom_call", output_to_operand_aliasing={{0}: (23, {}), {1}: (24, {}), {2}: (25, {}), {3}: (26, {}),... | custom-call | flops 1000000 | bytes 1024 | tf_op jit(solution)/shard_map/raw_grads_7/pallas_call | solution.py:496
  100.4 1.3 %collective-permute-done.21 = bf16[4,4096]{1,0:T(4,128)(2,1)S(1)} collective-permute-done((bf16[4,4096]{1,0:T(4,128)(2,1)S(1)}, bf16[4,4096]{1,0:T(4,128)(2,1)S(1)}, u32[]{:S(2)}, u32[]{:S(2)}) %collective-permute-start.21) | collective-permute-done | bytes 32800 | tf_op jit(solution)/shard_map/ppermute | solution.py:49
  101.8 0.2 slice_reduce_fusion
  102.0 0.6 fusion
  (57 shorter events, 1.0 us)
Async XLA Ops:
  1.4 4.0 %collective-permute-start = (bf16[4,4096]{1,0:T(4,128)(2,1)S(1)}, bf16[4,4096]{1,0:T(4,128)(2,1)S(1)}, u32[]{:S(2)}, u32[]{:S(2)}) collective-permute-start(bf16[4,4096]{1,0:T(4,128)(2,1)S(1)} %pad_maximum_fusion.5), channel_id=1, source_target_pairs={{0,16},{1,17},{2,18},{3,19},{4,20},{5,21},{6,22},{7,23},{8,72},{9,... | collective-permute-start | bytes 98312 | tf_op jit(solution)/shard_map/ppermute | solution.py:49
  5.4 6.9 %collective-permute-start.1 = (bf16[8,4096]{1,0:T(8,128)(2,1)S(1)}, bf16[8,4096]{1,0:T(8,128)(2,1)S(1)}, u32[]{:S(2)}, u32[]{:S(2)}) collective-permute-start(bf16[8,4096]{1,0:T(8,128)(2,1)S(1)} %bitcast.19), channel_id=1, source_target_pairs={{0,48},{1,49},{2,50},{3,51},{4,52},{5,53},{6,54},{7,55},{8,73},{9,... | collective-permute-start | bytes 196616 | tf_op jit(solution)/shard_map/ppermute | solution.py:49
  12.3 5.0 %collective-permute-start.2 = (bf16[16,4096]{1,0:T(8,128)(2,1)S(1)}, bf16[16,4096]{1,0:T(8,128)(2,1)S(1)}, u32[]{:S(2)}, u32[]{:S(2)}) collective-permute-start(bf16[16,4096]{1,0:T(8,128)(2,1)S(1)} %pad_maximum_fusion.3), channel_id=1, source_target_pairs={{0,2},{1,3},{2,0},{3,1},{4,6},{5,7},{6,4},{7,5},{8,24},{9,25},{10,... | collective-permute-start | bytes 393224 | tf_op jit(solution)/shard_map/ppermute | solution.py:49
  17.4 7.8 %collective-permute-start.3 = (bf16[32,4096]{1,0:T(8,128)(2,1)S(1)}, bf16[32,4096]{1,0:T(8,128)(2,1)S(1)}, u32[]{:S(2)}, u32[]{:S(2)}) collective-permute-start(bf16[32,4096]{1,0:T(8,128)(2,1)S(1)} %pad_maximum_fusion.2), channel_id=1, source_target_pairs={{0,6},{1,7},{2,4},{3,5},{4,2},{5,3},{6,0},{7,1},{8,56},{9,57},{10,... | collective-permute-start | bytes 786440 | tf_op jit(solution)/shard_map/ppermute | solution.py:49
  25.2 7.9 %copy-start = (bf16[1,512,2048]{2,1,0:T(8,128)(2,1)S(1)}, bf16[1,512,2048]{2,1,0:T(8,128)(2,1)}, u32[]{:S(2)}) copy-start(bf16[1,512,2048]{2,1,0:T(8,128)(2,1)} %refs_0_.19) | copy-start | bytes 6291460
  25.3 7.9 %copy-start.1 = (bf16[1,512,2048]{2,1,0:T(8,128)(2,1)S(1)}, bf16[1,512,2048]{2,1,0:T(8,128)(2,1)}, u32[]{:S(2)}) copy-start(bf16[1,512,2048]{2,1,0:T(8,128)(2,1)} %refs_3_.19) | copy-start | bytes 6291460
  25.3 7.9 %copy-start.4 = (f32[512,128]{1,0:T(8,128)S(1)}, f32[512,128]{1,0:T(8,128)}, u32[]{:S(2)}) copy-start(f32[512,128]{1,0:T(8,128)} %far_mask.1.refs_4_) | copy-start | bytes 786436
  25.3 7.9 %copy-start.6 = (bf16[1,4,2048]{2,1,0:T(4,128)(2,1)S(1)}, bf16[1,4,2048]{2,1,0:T(4,128)(2,1)}, u32[]{:S(2)}) copy-start(bf16[1,4,2048]{2,1,0:T(4,128)(2,1)} %refs_4_.4) | copy-start | bytes 49156
  25.3 7.9 %copy-start.7 = (bf16[1,4,2048]{2,1,0:T(4,128)(2,1)S(1)}, bf16[1,4,2048]{2,1,0:T(4,128)(2,1)}, u32[]{:S(2)}) copy-start(bf16[1,4,2048]{2,1,0:T(4,128)(2,1)} %refs_7_.9) | copy-start | bytes 49156
  25.3 7.9 %collective-permute-start.6 = (bf16[64,4096]{1,0:T(8,128)(2,1)S(1)}, bf16[64,4096]{1,0:T(8,128)(2,1)S(1)}, u32[]{:S(2)}, u32[]{:S(2)}) collective-permute-start(bf16[64,4096]{1,0:T(8,128)(2,1)S(1)} %pad_maximum_fusion.refs_5_.refs_14_), channel_id=1, source_target_pairs={{0,8},{8,0},{1,9},{9,1},{2,10},{10,2},{3,11},{11,3},{4,12},{12,4},... | collective-permute-start | bytes 1572872 | tf_op jit(solution)/shard_map/ppermute | solution.py:53
  25.4 11.1 %collective-permute-start.5 = (bf16[64,4096]{1,0:T(8,128)(2,1)S(1)}, bf16[64,4096]{1,0:T(8,128)(2,1)S(1)}, u32[]{:S(2)}, u32[]{:S(2)}) collective-permute-start(bf16[64,4096]{1,0:T(8,128)(2,1)S(1)} %pad_maximum_fusion.refs_5_.refs_14_), channel_id=1, source_target_pairs={{0,65},{1,64},{2,67},{3,66},{4,69},{5,68},{6,71},{7,70},{8,14},{9,... | collective-permute-start | bytes 1572872 | tf_op jit(solution)/shard_map/ppermute | solution.py:49
  28.2 9.2 %collective-permute-start.4 = (bf16[64,4096]{1,0:T(8,128)(2,1)S(1)}, bf16[64,4096]{1,0:T(8,128)(2,1)S(1)}, u32[]{:S(2)}, u32[]{:S(2)}) collective-permute-start(bf16[64,4096]{1,0:T(8,128)(2,1)S(1)} %pad_maximum_fusion.refs_5_.refs_14_), channel_id=1, source_target_pairs={{0,64},{1,65},{2,66},{3,67},{4,68},{5,69},{6,70},{7,71},{8,10},{9,... | collective-permute-start | bytes 1572872 | tf_op jit(solution)/shard_map/ppermute | solution.py:49
  37.4 2.5 %collective-permute-start.10 = (bf16[64,4096]{1,0:T(8,128)(2,1)S(1)}, bf16[64,4096]{1,0:T(8,128)(2,1)S(1)}, u32[]{:S(2)}, u32[]{:S(2)}) collective-permute-start(bf16[64,4096]{1,0:T(8,128)(2,1)S(1)} %collective-permute-done.5.refs_6_.refs_16_), channel_id=1, source_target_pairs={{0,8},{8,0},{1,9},{9,1},{2,10},{10,2},{3,11},{11,3},{4,12},{12,4},... | collective-permute-start | bytes 1572872 | tf_op jit(solution)/shard_map/ppermute | solution.py:53
  37.4 2.7 %collective-permute-start.9 = (bf16[64,4096]{1,0:T(8,128)(2,1)S(1)}, bf16[64,4096]{1,0:T(8,128)(2,1)S(1)}, u32[]{:S(2)}, u32[]{:S(2)}) collective-permute-start(bf16[64,4096]{1,0:T(8,128)(2,1)S(1)} %collective-permute-done.4.refs_5_.refs_15_), channel_id=1, source_target_pairs={{0,8},{8,0},{1,9},{9,1},{2,10},{10,2},{3,11},{11,3},{4,12},{12,4},... | collective-permute-start | bytes 1572872 | tf_op jit(solution)/shard_map/ppermute | solution.py:53
  38.0 10.4 %copy-start.5 = (f32[8,8,640]{2,1,0:T(8,128)S(1)}, f32[8,8,640]{2,1,0:T(8,128)}, u32[]{:S(2)}) copy-start(f32[8,8,640]{2,1,0:T(8,128)} %raw_stats_5.1.refs_8_) | copy-start | bytes 491524
  38.0 8.1 %collective-permute-start.8 = (bf16[64,2048]{1,0:T(8,128)(2,1)S(1)}, bf16[64,2048]{1,0:T(8,128)(2,1)S(1)}, u32[]{:S(2)}, u32[]{:S(2)}) collective-permute-start(bf16[64,2048]{1,0:T(8,128)(2,1)S(1)} %slice.67), channel_id=1, source_target_pairs={{0,65},{1,64},{2,67},{3,66},{4,69},{5,68},{6,71},{7,70},{8,14},{9,... | collective-permute-start | bytes 786440 | tf_op jit(solution)/shard_map/ppermute | solution.py:49
  39.7 6.4 %collective-permute-start.7 = (bf16[64,2048]{1,0:T(8,128)(2,1)S(1)}, bf16[64,2048]{1,0:T(8,128)(2,1)S(1)}, u32[]{:S(2)}, u32[]{:S(2)}) collective-permute-start(bf16[64,2048]{1,0:T(8,128)(2,1)S(1)} %slice.66), channel_id=1, source_target_pairs={{0,64},{1,65},{2,66},{3,67},{4,68},{5,69},{6,70},{7,71},{8,10},{9,... | collective-permute-start | bytes 786440 | tf_op jit(solution)/shard_map/ppermute | solution.py:49
  46.1 2.2 %collective-permute-start.11 = (bf16[64,4096]{1,0:T(8,128)(2,1)S(1)}, bf16[64,4096]{1,0:T(8,128)(2,1)S(1)}, u32[]{:S(2)}, u32[]{:S(2)}) collective-permute-start(bf16[64,4096]{1,0:T(8,128)(2,1)S(1)} %pad_maximum_fusion.1.refs_5_.refs_9_), channel_id=1, source_target_pairs={{0,8},{8,0},{1,9},{9,1},{2,10},{10,2},{3,11},{11,3},{4,12},{12,4},... | collective-permute-start | bytes 1572872 | tf_op jit(solution)/shard_map/ppermute | solution.py:53
  53.9 4.6 %collective-permute-start.12 = (bf16[64,4096]{1,0:T(8,128)(2,1)S(1)}, bf16[64,4096]{1,0:T(8,128)(2,1)S(1)}, u32[]{:S(2)}, u32[]{:S(2)}) collective-permute-start(bf16[64,4096]{1,0:T(8,128)(2,1)S(1)} %get-tuple-element.234), channel_id=1, source_target_pairs={{0,8},{8,0},{1,9},{9,1},{2,10},{10,2},{3,11},{11,3},{4,12},{12,4},... | collective-permute-start | bytes 1572872 | tf_op jit(solution)/shard_map/ppermute | solution.py:53
  58.6 8.1 %collective-permute-start.15 = (bf16[192,4096]{1,0:T(8,128)(2,1)S(1)}, bf16[192,4096]{1,0:T(8,128)(2,1)S(1)}, u32[]{:S(2)}, u32[]{:S(2)}) collective-permute-start(bf16[192,4096]{1,0:T(8,128)(2,1)S(1)} %get-tuple-element.251), channel_id=1, source_target_pairs={{0,8},{8,0},{1,9},{9,1},{2,10},{10,2},{3,11},{11,3},{4,12},{12,4},... | collective-permute-start | bytes 4718600 | tf_op jit(solution)/shard_map/ppermute | solution.py:53
  58.9 7.7 %collective-permute-start.14 = (bf16[64,2048]{1,0:T(8,128)(2,1)S(1)}, bf16[64,2048]{1,0:T(8,128)(2,1)S(1)}, u32[]{:S(2)}, u32[]{:S(2)}) collective-permute-start(bf16[64,2048]{1,0:T(8,128)(2,1)S(1)} %get-tuple-element.374), channel_id=1, source_target_pairs={{0,65},{1,64},{2,67},{3,66},{4,69},{5,68},{6,71},{7,70},{8,14},{9,... | collective-permute-start | bytes 786440 | tf_op jit(solution)/shard_map/ppermute | solution.py:49
  60.4 6.4 %collective-permute-start.13 = (bf16[64,2048]{1,0:T(8,128)(2,1)S(1)}, bf16[64,2048]{1,0:T(8,128)(2,1)S(1)}, u32[]{:S(2)}, u32[]{:S(2)}) collective-permute-start(bf16[64,2048]{1,0:T(8,128)(2,1)S(1)} %get-tuple-element.375), channel_id=1, source_target_pairs={{0,64},{1,65},{2,66},{3,67},{4,68},{5,69},{6,70},{7,71},{8,10},{9,... | collective-permute-start | bytes 786440 | tf_op jit(solution)/shard_map/ppermute | solution.py:49
  61.4 8.4 %copy-start.3 = (bf16[1,512,2048]{2,1,0:T(8,128)(2,1)S(1)}, bf16[1,512,2048]{2,1,0:T(8,128)(2,1)}, u32[]{:S(2)}) copy-start(bf16[1,512,2048]{2,1,0:T(8,128)(2,1)} %refs_2_.15) | copy-start | bytes 6291460
  65.3 4.5 %copy-start.2 = (bf16[1,512,2048]{2,1,0:T(8,128)(2,1)S(1)}, bf16[1,512,2048]{2,1,0:T(8,128)(2,1)}, u32[]{:S(2)}) copy-start(bf16[1,512,2048]{2,1,0:T(8,128)(2,1)} %refs_1_.19) | copy-start | bytes 6291460
  65.3 4.5 %copy-start.8 = (bf16[1,4,2048]{2,1,0:T(4,128)(2,1)S(1)}, bf16[1,4,2048]{2,1,0:T(4,128)(2,1)}, u32[]{:S(2)}) copy-start(bf16[1,4,2048]{2,1,0:T(4,128)(2,1)} %refs_5_.9) | copy-start | bytes 49156
  65.3 4.5 %copy-start.9 = (bf16[1,4,2048]{2,1,0:T(4,128)(2,1)S(1)}, bf16[1,4,2048]{2,1,0:T(4,128)(2,1)}, u32[]{:S(2)}) copy-start(bf16[1,4,2048]{2,1,0:T(4,128)(2,1)} %refs_6_.9) | copy-start | bytes 49156
  67.1 9.7 %collective-permute-start.16 = (bf16[64,4096]{1,0:T(8,128)(2,1)S(1)}, bf16[64,4096]{1,0:T(8,128)(2,1)S(1)}, u32[]{:S(2)}, u32[]{:S(2)}) collective-permute-start(bf16[64,4096]{1,0:T(8,128)(2,1)S(1)} %get-tuple-element.260), channel_id=1, source_target_pairs={{0,64},{1,65},{2,66},{3,67},{4,68},{5,69},{6,70},{7,71},{8,10},{9,... | collective-permute-start | bytes 1572872 | tf_op jit(solution)/shard_map/ppermute | solution.py:49
  68.2 10.4 %collective-permute-start.17 = (bf16[64,4096]{1,0:T(8,128)(2,1)S(1)}, bf16[64,4096]{1,0:T(8,128)(2,1)S(1)}, u32[]{:S(2)}, u32[]{:S(2)}) collective-permute-start(bf16[64,4096]{1,0:T(8,128)(2,1)S(1)} %get-tuple-element.261), channel_id=1, source_target_pairs={{0,65},{1,64},{2,67},{3,66},{4,69},{5,68},{6,71},{7,70},{8,14},{9,... | collective-permute-start | bytes 1572872 | tf_op jit(solution)/shard_map/ppermute | solution.py:49
  78.9 7.8 %collective-permute-start.18 = (bf16[32,4096]{1,0:T(8,128)(2,1)S(1)}, bf16[32,4096]{1,0:T(8,128)(2,1)S(1)}, u32[]{:S(2)}, u32[]{:S(2)}) collective-permute-start(bf16[32,4096]{1,0:T(8,128)(2,1)S(1)} %slice.89), channel_id=1, source_target_pairs={{0,6},{1,7},{2,4},{3,5},{4,2},{5,3},{6,0},{7,1},{8,56},{9,57},{10,... | collective-permute-start | bytes 786440 | tf_op jit(solution)/shard_map/ppermute | solution.py:49
  86.8 5.0 %collective-permute-start.19 = (bf16[16,4096]{1,0:T(8,128)(2,1)S(1)}, bf16[16,4096]{1,0:T(8,128)(2,1)S(1)}, u32[]{:S(2)}, u32[]{:S(2)}) collective-permute-start(bf16[16,4096]{1,0:T(8,128)(2,1)S(1)} %slice.91), channel_id=1, source_target_pairs={{0,2},{1,3},{2,0},{3,1},{4,6},{5,7},{6,4},{7,5},{8,24},{9,25},{10,... | collective-permute-start | bytes 393224 | tf_op jit(solution)/shard_map/ppermute | solution.py:49
  91.9 5.8 %collective-permute-start.20 = (bf16[8,4096]{1,0:T(8,128)(2,1)S(1)}, bf16[8,4096]{1,0:T(8,128)(2,1)S(1)}, u32[]{:S(2)}, u32[]{:S(2)}) collective-permute-start(bf16[8,4096]{1,0:T(8,128)(2,1)S(1)} %slice.93), channel_id=1, source_target_pairs={{0,48},{1,49},{2,50},{3,51},{4,52},{5,53},{6,54},{7,55},{8,73},{9,... | collective-permute-start | bytes 196616 | tf_op jit(solution)/shard_map/ppermute | solution.py:49
  97.7 4.0 %collective-permute-start.21 = (bf16[4,4096]{1,0:T(4,128)(2,1)S(1)}, bf16[4,4096]{1,0:T(4,128)(2,1)S(1)}, u32[]{:S(2)}, u32[]{:S(2)}) collective-permute-start(bf16[4,4096]{1,0:T(4,128)(2,1)S(1)} %slice.94), channel_id=1, source_target_pairs={{0,16},{1,17},{2,18},{3,19},{4,20},{5,21},{6,22},{7,23},{8,72},{9,... | collective-permute-start | bytes 98312 | tf_op jit(solution)/shard_map/ppermute | solution.py:49

commit v4 on v3

--- a/solution.py
+++ b/solution.py
@@ -28,7 +28,7 @@
 SIZES = (2, 4, 2, 4, 2)
 
 X0, X1, Y0, Y1, Z0, Z1 = 1, 2, 4, 8, 16, 32
-STEPS = ((Z0, Z1, Y0, Y1, X0, X1), (X0, X1, Z0, Z1, Y0, Y1))
+STEPS = ((Z1, Z0, X1, Y1, X0, Y0), (Y1, X0, Y0, Z1, Z0, X1))
 
 
 def gray(position):

time: 103 us -> 103 us (level)
    ppermute x16, waiting for transfers between devices: 8.61 us -> 7.22 us  [exchange(): return lax.ppermute(value, NAMES, sorted(pairs))]
    ppermute x6, starting transfers between devices: 2.12 us -> 3.29 us  [swap(): return lax.ppermute(value, 'core', [(0, 1), (1, 0)])]
  transfers between devices with their start and end apart: 22 -> 22, of which waited for: 10 -> 12; matrix products, arithmetic and copies ran while one was open for 0% -> 0% of each run, Pallas kernels for 52% -> 52%
where the time goes in v4:
time: 103 us; the launch traced here: 102 us
  Pallas kernels  59.1 us (57%)
  starting transfers between devices  29.9 us (29%)
  waiting for transfers between devices  9.4 us (9%)
  other arithmetic  2.39 us (2%)
    pallas_call x9, Pallas kernels, pieces(): pl.pallas_call(kernel, grid=(count,), in_specs=in_specs + [pl.BlockSpec(m...  34.6 us
    ppermute x16, starting transfers between devices, exchange(): return lax.ppermute(value, NAMES, sorted(pairs))  26.7 us
    pallas_call x5, Pallas kernels, far_call(): pl.pallas_call(kernel, grid=(PAIRS // STEP_PAIRS,), in_specs=shared + in_...  22.7 us
    ppermute x16, waiting for transfers between devices, exchange(): return lax.ppermute(value, NAMES, sorted(pairs))  7.22 us
    ppermute x6, starting transfers between devices, swap(): return lax.ppermute(value, 'core', [(0, 1), (1, 0)])  3.29 us
    ppermute x6, waiting for transfers between devices, swap(): return lax.ppermute(value, 'core', [(0, 1), (1, 0)])  2.17 us
  transfers between devices with their start and end apart: 22, of which 12 were waited for; matrix products, arithmetic and copies ran while one was open for 0% of the time, Pallas kernels for 52%

profile of v4, /device:TPU:0, one launch (start us, length us, event | category | flops | bytes accessed | tf_op | source)
XLA Modules:
  0.0 102.4 jit_solution(6466893110283616352)
XLA Ops:
  0.6 0.8 pad_maximum_fusion.5
  1.4 4.2 %collective-permute-start = (bf16[4,4096]{1,0:T(4,128)(2,1)S(1)}, bf16[4,4096]{1,0:T(4,128)(2,1)S(1)}, u32[]{:S(2)}, u32[]{:S(2)}) collective-permute-start(bf16[4,4096]{1,0:T(4,128)(2,1)S(1)} %pad_maximum_fusion.5), channel_id=1, source_target_pairs={{0,48},{1,49},{2,50},{3,51},{4,52},{5,53},{6,54},{7,55},{8,14},{9,... | collective-permute-start | bytes 98312 | tf_op jit(solution)/shard_map/ppermute | solution.py:49
  5.6 1.9 %far_mask.1.refs_4_ = f32[512,128]{1,0:T(8,128)} custom-call(s32[1,128]{1,0:T(1,128)} %bitcast.25, s32[1,128]{1,0:T(1,128)} %bitcast.26), custom_call_target="tpu_custom_call" | custom-call | tf_op jit(solution)/shard_map/far_mask/pallas_call | solution.py:102
  7.6 2.7 %raw_stats_0.1.refs_0_ = f32[8,8,640]{2,1,0:T(8,128)} custom-call(bf16[1,512,2048]{2,1,0:T(8,128)(2,1)} %refs_0_.19, bf16[1,512,2048]{2,1,0:T(8,128)(2,1)} %refs_1_.19, bf16[1,512,2048]{2,1,0:T(8,128)(2,1)} %refs_2_.15, bf16[1,512,2048]{2,1,0:T(8,128)(2,1)} %refs_3_.19, bf16[1,4,2048]{2,1,0:T(4,128)(2,1)} %refs_4_.4, bf16[1,4,2048]{2,1,0:T(4,128)(2,1)} %refs_5_.9, ...), custom_call_target="tpu_custom_call" | custom-call | flops 1000000 | bytes 1024 | tf_op jit(solution)/shard_map/raw_stats_0/pallas_call | solution.py:496
  10.3 1.6 %collective-permute-done.1 = bf16[8,4096]{1,0:T(8,128)(2,1)S(1)} collective-permute-done((bf16[8,4096]{1,0:T(8,128)(2,1)S(1)}, bf16[8,4096]{1,0:T(8,128)(2,1)S(1)}, u32[]{:S(2)}, u32[]{:S(2)}) %collective-permute-start.1) | collective-permute-done | bytes 65568 | tf_op jit(solution)/shard_map/ppermute | solution.py:49
  11.9 2.8 %collective-permute-start.2 = (bf16[16,4096]{1,0:T(8,128)(2,1)S(1)}, bf16[16,4096]{1,0:T(8,128)(2,1)S(1)}, u32[]{:S(2)}, u32[]{:S(2)}) collective-permute-start(bf16[16,4096]{1,0:T(8,128)(2,1)S(1)} %pad_maximum_fusion.3), channel_id=1, source_target_pairs={{0,65},{1,64},{2,67},{3,66},{4,69},{5,68},{6,71},{7,70},{8,10},{9,... | collective-permute-start | bytes 393224 | tf_op jit(solution)/shard_map/ppermute | solution.py:49
  14.7 2.6 %raw_stats_1.1.refs_0_ = f32[8,8,640]{2,1,0:T(8,128)} custom-call(bf16[1,512,2048]{2,1,0:T(8,128)(2,1)} %refs_0_.19, bf16[1,512,2048]{2,1,0:T(8,128)(2,1)} %refs_1_.19, bf16[1,512,2048]{2,1,0:T(8,128)(2,1)} %refs_2_.15, bf16[1,512,2048]{2,1,0:T(8,128)(2,1)} %refs_3_.19, bf16[1,4,2048]{2,1,0:T(4,128)(2,1)} %refs_4_.4, ...), custom_call_target="tpu_custom_call", output_to_operand_aliasing={{}: (8, {})} | custom-call | flops 1000000 | bytes 1024 | tf_op jit(solution)/shard_map/raw_stats_1/pallas_call | solution.py:496
  17.4 0.8 collective-permute-done.2
  18.2 3.1 %collective-permute-start.3 = (bf16[32,4096]{1,0:T(8,128)(2,1)S(1)}, bf16[32,4096]{1,0:T(8,128)(2,1)S(1)}, u32[]{:S(2)}, u32[]{:S(2)}) collective-permute-start(bf16[32,4096]{1,0:T(8,128)(2,1)S(1)} %pad_maximum_fusion.2), channel_id=1, source_target_pairs={{0,6},{1,7},{2,4},{3,5},{4,2},{5,3},{6,0},{7,1},{8,56},{9,57},{10,... | collective-permute-start | bytes 786440 | tf_op jit(solution)/shard_map/ppermute | solution.py:49
  21.3 4.7 %raw_stats_2.1.refs_0_ = f32[8,8,640]{2,1,0:T(8,128)} custom-call(bf16[1,512,2048]{2,1,0:T(8,128)(2,1)} %refs_0_.19, bf16[1,512,2048]{2,1,0:T(8,128)(2,1)} %refs_1_.19, bf16[1,512,2048]{2,1,0:T(8,128)(2,1)} %refs_2_.15, bf16[1,512,2048]{2,1,0:T(8,128)(2,1)} %refs_3_.19, bf16[1,4,2048]{2,1,0:T(4,128)(2,1)} %refs_4_.4, ...), custom_call_target="tpu_custom_call", output_to_operand_aliasing={{}: (8, {})} | custom-call | flops 1000000 | bytes 1024 | tf_op jit(solution)/shard_map/raw_stats_2/pallas_call | solution.py:496
  26.2 0.3 collective-permute-start.5
  26.5 0.3 collective-permute-start.4
  26.8 5.1 %raw_stats_5.1.refs_8_ = f32[8,8,640]{2,1,0:T(8,128)} custom-call(bf16[1,512,2048]{2,1,0:T(8,128)(2,1)} %refs_0_.19, bf16[1,512,2048]{2,1,0:T(8,128)(2,1)} %refs_1_.19, bf16[1,512,2048]{2,1,0:T(8,128)(2,1)} %refs_2_.15, bf16[1,512,2048]{2,1,0:T(8,128)(2,1)} %refs_3_.19, bf16[1,4,2048]{2,1,0:T(4,128)(2,1)} %refs_4_.4, ...), custom_call_target="tpu_custom_call", output_to_operand_aliasing={{}: (8, {})} | custom-call | flops 1000000 | bytes 1024 | tf_op jit(solution)/shard_map/raw_stats_5/pallas_call | solution.py:496
  31.9 3.3 %far_weights_0_4.1 = (bf16[16,128,512]{2,1,0:T(8,128)(2,1)S(1)}, bf16[8,128,128]{2,1,0:T(8,128)(2,1)S(1)}, bf16[16,128,512]{2,1,0:T(8,128)(2,1)S(1)}, bf16[8,128,128]{2,1,0:T(8,128)(2,1)S(1)}, f32[8,8,640]{2,1,0:T(8,128)S(1)}) custom-call(bf16[1,512,2048]{2,1,0:T(8,128)(2,1)S(1)} %copy-done, bf16[1,512,2048]{2,1,0:T(8,128)(2,1)S(1)} %copy-done.1, ...), custom_call_target="tpu_custom_call" | custom-call | flops 1000000 | bytes 1024 | tf_op jit(solution)/shard_map/far_weights_0_4/pallas_call | solution.py:554
  35.2 0.3 collective-permute-done.5.refs_6_.refs_16_
  35.4 0.2 collective-permute-done.4.refs_5_.refs_15_
  35.7 1.8 %collective-permute-start.10 = (bf16[64,4096]{1,0:T(8,128)(2,1)S(1)}, bf16[64,4096]{1,0:T(8,128)(2,1)S(1)}, u32[]{:S(2)}, u32[]{:S(2)}) collective-permute-start(bf16[64,4096]{1,0:T(8,128)(2,1)S(1)} %collective-permute-done.5.refs_6_.refs_16_), channel_id=1, source_target_pairs={{0,8},{8,0},{1,9},{9,1},{2,10},{10,2},{3,11},{11,3},{4,12},{12,4},... | collective-permute-start | bytes 1572872 | tf_op jit(solution)/shard_map/ppermute | solution.py:53
  37.6 0.5 collective-permute-start.8
  38.1 1.0 collective-permute-start.7
  39.1 0.6 collective-permute-done.9.refs_7_.refs_12_
  39.8 6.0 %far_weights_1_2_5_6.1 = (bf16[16,256,512]{2,1,0:T(8,128)(2,1)S(1)}, bf16[8,256,128]{2,1,0:T(8,128)(2,1)S(1)}, bf16[16,256,512]{2,1,0:T(8,128)(2,1)S(1)}, bf16[8...) custom-call(bf16[1,512,2048]{2,1,0:T(8,128)(2,1)S(1)} %copy-done, bf16[1,512,2048]{2,1,0:T(8,128)(2,1)S(1)} %copy-done.1, ...), custom_call_target="tpu_custom_call" | custom-call | flops 1000000 | bytes 1024 | tf_op jit(solution)/shard_map/far_weights_1_2_5_6/pallas_call | solution.py:554
  45.8 0.4 collective-permute-start.11
  46.2 1.5 %collective-permute-done.11.refs_6_.refs_10_ = bf16[64,4096]{1,0:T(8,128)(2,1)S(1)} collective-permute-done((bf16[64,4096]{1,0:T(8,128)(2,1)S(1)}, bf16[64,4096]{1,0:T(8,128)(2,1)S(1)}, u32[]{:S(2)}, u32[]{:S(2)}) %collective-permute-start.11) | collective-permute-done | bytes 524320 | tf_op jit(solution)/shard_map/ppermute | solution.py:53
  47.8 5.6 %far_diagonal.1 = (bf16[64,4096]{1,0:T(8,128)(2,1)S(1)}, bf16[64,4096]{1,0:T(8,128)(2,1)S(1)}, bf16[16,128,512]{2,1,0:T(8,128)(2,1)S(1)}, bf16[8,128,128]{2,1,0:T(8,128)(2,1)S(1)}, f32[8,8,640]{2,1,0:T(8,128)S(1)}) custom-call(bf16[1,512,2048]{2,1,0:T(8,128)(2,1)S(1)} %copy-done, bf16[1,512,2048]{2,1,0:T(8,128)(2,1)S(1)} %copy-done.1, ...), custom_call_target="tpu_custom_call" | custom-call | flops 1000000 | bytes 1024 | tf_op jit(solution)/shard_map/far_diagonal/pallas_call | solution.py:554
  53.4 0.6 collective-permute-start.12
  54.1 3.9 %other_rest.1 = (bf16[192,4096]{1,0:T(8,128)(2,1)S(1)}, bf16[16,192,512]{2,1,0:T(8,128)(2,1)S(1)}, bf16[8,192,128]{2,1,0:T(8,128)(2,1)S(1)}) custom-call(bf16[1,512,2048]{2,1,0:T(8,128)(2,1)S(1)} %copy-done, bf16[1,512,2048]{2,1,0:T(8,128)(2,1)S(1)} %copy-done.1, bf16[1,4,2048]{2,1,0:T(4,128)(2,1)S(1)} %copy-done.6, bf16[1,4,2048]{2,1,0:T(4,128)(2,1)S(1)} %copy-done.7, ...), custom_call_target="tpu_custom_call" | custom-call | flops 1000000 | bytes 1024 | tf_op jit(solution)/shard_map/other_rest/pallas_call | solution.py:554
  58.4 0.7 collective-permute-start.14
  59.1 1.4 %collective-permute-start.13 = (bf16[64,2048]{1,0:T(8,128)(2,1)S(1)}, bf16[64,2048]{1,0:T(8,128)(2,1)S(1)}, u32[]{:S(2)}, u32[]{:S(2)}) collective-permute-start(bf16[64,2048]{1,0:T(8,128)(2,1)S(1)} %get-tuple-element.375), channel_id=1, source_target_pairs={{0,64},{1,65},{2,66},{3,67},{4,68},{5,69},{6,70},{7,71},{8,24},{9,... | collective-permute-start | bytes 786440 | tf_op jit(solution)/shard_map/ppermute | solution.py:49
  60.5 3.9 %own_rest.1 = (bf16[192,4096]{1,0:T(8,128)(2,1)S(1)}, bf16[16,192,512]{2,1,0:T(8,128)(2,1)S(1)}, bf16[8,192,128]{2,1,0:T(8,128)(2,1)S(1)}) custom-call(bf16[1,512,2048]{2,1,0:T(8,128)(2,1)S(1)} %copy-done, bf16[1,512,2048]{2,1,0:T(8,128)(2,1)S(1)} %copy-done.1, bf16[1,4,2048]{2,1,0:T(4,128)(2,1)S(1)} %copy-done.6, bf16[1,4,2048]{2,1,0:T(4,128)(2,1)S(1)} %copy-done.7, ...), custom_call_target="tpu_custom_call" | custom-call | flops 1000000 | bytes 1024 | tf_op jit(solution)/shard_map/own_rest/pallas_call | solution.py:554
  64.4 0.4 collective-permute-done.14
  64.8 0.6 collective-permute-done.13
  65.4 0.4 add_convert_fusion.1
  65.8 1.5 %collective-permute-start.16 = (bf16[64,4096]{1,0:T(8,128)(2,1)S(1)}, bf16[64,4096]{1,0:T(8,128)(2,1)S(1)}, u32[]{:S(2)}, u32[]{:S(2)}) collective-permute-start(bf16[64,4096]{1,0:T(8,128)(2,1)S(1)} %get-tuple-element.260), channel_id=1, source_target_pairs={{0,64},{1,65},{2,66},{3,67},{4,68},{5,69},{6,70},{7,71},{8,24},{9,... | collective-permute-start | bytes 1572872 | tf_op jit(solution)/shard_map/ppermute | solution.py:49
  67.3 0.4 collective-permute-start.17
  67.7 7.0 %raw_grads_0.1 = (bf16[1,512,2048]{2,1,0:T(8,128)(2,1)}, bf16[1,512,2048]{2,1,0:T(8,128)(2,1)}, bf16[1,512,2048]{2,1,0:T(8,128)(2,1)}, bf16[1,4,2048]{2,1,0:T(4,...) custom-call(bf16[1,512,2048]{2,1,0:T(8,128)(2,1)S(1)} %copy-done, bf16[1,512,2048]{2,1,0:T(8,128)(2,1)S(1)} %copy-done.2, ...), custom_call_target="tpu_custom_call" | custom-call | flops 1000000 | bytes 1024 | tf_op jit(solution)/shard_map/raw_grads_0/pallas_call | solution.py:496
  74.7 0.4 collective-permute-done.16
  75.1 1.4 %collective-permute-done.17 = bf16[64,4096]{1,0:T(8,128)(2,1)S(1)} collective-permute-done((bf16[64,4096]{1,0:T(8,128)(2,1)S(1)}, bf16[64,4096]{1,0:T(8,128)(2,1)S(1)}, u32[]{:S(2)}, u32[]{:S(2)}) %collective-permute-start.17) | collective-permute-done | bytes 524320 | tf_op jit(solution)/shard_map/ppermute | solution.py:49
  76.4 0.3 add_convert_fusion
  76.7 2.9 %collective-permute-start.18 = (bf16[32,4096]{1,0:T(8,128)(2,1)S(1)}, bf16[32,4096]{1,0:T(8,128)(2,1)S(1)}, u32[]{:S(2)}, u32[]{:S(2)}) collective-permute-start(bf16[32,4096]{1,0:T(8,128)(2,1)S(1)} %slice.89), channel_id=1, source_target_pairs={{0,6},{1,7},{2,4},{3,5},{4,2},{5,3},{6,0},{7,1},{8,56},{9,57},{10,... | collective-permute-start | bytes 786440 | tf_op jit(solution)/shard_map/ppermute | solution.py:49
  79.7 4.8 %raw_grads_3.1 = (bf16[1,512,2048]{2,1,0:T(8,128)(2,1)}, bf16[1,512,2048]{2,1,0:T(8,128)(2,1)}, bf16[1,512,2048]{2,1,0:T(8,128)(2,1)}, bf16[1,4,2048]{2,1,0:T(4,...) custom-call(bf16[1,512,2048]{2,1,0:T(8,128)(2,1)S(1)} %copy-done, ...), custom_call_target="tpu_custom_call", output_to_operand_aliasing={{0}: (23, {}), {1}: (24, {}), {2}: (25, {}), {3}: (26, {}),... | custom-call | flops 1000000 | bytes 1024 | tf_op jit(solution)/shard_map/raw_grads_3/pallas_call | solution.py:496
  84.6 2.2 %collective-permute-start.19 = (bf16[16,4096]{1,0:T(8,128)(2,1)S(1)}, bf16[16,4096]{1,0:T(8,128)(2,1)S(1)}, u32[]{:S(2)}, u32[]{:S(2)}) collective-permute-start(bf16[16,4096]{1,0:T(8,128)(2,1)S(1)} %slice.91), channel_id=1, source_target_pairs={{0,65},{1,64},{2,67},{3,66},{4,69},{5,68},{6,71},{7,70},{8,10},{9,... | collective-permute-start | bytes 393224 | tf_op jit(solution)/shard_map/ppermute | solution.py:49
  86.9 2.5 %raw_grads_5.1 = (bf16[1,512,2048]{2,1,0:T(8,128)(2,1)}, bf16[1,512,2048]{2,1,0:T(8,128)(2,1)}, bf16[1,512,2048]{2,1,0:T(8,128)(2,1)}, bf16[1,4,2048]{2,1,0:T(4,...) custom-call(bf16[1,512,2048]{2,1,0:T(8,128)(2,1)S(1)} %copy-done, ...), custom_call_target="tpu_custom_call", output_to_operand_aliasing={{0}: (23, {}), {1}: (24, {}), {2}: (25, {}), {3}: (26, {}),... | custom-call | flops 1000000 | bytes 1024 | tf_op jit(solution)/shard_map/raw_grads_5/pallas_call | solution.py:496
  89.4 1.5 %collective-permute-done.19 = bf16[16,4096]{1,0:T(8,128)(2,1)S(1)} collective-permute-done((bf16[16,4096]{1,0:T(8,128)(2,1)S(1)}, bf16[16,4096]{1,0:T(8,128)(2,1)S(1)}, u32[]{:S(2)}, u32[]{:S(2)}) %collective-permute-start.19) | collective-permute-done | bytes 131104 | tf_op jit(solution)/shard_map/ppermute | solution.py:49
  90.9 1.9 %collective-permute-start.20 = (bf16[8,4096]{1,0:T(8,128)(2,1)S(1)}, bf16[8,4096]{1,0:T(8,128)(2,1)S(1)}, u32[]{:S(2)}, u32[]{:S(2)}) collective-permute-start(bf16[8,4096]{1,0:T(8,128)(2,1)S(1)} %slice.93), channel_id=1, source_target_pairs={{0,16},{1,17},{2,18},{3,19},{4,20},{5,21},{6,22},{7,23},{8,72},{9,... | collective-permute-start | bytes 196616 | tf_op jit(solution)/shard_map/ppermute | solution.py:49
  92.8 2.5 %raw_grads_6.1 = (bf16[1,512,2048]{2,1,0:T(8,128)(2,1)}, bf16[1,512,2048]{2,1,0:T(8,128)(2,1)}, bf16[1,512,2048]{2,1,0:T(8,128)(2,1)}, bf16[1,4,2048]{2,1,0:T(4,...) custom-call(bf16[1,512,2048]{2,1,0:T(8,128)(2,1)S(1)} %copy-done, ...), custom_call_target="tpu_custom_call", output_to_operand_aliasing={{0}: (23, {}), {1}: (24, {}), {2}: (25, {}), {3}: (26, {}),... | custom-call | flops 1000000 | bytes 1024 | tf_op jit(solution)/shard_map/raw_grads_6/pallas_call | solution.py:496
  95.6 3.3 %collective-permute-start.21 = (bf16[4,4096]{1,0:T(4,128)(2,1)S(1)}, bf16[4,4096]{1,0:T(4,128)(2,1)S(1)}, u32[]{:S(2)}, u32[]{:S(2)}) collective-permute-start(bf16[4,4096]{1,0:T(4,128)(2,1)S(1)} %slice.94), channel_id=1, source_target_pairs={{0,48},{1,49},{2,50},{3,51},{4,52},{5,53},{6,54},{7,55},{8,14},{9,... | collective-permute-start | bytes 98312 | tf_op jit(solution)/shard_map/ppermute | solution.py:49
  98.9 2.5 %raw_grads_7.1 = (bf16[1,512,2048]{2,1,0:T(8,128)(2,1)}, bf16[1,512,2048]{2,1,0:T(8,128)(2,1)}, bf16[1,512,2048]{2,1,0:T(8,128)(2,1)}, bf16[1,4,2048]{2,1,0:T(4,...) custom-call(bf16[1,512,2048]{2,1,0:T(8,128)(2,1)S(1)} %copy-done, ...), custom_call_target="tpu_custom_call", output_to_operand_aliasing={{0}: (23, {}), {1}: (24, {}), {2}: (25, {}), {3}: (26, {}),... | custom-call | flops 1000000 | bytes 1024 | tf_op jit(solution)/shard_map/raw_grads_7/pallas_call | solution.py:496
  101.7 0.6 fusion
  (57 shorter events, 1.5 us)
Async XLA Ops:
  1.4 6.1 %collective-permute-start = (bf16[4,4096]{1,0:T(4,128)(2,1)S(1)}, bf16[4,4096]{1,0:T(4,128)(2,1)S(1)}, u32[]{:S(2)}, u32[]{:S(2)}) collective-permute-start(bf16[4,4096]{1,0:T(4,128)(2,1)S(1)} %pad_maximum_fusion.5), channel_id=1, source_target_pairs={{0,48},{1,49},{2,50},{3,51},{4,52},{5,53},{6,54},{7,55},{8,14},{9,... | collective-permute-start | bytes 98312 | tf_op jit(solution)/shard_map/ppermute | solution.py:49
  7.5 4.3 %collective-permute-start.1 = (bf16[8,4096]{1,0:T(8,128)(2,1)S(1)}, bf16[8,4096]{1,0:T(8,128)(2,1)S(1)}, u32[]{:S(2)}, u32[]{:S(2)}) collective-permute-start(bf16[8,4096]{1,0:T(8,128)(2,1)S(1)} %bitcast.19), channel_id=1, source_target_pairs={{0,16},{1,17},{2,18},{3,19},{4,20},{5,21},{6,22},{7,23},{8,72},{9,... | collective-permute-start | bytes 196616 | tf_op jit(solution)/shard_map/ppermute | solution.py:49
  11.9 6.3 %collective-permute-start.2 = (bf16[16,4096]{1,0:T(8,128)(2,1)S(1)}, bf16[16,4096]{1,0:T(8,128)(2,1)S(1)}, u32[]{:S(2)}, u32[]{:S(2)}) collective-permute-start(bf16[16,4096]{1,0:T(8,128)(2,1)S(1)} %pad_maximum_fusion.3), channel_id=1, source_target_pairs={{0,65},{1,64},{2,67},{3,66},{4,69},{5,68},{6,71},{7,70},{8,10},{9,... | collective-permute-start | bytes 393224 | tf_op jit(solution)/shard_map/ppermute | solution.py:49
  18.2 7.8 %collective-permute-start.3 = (bf16[32,4096]{1,0:T(8,128)(2,1)S(1)}, bf16[32,4096]{1,0:T(8,128)(2,1)S(1)}, u32[]{:S(2)}, u32[]{:S(2)}) collective-permute-start(bf16[32,4096]{1,0:T(8,128)(2,1)S(1)} %pad_maximum_fusion.2), channel_id=1, source_target_pairs={{0,6},{1,7},{2,4},{3,5},{4,2},{5,3},{6,0},{7,1},{8,56},{9,57},{10,... | collective-permute-start | bytes 786440 | tf_op jit(solution)/shard_map/ppermute | solution.py:49
  26.0 5.8 %copy-start = (bf16[1,512,2048]{2,1,0:T(8,128)(2,1)S(1)}, bf16[1,512,2048]{2,1,0:T(8,128)(2,1)}, u32[]{:S(2)}) copy-start(bf16[1,512,2048]{2,1,0:T(8,128)(2,1)} %refs_0_.19) | copy-start | bytes 6291460
  26.0 5.8 %copy-start.1 = (bf16[1,512,2048]{2,1,0:T(8,128)(2,1)S(1)}, bf16[1,512,2048]{2,1,0:T(8,128)(2,1)}, u32[]{:S(2)}) copy-start(bf16[1,512,2048]{2,1,0:T(8,128)(2,1)} %refs_3_.19) | copy-start | bytes 6291460
  26.1 5.8 %copy-start.4 = (f32[512,128]{1,0:T(8,128)S(1)}, f32[512,128]{1,0:T(8,128)}, u32[]{:S(2)}) copy-start(f32[512,128]{1,0:T(8,128)} %far_mask.1.refs_4_) | copy-start | bytes 786436
  26.1 5.8 %copy-start.6 = (bf16[1,4,2048]{2,1,0:T(4,128)(2,1)S(1)}, bf16[1,4,2048]{2,1,0:T(4,128)(2,1)}, u32[]{:S(2)}) copy-start(bf16[1,4,2048]{2,1,0:T(4,128)(2,1)} %refs_4_.4) | copy-start | bytes 49156
  26.1 5.8 %copy-start.7 = (bf16[1,4,2048]{2,1,0:T(4,128)(2,1)S(1)}, bf16[1,4,2048]{2,1,0:T(4,128)(2,1)}, u32[]{:S(2)}) copy-start(bf16[1,4,2048]{2,1,0:T(4,128)(2,1)} %refs_7_.9) | copy-start | bytes 49156
  26.1 5.7 %collective-permute-start.6 = (bf16[64,4096]{1,0:T(8,128)(2,1)S(1)}, bf16[64,4096]{1,0:T(8,128)(2,1)S(1)}, u32[]{:S(2)}, u32[]{:S(2)}) collective-permute-start(bf16[64,4096]{1,0:T(8,128)(2,1)S(1)} %pad_maximum_fusion.refs_5_.refs_14_), channel_id=1, source_target_pairs={{0,8},{8,0},{1,9},{9,1},{2,10},{10,2},{3,11},{11,3},{4,12},{12,4},... | collective-permute-start | bytes 1572872 | tf_op jit(solution)/shard_map/ppermute | solution.py:53
  26.2 9.3 %collective-permute-start.5 = (bf16[64,4096]{1,0:T(8,128)(2,1)S(1)}, bf16[64,4096]{1,0:T(8,128)(2,1)S(1)}, u32[]{:S(2)}, u32[]{:S(2)}) collective-permute-start(bf16[64,4096]{1,0:T(8,128)(2,1)S(1)} %pad_maximum_fusion.refs_5_.refs_14_), channel_id=1, source_target_pairs={{0,2},{1,3},{2,0},{3,1},{4,6},{5,7},{6,4},{7,5},{8,73},{9,72},{10,... | collective-permute-start | bytes 1572872 | tf_op jit(solution)/shard_map/ppermute | solution.py:49
  26.5 9.2 %collective-permute-start.4 = (bf16[64,4096]{1,0:T(8,128)(2,1)S(1)}, bf16[64,4096]{1,0:T(8,128)(2,1)S(1)}, u32[]{:S(2)}, u32[]{:S(2)}) collective-permute-start(bf16[64,4096]{1,0:T(8,128)(2,1)S(1)} %pad_maximum_fusion.refs_5_.refs_14_), channel_id=1, source_target_pairs={{0,64},{1,65},{2,66},{3,67},{4,68},{5,69},{6,70},{7,71},{8,24},{9,... | collective-permute-start | bytes 1572872 | tf_op jit(solution)/shard_map/ppermute | solution.py:49
  35.7 3.5 %collective-permute-start.10 = (bf16[64,4096]{1,0:T(8,128)(2,1)S(1)}, bf16[64,4096]{1,0:T(8,128)(2,1)S(1)}, u32[]{:S(2)}, u32[]{:S(2)}) collective-permute-start(bf16[64,4096]{1,0:T(8,128)(2,1)S(1)} %collective-permute-done.5.refs_6_.refs_16_), channel_id=1, source_target_pairs={{0,8},{8,0},{1,9},{9,1},{2,10},{10,2},{3,11},{11,3},{4,12},{12,4},... | collective-permute-start | bytes 1572872 | tf_op jit(solution)/shard_map/ppermute | solution.py:53
  37.5 2.3 %collective-permute-start.9 = (bf16[64,4096]{1,0:T(8,128)(2,1)S(1)}, bf16[64,4096]{1,0:T(8,128)(2,1)S(1)}, u32[]{:S(2)}, u32[]{:S(2)}) collective-permute-start(bf16[64,4096]{1,0:T(8,128)(2,1)S(1)} %collective-permute-done.4.refs_5_.refs_15_), channel_id=1, source_target_pairs={{0,8},{8,0},{1,9},{9,1},{2,10},{10,2},{3,11},{11,3},{4,12},{12,4},... | collective-permute-start | bytes 1572872 | tf_op jit(solution)/shard_map/ppermute | solution.py:53
  37.6 10.2 %copy-start.5 = (f32[8,8,640]{2,1,0:T(8,128)S(1)}, f32[8,8,640]{2,1,0:T(8,128)}, u32[]{:S(2)}) copy-start(f32[8,8,640]{2,1,0:T(8,128)} %raw_stats_5.1.refs_8_) | copy-start | bytes 491524
  37.6 8.1 %collective-permute-start.8 = (bf16[64,2048]{1,0:T(8,128)(2,1)S(1)}, bf16[64,2048]{1,0:T(8,128)(2,1)S(1)}, u32[]{:S(2)}, u32[]{:S(2)}) collective-permute-start(bf16[64,2048]{1,0:T(8,128)(2,1)S(1)} %slice.67), channel_id=1, source_target_pairs={{0,2},{1,3},{2,0},{3,1},{4,6},{5,7},{6,4},{7,5},{8,73},{9,72},{10,... | collective-permute-start | bytes 786440 | tf_op jit(solution)/shard_map/ppermute | solution.py:49
  38.1 7.6 %collective-permute-start.7 = (bf16[64,2048]{1,0:T(8,128)(2,1)S(1)}, bf16[64,2048]{1,0:T(8,128)(2,1)S(1)}, u32[]{:S(2)}, u32[]{:S(2)}) collective-permute-start(bf16[64,2048]{1,0:T(8,128)(2,1)S(1)} %slice.66), channel_id=1, source_target_pairs={{0,64},{1,65},{2,66},{3,67},{4,68},{5,69},{6,70},{7,71},{8,24},{9,... | collective-permute-start | bytes 786440 | tf_op jit(solution)/shard_map/ppermute | solution.py:49
  45.8 2.0 %collective-permute-start.11 = (bf16[64,4096]{1,0:T(8,128)(2,1)S(1)}, bf16[64,4096]{1,0:T(8,128)(2,1)S(1)}, u32[]{:S(2)}, u32[]{:S(2)}) collective-permute-start(bf16[64,4096]{1,0:T(8,128)(2,1)S(1)} %pad_maximum_fusion.1.refs_5_.refs_9_), channel_id=1, source_target_pairs={{0,8},{8,0},{1,9},{9,1},{2,10},{10,2},{3,11},{11,3},{4,12},{12,4},... | collective-permute-start | bytes 1572872 | tf_op jit(solution)/shard_map/ppermute | solution.py:53
  53.4 4.6 %collective-permute-start.12 = (bf16[64,4096]{1,0:T(8,128)(2,1)S(1)}, bf16[64,4096]{1,0:T(8,128)(2,1)S(1)}, u32[]{:S(2)}, u32[]{:S(2)}) collective-permute-start(bf16[64,4096]{1,0:T(8,128)(2,1)S(1)} %get-tuple-element.234), channel_id=1, source_target_pairs={{0,8},{8,0},{1,9},{9,1},{2,10},{10,2},{3,11},{11,3},{4,12},{12,4},... | collective-permute-start | bytes 1572872 | tf_op jit(solution)/shard_map/ppermute | solution.py:53
  58.1 7.3 %collective-permute-start.15 = (bf16[192,4096]{1,0:T(8,128)(2,1)S(1)}, bf16[192,4096]{1,0:T(8,128)(2,1)S(1)}, u32[]{:S(2)}, u32[]{:S(2)}) collective-permute-start(bf16[192,4096]{1,0:T(8,128)(2,1)S(1)} %get-tuple-element.251), channel_id=1, source_target_pairs={{0,8},{8,0},{1,9},{9,1},{2,10},{10,2},{3,11},{11,3},{4,12},{12,4},... | collective-permute-start | bytes 4718600 | tf_op jit(solution)/shard_map/ppermute | solution.py:53
  58.4 6.5 %collective-permute-start.14 = (bf16[64,2048]{1,0:T(8,128)(2,1)S(1)}, bf16[64,2048]{1,0:T(8,128)(2,1)S(1)}, u32[]{:S(2)}, u32[]{:S(2)}) collective-permute-start(bf16[64,2048]{1,0:T(8,128)(2,1)S(1)} %get-tuple-element.374), channel_id=1, source_target_pairs={{0,2},{1,3},{2,0},{3,1},{4,6},{5,7},{6,4},{7,5},{8,73},{9,72},{10,... | collective-permute-start | bytes 786440 | tf_op jit(solution)/shard_map/ppermute | solution.py:49
  59.1 6.4 %collective-permute-start.13 = (bf16[64,2048]{1,0:T(8,128)(2,1)S(1)}, bf16[64,2048]{1,0:T(8,128)(2,1)S(1)}, u32[]{:S(2)}, u32[]{:S(2)}) collective-permute-start(bf16[64,2048]{1,0:T(8,128)(2,1)S(1)} %get-tuple-element.375), channel_id=1, source_target_pairs={{0,64},{1,65},{2,66},{3,67},{4,68},{5,69},{6,70},{7,71},{8,24},{9,... | collective-permute-start | bytes 786440 | tf_op jit(solution)/shard_map/ppermute | solution.py:49
  60.4 7.2 %copy-start.3 = (bf16[1,512,2048]{2,1,0:T(8,128)(2,1)S(1)}, bf16[1,512,2048]{2,1,0:T(8,128)(2,1)}, u32[]{:S(2)}) copy-start(bf16[1,512,2048]{2,1,0:T(8,128)(2,1)} %refs_2_.15) | copy-start | bytes 6291460
  64.4 3.3 %copy-start.2 = (bf16[1,512,2048]{2,1,0:T(8,128)(2,1)S(1)}, bf16[1,512,2048]{2,1,0:T(8,128)(2,1)}, u32[]{:S(2)}) copy-start(bf16[1,512,2048]{2,1,0:T(8,128)(2,1)} %refs_1_.19) | copy-start | bytes 6291460
  64.4 3.3 %copy-start.8 = (bf16[1,4,2048]{2,1,0:T(4,128)(2,1)S(1)}, bf16[1,4,2048]{2,1,0:T(4,128)(2,1)}, u32[]{:S(2)}) copy-start(bf16[1,4,2048]{2,1,0:T(4,128)(2,1)} %refs_5_.9) | copy-start | bytes 49156
  64.4 3.3 %copy-start.9 = (bf16[1,4,2048]{2,1,0:T(4,128)(2,1)S(1)}, bf16[1,4,2048]{2,1,0:T(4,128)(2,1)}, u32[]{:S(2)}) copy-start(bf16[1,4,2048]{2,1,0:T(4,128)(2,1)} %refs_6_.9) | copy-start | bytes 49156
  65.8 9.3 %collective-permute-start.16 = (bf16[64,4096]{1,0:T(8,128)(2,1)S(1)}, bf16[64,4096]{1,0:T(8,128)(2,1)S(1)}, u32[]{:S(2)}, u32[]{:S(2)}) collective-permute-start(bf16[64,4096]{1,0:T(8,128)(2,1)S(1)} %get-tuple-element.260), channel_id=1, source_target_pairs={{0,64},{1,65},{2,66},{3,67},{4,68},{5,69},{6,70},{7,71},{8,24},{9,... | collective-permute-start | bytes 1572872 | tf_op jit(solution)/shard_map/ppermute | solution.py:49
  67.3 9.2 %collective-permute-start.17 = (bf16[64,4096]{1,0:T(8,128)(2,1)S(1)}, bf16[64,4096]{1,0:T(8,128)(2,1)S(1)}, u32[]{:S(2)}, u32[]{:S(2)}) collective-permute-start(bf16[64,4096]{1,0:T(8,128)(2,1)S(1)} %get-tuple-element.261), channel_id=1, source_target_pairs={{0,2},{1,3},{2,0},{3,1},{4,6},{5,7},{6,4},{7,5},{8,73},{9,72},{10,... | collective-permute-start | bytes 1572872 | tf_op jit(solution)/shard_map/ppermute | solution.py:49
  76.7 7.8 %collective-permute-start.18 = (bf16[32,4096]{1,0:T(8,128)(2,1)S(1)}, bf16[32,4096]{1,0:T(8,128)(2,1)S(1)}, u32[]{:S(2)}, u32[]{:S(2)}) collective-permute-start(bf16[32,4096]{1,0:T(8,128)(2,1)S(1)} %slice.89), channel_id=1, source_target_pairs={{0,6},{1,7},{2,4},{3,5},{4,2},{5,3},{6,0},{7,1},{8,56},{9,57},{10,... | collective-permute-start | bytes 786440 | tf_op jit(solution)/shard_map/ppermute | solution.py:49
  84.6 6.3 %collective-permute-start.19 = (bf16[16,4096]{1,0:T(8,128)(2,1)S(1)}, bf16[16,4096]{1,0:T(8,128)(2,1)S(1)}, u32[]{:S(2)}, u32[]{:S(2)}) collective-permute-start(bf16[16,4096]{1,0:T(8,128)(2,1)S(1)} %slice.91), channel_id=1, source_target_pairs={{0,65},{1,64},{2,67},{3,66},{4,69},{5,68},{6,71},{7,70},{8,10},{9,... | collective-permute-start | bytes 393224 | tf_op jit(solution)/shard_map/ppermute | solution.py:49
  90.9 4.6 %collective-permute-start.20 = (bf16[8,4096]{1,0:T(8,128)(2,1)S(1)}, bf16[8,4096]{1,0:T(8,128)(2,1)S(1)}, u32[]{:S(2)}, u32[]{:S(2)}) collective-permute-start(bf16[8,4096]{1,0:T(8,128)(2,1)S(1)} %slice.93), channel_id=1, source_target_pairs={{0,16},{1,17},{2,18},{3,19},{4,20},{5,21},{6,22},{7,23},{8,72},{9,... | collective-permute-start | bytes 196616 | tf_op jit(solution)/shard_map/ppermute | solution.py:49
  95.6 5.9 %collective-permute-start.21 = (bf16[4,4096]{1,0:T(4,128)(2,1)S(1)}, bf16[4,4096]{1,0:T(4,128)(2,1)S(1)}, u32[]{:S(2)}, u32[]{:S(2)}) collective-permute-start(bf16[4,4096]{1,0:T(4,128)(2,1)S(1)} %slice.94), channel_id=1, source_target_pairs={{0,48},{1,49},{2,50},{3,51},{4,52},{5,53},{6,54},{7,55},{8,14},{9,... | collective-permute-start | bytes 98312 | tf_op jit(solution)/shard_map/ppermute | solution.py:49
